TPU v7x, 256 devices: a whole 4x4x8 slice. The times are simulated.
256 devices in a mesh: lat: 8 (over y, x_hi), lon: 32 (over x_lo, z, core).
Axes of the slice: x: 4 (x_hi: 2, x_lo: 2; x = x_hi * 2 + x_lo), y: 4, z: 8, core: 2. Of those that a mesh axis runs over, the one named last changes fastest.
Arguments:
- latent: bfloat16 [2, 96, 192, 512], P(None, 'lat', 'lon'), may hold values from -40 to 40
- cotangent: bfloat16 [2, 96, 192, 512], P(None, 'lat', 'lon'), may hold values from -6 to 6
- norm_gain: float32 [512], replicated, may hold values from 0.25 to 1.75
- qkv_weight: bfloat16 [512, 1536], replicated, may hold values from -1 to 1
- out_weight: bfloat16 [512, 512], replicated, may hold values from -0.25 to 0.25
Outputs:
- updated: bfloat16 [2, 96, 192, 512], P(None, 'lat', 'lon')
- latent_grad: bfloat16 [2, 96, 192, 512], P(None, 'lat', 'lon')
All inputs are finite; a program needn't handle non-finite values.
Results may differ from a plain program's by a relative error of at most 0.022.
Values may be sent and summed in bfloat16 or wider, within the bound.
No kernel may reach another device: no remote copies, remote signals or barrier semaphores. Data moves between devices by JAX's collectives and lax.ppermute only.
A program may use at most 64 MiB of HBM per device.

v0:
```python
import math

import jax
import jax.numpy as jnp
from jax import lax
from jax.sharding import PartitionSpec as P

HEADS = 8
WLAT = 12
WLON = 6
SLAT = 6
SLON = 3


NORM_EPS = 1e-05
MASK_FILL = -1000000000.0


def passed_along(shard, axis, by):
    devices = lax.axis_size(axis)
    return lax.ppermute(shard, axis, [(i, (i + by) % devices) for i in range(devices)])


def grid_heads(flat, levels, lat_rows, lon_cols, heads):
    return flat.reshape(levels, lat_rows // WLAT, WLAT, lon_cols // WLON, WLON, heads, -1)


def window_bias(global_rows, total_rows, levels):
    region_rows = (global_rows >= total_rows - WLAT).astype(jnp.int32) + (
        global_rows >= total_rows - SLAT
    ).astype(jnp.int32)
    row_blocks = region_rows.shape[0] // WLAT
    region = jnp.broadcast_to(
        region_rows.reshape(row_blocks, 1, WLAT, 1), (row_blocks, levels, WLAT, WLON)
    )
    region = region.reshape(row_blocks, levels * WLAT * WLON)
    return jnp.where(region[:, :, None] != region[:, None, :], MASK_FILL, 0.0).astype(jnp.float32)


def attend(shifted, bias, qkv_weight, out_weight, heads):
    levels, lat_rows, lon_cols, features = shifted.shape
    head_dim = features // heads
    row_blocks = lat_rows // WLAT
    col_blocks = lon_cols // WLON
    window = levels * WLAT * WLON
    projected = jnp.dot(
        shifted.reshape(-1, features), qkv_weight, preferred_element_type=jnp.float32
    )
    projected = projected.astype(jnp.bfloat16).reshape(-1, 3, features)
    query_grid = grid_heads(projected[:, 0], levels, lat_rows, lon_cols, heads)
    key_grid = grid_heads(projected[:, 1], levels, lat_rows, lon_cols, heads)
    value_grid = grid_heads(projected[:, 2], levels, lat_rows, lon_cols, heads)
    scores = jnp.einsum(
        "larbchd,masbehd->abhlrcmse", query_grid, key_grid, preferred_element_type=jnp.float32
    )
    scores = scores.reshape(row_blocks, col_blocks, heads, window, window)
    scores = scores / math.sqrt(head_dim) + bias[:, None, None]
    probs = jax.nn.softmax(scores, axis=-1)
    probs_low = probs.astype(jnp.bfloat16)
    probs_grid = probs_low.reshape(
        row_blocks, col_blocks, heads, levels, WLAT, WLON, levels, WLAT, WLON
    )
    mixed = jnp.einsum(
        "abhlrcmse,masbehd->larbchd", probs_grid, value_grid, preferred_element_type=jnp.float32
    ).astype(jnp.bfloat16)
    output = jnp.dot(
        mixed.reshape(-1, features), out_weight, preferred_element_type=jnp.float32
    ).astype(jnp.bfloat16)
    return ((query_grid, key_grid, value_grid, probs, probs_grid), output.reshape(shifted.shape))


def attend_back(saved, grad_shifted, qkv_weight, out_weight):
    query_grid, key_grid, value_grid, probs, probs_grid = saved
    levels, lat_rows, lon_cols, features = grad_shifted.shape
    heads = query_grid.shape[5]
    head_dim = features // heads
    grad_mixed = jnp.einsum(
        "tf,gf->tg",
        grad_shifted.reshape(-1, features),
        out_weight,
        preferred_element_type=jnp.float32,
    )
    grad_mixed = grid_heads(grad_mixed.astype(jnp.bfloat16), levels, lat_rows, lon_cols, heads)
    grad_probs = jnp.einsum(
        "larbchd,masbehd->abhlrcmse", grad_mixed, value_grid, preferred_element_type=jnp.float32
    )
    grad_probs = grad_probs.reshape(probs.shape)
    grad_value = jnp.einsum(
        "abhlrcmse,larbchd->masbehd", probs_grid, grad_mixed, preferred_element_type=jnp.float32
    )
    grad_scores = (
        probs
        * (grad_probs - jnp.sum(grad_probs * probs, axis=-1, keepdims=True))
        / math.sqrt(head_dim)
    )
    grad_scores = grad_scores.astype(jnp.bfloat16).reshape(probs_grid.shape)
    grad_query = jnp.einsum(
        "abhlrcmse,masbehd->larbchd", grad_scores, key_grid, preferred_element_type=jnp.float32
    )
    grad_key = jnp.einsum(
        "abhlrcmse,larbchd->masbehd", grad_scores, query_grid, preferred_element_type=jnp.float32
    )
    token_count = levels * lat_rows * lon_cols
    grad_proj = jnp.stack(
        [
            grad_query.reshape(token_count, features),
            grad_key.reshape(token_count, features),
            grad_value.reshape(token_count, features),
        ],
        axis=1,
    )
    grad_proj = grad_proj.astype(jnp.bfloat16).reshape(token_count, 3 * features)
    grad_tokens = jnp.einsum(
        "tc,fc->tf", grad_proj, qkv_weight, preferred_element_type=jnp.float32
    ).astype(jnp.bfloat16)
    return grad_tokens.reshape(grad_shifted.shape)


def normalize(branch):
    values = branch.astype(jnp.float32)
    centred = values - jnp.mean(values, axis=-1, keepdims=True)
    inverse = lax.rsqrt(jnp.mean(centred * centred, axis=-1, keepdims=True) + NORM_EPS)
    return (centred * inverse, inverse)


def grad_from_normed(normed, inverse, cotangent, norm_gain):
    upstream = norm_gain * cotangent.astype(jnp.float32)
    centre_up = jnp.mean(upstream, axis=-1, keepdims=True)
    along = jnp.mean(upstream * normed, axis=-1, keepdims=True)
    return (inverse * (upstream - centre_up - normed * along)).astype(jnp.bfloat16)


def ahead_lat(field):
    strip = passed_along(field[:, :SLAT], "lat", -1)
    return jnp.concatenate([field[:, SLAT:], strip], axis=1)


def ahead_lon(field):
    strip = passed_along(field[:, :, :SLON], "lon", -1)
    return jnp.concatenate([field[:, :, SLON:], strip], axis=2)


def behind_lat(field):
    strip = passed_along(field[:, -SLAT:], "lat", 1)
    return jnp.concatenate([strip, field[:, :-SLAT]], axis=1)


def behind_lon(field):
    strip = passed_along(field[:, :, -SLON:], "lon", 1)
    return jnp.concatenate([strip, field[:, :, :-SLON]], axis=2)


def body(latent, cotangent, norm_gain, qkv_weight, out_weight):
    levels, lat_rows, lon_cols, features = latent.shape
    global_rows = lax.axis_index("lat") * lat_rows + jnp.arange(lat_rows, dtype=jnp.int32)
    bias = window_bias(global_rows, lax.axis_size("lat") * lat_rows, levels)
    saved, branch_shifted = attend(
        ahead_lon(ahead_lat(latent)), bias, qkv_weight, out_weight, HEADS
    )
    branch = behind_lon(behind_lat(branch_shifted))
    normed, inverse = normalize(branch)
    updated = (latent.astype(jnp.float32) + norm_gain * normed).astype(jnp.bfloat16)
    grad_branch = grad_from_normed(normed, inverse, cotangent, norm_gain)
    grad_shifted = attend_back(saved, ahead_lon(ahead_lat(grad_branch)), qkv_weight, out_weight)
    grad_attn = behind_lon(behind_lat(grad_shifted))
    latent_grad = (cotangent.astype(jnp.float32) + grad_attn.astype(jnp.float32)).astype(
        jnp.bfloat16
    )
    return (updated, latent_grad)


def solution(mesh):
    placed = (P(None, "lat", "lon", None), P(None, "lat", "lon", None), P(), P(), P())
    return jax.shard_map(
        body,
        mesh=mesh,
        in_specs=placed,
        out_specs=(P(None, "lat", "lon", None), P(None, "lat", "lon", None)),
        check_vma=False,
    )
```

profile of v0, /device:TPU:2, one launch (start us, length us, event | category | flops | bytes accessed | tf_op | source)
XLA Modules:
  0.0 115.1 jit_solution(803163335697067060)
XLA Ops:
  1.8 4.7 %collective-permute-start = (bf16[2,6,6,512]{3,0,2,1:T(2,128)(2,1)S(1)}, bf16[2,6,6,512]{3,0,2,1:T(2,128)(2,1)S(1)}, u32[]{:S(2)}, u32[]{:S(2)}) collective-permute-start(bf16[2,6,6,512]{3,0,2,1:T(2,128)(2,1)S(1)} %get-tuple-element.24), channel_id=1, source_target_pairs={{0,224},{32,0},{64,32},{96,64},{128,96},{160,128},{192,160},{224,1... | collective-permute-start | bytes 221192 | tf_op jit(solution)/shard_map/ppermute | solution.py:21
  6.5 2.0 %collective-permute-done = bf16[2,6,6,512]{3,0,2,1:T(2,128)(2,1)S(1)} collective-permute-done((bf16[2,6,6,512]{3,0,2,1:T(2,128)(2,1)S(1)}, bf16[2,6,6,512]{3,0,2,1:T(2,128)(2,1)S(1)}, u32[]{:S(2)}, u32[]{:S(2)}) %collective-permute-start) | collective-permute-done | bytes 73760 | tf_op jit(solution)/shard_map/ppermute | solution.py:21
  8.6 5.4 %collective-permute-start.1 = (bf16[2,12,3,512]{3,0,2,1:T(2,128)(2,1)S(1)}, bf16[2,12,3,512]{3,0,2,1:T(2,128)(2,1)S(1)}, u32[]{:S(2)}, u32[]{:S(2)}) collective-permute-start(bf16[2,12,3,512]{3,0,2,1:T(2,128)(2,1)S(1)} %get-tuple-element.22), channel_id=1, source_target_pairs={{0,31},{1,0},{2,1},{3,2},{4,3},{5,4},{6,5},{7,6},{8,7},{9,8},{10,9... | collective-permute-start | bytes 221192 | tf_op jit(solution)/shard_map/ppermute | solution.py:21
  14.2 1.8 %collective-permute-done.1 = bf16[2,12,3,512]{3,0,2,1:T(2,128)(2,1)S(1)} collective-permute-done((bf16[2,12,3,512]{3,0,2,1:T(2,128)(2,1)S(1)}, bf16[2,12,3,512]{3,0,2,1:T(2,128)(2,1)S(1)}, u32[]{:S(2)}, u32[]{:S(2)}) %collective-permute-start.1) | collective-permute-done | bytes 73760 | tf_op jit(solution)/shard_map/ppermute | solution.py:21
  17.5 1.7 %reshape.216 = bf16[144,3,512]{2,1,0:T(4,128)(2,1)S(1)} reshape(bf16[144,1536]{1,0:T(8,128)(2,1)} %convolution_convert_fusion) | data formatting | bytes 884736 | tf_op jit(solution)/shard_map/reshape | solution.py:49
  19.2 2.5 %slice_reduce_fusion.2 = (bf16[144,512]{1,0:T(8,128)(2,1)}, bf16[144,512]{1,0:T(8,128)(2,1)}, bf16[144,512]{1,0:T(8,128)(2,1)S(1)}) fusion(bf16[144,3,512]{2,1,0:T(4,128)(2,1)S(1)} %reshape.216), kind=kLoop, calls=%fused_computation.64 | loop fusion | bytes 884736 | tf_op jit(solution)/shard_map/slice | solution.py:52
  21.7 1.8 %reshape.217 = bf16[2,12,6,8,64]{4,3,2,1,0:T(8,128)(2,1)} reshape(bf16[144,512]{1,0:T(8,128)(2,1)} %get-tuple-element.4) | data formatting | bytes 294912 | tf_op jit(solution)/shard_map/reshape.11
  24.8 2.1 %fusion = (f32[8,2,12,6]{2,3,1,0:T(8,128)S(1)}, f32[8,2,12,6,2,12,6]{2,5,6,4,3,1,0:T(8,128)S(1)}) fusion(f32[2,12,6,2,12,6]{1,4,5,3,2,0:T(8,128)S(1)} %compare_select_fusion, bf16[2,12,6,8,64,1,1]{4,3,2,1,0,6,5:T(8,128)(2,1)S(1)} %bitcast.85, bf16[2,12,6,8,64,1,1]{4,3,2,1,0,6,5:T(8,128)(2,1)S(1)} %bitcast.87), kind=kOutput, calls=%fused_computation.4 | convolution fusion | flops 21730176 | bytes 1046016 | tf_op jit(solution)/shard_map/larbchd,masbehd->abhlrcmse/dot_general | solution.py:53
  27.0 3.1 %fusion.2 = f32[8,2,12,6]{2,3,1,0:T(8,128)S(1)} fusion(f32[8,2,12,6,2,12,6]{2,5,6,4,3,1,0:T(8,128)S(1)} %get-tuple-element.26, f32[8,2,12,6]{2,3,1,0:T(8,128)S(1)} %get-tuple-element.25, f32[2,12,6,2,12,6]{1,4,5,3,2,0:T(8,128)S(1)} %compare_select_fusion), kind=kLoop, calls=%fused_computation.6 | loop fusion | flops 662400 | bytes 755712 | tf_op jit(solution)/shard_map/reduce_sum | solution.py:58
  30.1 2.5 %fusion.79 = bf16[8,2,12,6,2,12,6]{2,5,6,4,3,1,0:T(8,128)(2,1)S(1)} fusion(f32[8,2,12,6]{2,3,1,0:T(8,128)S(1)} %fusion.2, f32[8,2,12,6]{2,3,1,0:T(8,128)S(1)} %get-tuple-element.25, f32[2,12,6,2,12,6]{1,4,5,3,2,0:T(8,128)S(1)} %compare_select_fusion, f32[8,2,12,6,2,12,6]{2,5,6,4,3,1,0:T(8,128)S(1)} %get-tuple-element.26), kind=kLoop, calls=%fused_computation.92 | loop fusion | flops 829440 | bytes 1087488 | tf_op jit(solution)/shard_map/convert_element_type | solution.py:59
  32.7 2.2 %copy-done.2 = bf16[8,2,12,6,2,12,6]{2,5,6,4,3,1,0:T(8,128)(2,1)} copy-done((bf16[8,2,12,6,2,12,6]{2,5,6,4,3,1,0:T(8,128)(2,1)}, bf16[8,2,12,6,2,12,6]{2,5,6,4,3,1,0:T(8,128)(2,1)S(1)}, u32[]{:S(2)}) %copy-start.2) | copy-done | bytes 331800
  34.9 1.4 %fusion.35 = bf16[2,1,12,1,6,8,64]{6,2,4,0,5,3,1:T(8,128)(2,1)S(1)} fusion(bf16[8,2,12,6,2,12,6]{2,5,6,4,3,1,0:T(8,128)(2,1)S(1)} %fusion.79, bf16[2,12,6,8,64,1,1]{4,3,2,1,0,6,5:T(8,128)(2,1)S(1)} %bitcast.91), kind=kOutput, calls=%fused_computation.24 | convolution fusion | flops 21307392 | bytes 626688 | tf_op jit(solution)/shard_map/abhlrcmse,masbehd->larbchd/dot_general | solution.py:63
  37.2 1.9 %reshape.220 = bf16[144,512]{1,0:T(8,128)(2,1)} reshape(bf16[2,1,12,1,6,8,64]{6,5,4,2,0,3,1:T(8,128)(2,1)} %copy.26) | data formatting | bytes 294912 | tf_op jit(solution)/shard_map/reshape | solution.py:67
  39.1 2.0 %convolution_convert_fusion.2 = bf16[144,512]{1,0:T(8,128)(2,1)} fusion(bf16[144,512]{1,0:T(8,128)(2,1)} %reshape.220, bf16[512,512]{1,0:T(8,128)(2,1)} %param.9), kind=kOutput, calls=%fused_computation.30 | convolution fusion | flops 75571200 | bytes 819200 | tf_op jit(solution)/shard_map/dot_general | solution.py:66
  41.1 1.6 %reshape.221 = bf16[2,12,6,512]{3,2,1,0:T(8,128)(2,1)} reshape(bf16[144,512]{1,0:T(8,128)(2,1)} %convolution_convert_fusion.2) | data formatting | bytes 294912 | tf_op jit(solution)/shard_map/reshape | solution.py:69
  43.7 1.8 %collective-permute-start.2 = (bf16[2,6,6,512]{3,2,1,0:T(8,128)(2,1)S(1)}, bf16[2,6,6,512]{3,2,1,0:T(8,128)(2,1)S(1)}, u32[]{:S(2)}, u32[]{:S(2)}) collective-permute-start(bf16[2,6,6,512]{3,2,1,0:T(8,128)(2,1)S(1)} %get-tuple-element.19), channel_id=1, source_target_pairs={{0,32},{32,64},{64,96},{96,128},{128,160},{160,192},{192,224},{224... | collective-permute-start | bytes 221192 | tf_op jit(solution)/shard_map/ppermute | solution.py:21
  45.4 6.8 %collective-permute-done.2 = bf16[2,6,6,512]{3,2,1,0:T(8,128)(2,1)S(1)} collective-permute-done((bf16[2,6,6,512]{3,2,1,0:T(8,128)(2,1)S(1)}, bf16[2,6,6,512]{3,2,1,0:T(8,128)(2,1)S(1)}, u32[]{:S(2)}, u32[]{:S(2)}) %collective-permute-start.2) | collective-permute-done | bytes 73760 | tf_op jit(solution)/shard_map/ppermute | solution.py:21
  52.4 6.1 %collective-permute-done.3 = bf16[2,12,3,512]{3,2,1,0:T(4,128)(2,1)S(1)} collective-permute-done((bf16[2,12,3,512]{3,2,1,0:T(4,128)(2,1)S(1)}, bf16[2,12,3,512]{3,2,1,0:T(4,128)(2,1)S(1)}, u32[]{:S(2)}, u32[]{:S(2)}) %collective-permute-start.3) | collective-permute-done | bytes 73760 | tf_op jit(solution)/shard_map/ppermute | solution.py:21
  59.9 1.8 %fusion.58 = (bf16[2,12,6,512]{3,2,1,0:T(8,128)(2,1)S(1)}, bf16[2,12,6,512]{3,2,1,0:T(8,128)(2,1)}) fusion(bf16[2,12,6,512]{3,2,1,0:T(8,128)(2,1)S(1)} %get-tuple-element.10, bf16[2,12,6,512]{3,0,2,1:T(2,128)(2,1)S(1)} %copy-done.4, f32[2,12,6]{2,1,0:T(8,128)S(1)} %get-tuple-element.29, f32[2,12,6]{2,1,0:T(8,128)S(1)} %get-tuple-element.30, ...), kind=kLoop, calls=%fused_computation.48 | loop fusion | flops 1032192 | bytes 741632 | tf_op jit(solution)/shard_map/convert_element_type | solution.py:130
  61.7 3.0 %collective-permute-start.4 = (bf16[2,6,6,512]{3,2,1,0:T(8,128)(2,1)S(1)}, bf16[2,6,6,512]{3,2,1,0:T(8,128)(2,1)S(1)}, u32[]{:S(2)}, u32[]{:S(2)}) collective-permute-start(bf16[2,6,6,512]{3,2,1,0:T(8,128)(2,1)S(1)} %get-tuple-element.18), channel_id=1, source_target_pairs={{0,224},{32,0},{64,32},{96,64},{128,96},{160,128},{192,160},{224,1... | collective-permute-start | bytes 221192 | tf_op jit(solution)/shard_map/ppermute | solution.py:21
  64.8 3.2 %collective-permute-done.4 = bf16[2,6,6,512]{3,2,1,0:T(8,128)(2,1)S(1)} collective-permute-done((bf16[2,6,6,512]{3,2,1,0:T(8,128)(2,1)S(1)}, bf16[2,6,6,512]{3,2,1,0:T(8,128)(2,1)S(1)}, u32[]{:S(2)}, u32[]{:S(2)}) %collective-permute-start.4) | collective-permute-done | bytes 73760 | tf_op jit(solution)/shard_map/ppermute | solution.py:21
  68.1 2.2 %collective-permute-done.5 = bf16[2,12,3,512]{3,2,1,0:T(4,128)(2,1)S(1)} collective-permute-done((bf16[2,12,3,512]{3,2,1,0:T(4,128)(2,1)S(1)}, bf16[2,12,3,512]{3,2,1,0:T(4,128)(2,1)S(1)}, u32[]{:S(2)}, u32[]{:S(2)}) %collective-permute-start.5) | collective-permute-done | bytes 73760 | tf_op jit(solution)/shard_map/ppermute | solution.py:21
  71.1 1.6 %reshape.222 = bf16[144,512]{1,0:T(8,128)(2,1)} reshape(bf16[2,12,6,512]{3,2,1,0:T(8,128)(2,1)} %pad_maximum_fusion.2) | data formatting | bytes 294912 | tf_op jit(solution)/shard_map/reshape | solution.py:79
  72.7 2.1 %convolution_convert_fusion.1 = bf16[144,512]{1,0:T(8,128)(2,1)} fusion(bf16[144,512]{1,0:T(8,128)(2,1)} %reshape.222, bf16[512,512]{1,0:T(8,128)(2,1)} %param.9), kind=kOutput, calls=%fused_computation.29 | convolution fusion | flops 75571200 | bytes 819200 | tf_op jit(solution)/shard_map/tf,gf->tg/dot_general | solution.py:77
  74.8 1.8 %reshape.223 = bf16[2,12,6,8,64]{4,3,2,1,0:T(8,128)(2,1)} reshape(bf16[144,512]{1,0:T(8,128)(2,1)} %convolution_convert_fusion.1) | data formatting | bytes 294912 | tf_op jit(solution)/shard_map/reshape.27
  76.6 4.1 %fusion.44 = bf16[2,1,12,1,6,8,64]{6,2,4,0,5,3,1:T(8,128)(2,1)S(1)} fusion(bf16[8,2,12,6,2,12,6]{2,5,6,4,3,1,0:T(8,128)(2,1)} %copy-done.2, bf16[2,12,6,8,64,1,1]{4,3,2,1,0,6,5:T(8,128)(2,1)} %bitcast.92), kind=kOutput, calls=%fused_computation.27 | convolution fusion | flops 21307392 | bytes 626688 | tf_op jit(solution)/shard_map/abhlrcmse,larbchd->masbehd/dot_general | solution.py:88
  80.7 7.9 %multiply_reduce_fusion = (f32[8,2,12,6]{2,3,1,0:T(8,128)S(1)}, f32[8,2,12,6,2,12,6]{2,5,6,4,3,1,0:T(8,128)S(1)}) fusion(f32[8,2,12,6]{2,3,1,0:T(8,128)} %copy-done.6, f32[8,2,12,6]{2,3,1,0:T(8,128)S(1)} %get-tuple-element.25, f32[2,12,6,2,12,6]{1,4,5,3,2,0:T(8,128)S(1)} %compare_select_fusion, f32[8,2,12,6,2,12,6]{2,5,6,4,3,1,0:T(8,128)} %copy-done.1, ...), kind=kOutput, calls=%fused_computation.1 | convolution fusion | flops 22227840 | bytes 1718784 | tf_op jit(solution)/shard_map/larbchd,masbehd->abhlrcmse/dot_general | solution.py:84
  88.7 4.0 %multiply_convert_fusion = bf16[8,2,12,6,2,12,6]{2,5,6,4,3,1,0:T(8,128)(2,1)S(1)} fusion(f32[8,2,12,6,2,12,6]{2,5,6,4,3,1,0:T(8,128)S(1)} %get-tuple-element.28, f32[8,2,12,6]{2,3,1,0:T(8,128)S(1)} %get-tuple-element.27, f32[8,2,12,6]{2,3,1,0:T(8,128)S(1)} %copy-done.7, f32[8,2,12,6]{2,3,1,0:T(8,128)S(1)} %get-tuple-element.25, ...), kind=kLoop, calls=%fused_computation | loop fusion | flops 1327104 | bytes 1755648 | tf_op jit(solution)/shard_map/convert_element_type | solution.py:96
  92.8 2.3 %fusion.41 = bf16[2,1,12,1,6,8,64]{6,2,4,0,5,3,1:T(8,128)(2,1)} fusion(bf16[8,2,12,6,2,12,6]{2,5,6,4,3,1,0:T(8,128)(2,1)S(1)} %multiply_convert_fusion, bf16[2,12,6,8,64,1,1]{4,3,2,1,0,6,5:T(8,128)(2,1)S(1)} %bitcast.88), kind=kOutput, calls=%fused_computation.26 | convolution fusion | flops 21307392 | bytes 626688 | tf_op jit(solution)/shard_map/abhlrcmse,larbchd->masbehd/dot_general | solution.py:100
  95.0 1.4 %fusion.38 = bf16[2,1,12,1,6,8,64]{6,2,4,0,5,3,1:T(8,128)(2,1)S(1)} fusion(bf16[8,2,12,6,2,12,6]{2,5,6,4,3,1,0:T(8,128)(2,1)S(1)} %multiply_convert_fusion, bf16[2,12,6,8,64,1,1]{4,3,2,1,0,6,5:T(8,128)(2,1)S(1)} %bitcast.86), kind=kOutput, calls=%fused_computation.25 | convolution fusion | flops 21307392 | bytes 626688 | tf_op jit(solution)/shard_map/abhlrcmse,masbehd->larbchd/dot_general | solution.py:97
  99.9 8.0 %collective-permute-done.6 = bf16[2,6,6,512]{3,2,1,0:T(8,128)(2,1)S(1)} collective-permute-done((bf16[2,6,6,512]{3,2,1,0:T(8,128)(2,1)S(1)}, bf16[2,6,6,512]{3,2,1,0:T(8,128)(2,1)S(1)}, u32[]{:S(2)}, u32[]{:S(2)}) %collective-permute-start.6) | collective-permute-done | bytes 73760 | tf_op jit(solution)/shard_map/ppermute | solution.py:21
  108.8 5.3 %collective-permute-done.7 = bf16[2,12,3,512]{3,2,1,0:T(4,128)(2,1)S(1)} collective-permute-done((bf16[2,12,3,512]{3,2,1,0:T(4,128)(2,1)S(1)}, bf16[2,12,3,512]{3,2,1,0:T(4,128)(2,1)S(1)}, u32[]{:S(2)}, u32[]{:S(2)}) %collective-permute-start.7) | collective-permute-done | bytes 73760 | tf_op jit(solution)/shard_map/ppermute | solution.py:21
  (63 shorter events, 13.9 us)
Async XLA Ops:
  0.6 15.7 %copy-start = (bf16[512,1536]{1,0:T(8,128)(2,1)S(1)}, bf16[512,1536]{1,0:T(8,128)(2,1)}, u32[]{:S(2)}) copy-start(bf16[512,1536]{1,0:T(8,128)(2,1)} %param.8) | copy-start | bytes 4718596
  1.8 6.6 %collective-permute-start = (bf16[2,6,6,512]{3,0,2,1:T(2,128)(2,1)S(1)}, bf16[2,6,6,512]{3,0,2,1:T(2,128)(2,1)S(1)}, u32[]{:S(2)}, u32[]{:S(2)}) collective-permute-start(bf16[2,6,6,512]{3,0,2,1:T(2,128)(2,1)S(1)} %get-tuple-element.24), channel_id=1, source_target_pairs={{0,224},{32,0},{64,32},{96,64},{128,96},{160,128},{192,160},{224,1... | collective-permute-start | bytes 221192 | tf_op jit(solution)/shard_map/ppermute | solution.py:21
  8.6 7.4 %collective-permute-start.1 = (bf16[2,12,3,512]{3,0,2,1:T(2,128)(2,1)S(1)}, bf16[2,12,3,512]{3,0,2,1:T(2,128)(2,1)S(1)}, u32[]{:S(2)}, u32[]{:S(2)}) collective-permute-start(bf16[2,12,3,512]{3,0,2,1:T(2,128)(2,1)S(1)} %get-tuple-element.22), channel_id=1, source_target_pairs={{0,31},{1,0},{2,1},{3,2},{4,3},{5,4},{6,5},{7,6},{8,7},{9,8},{10,9... | collective-permute-start | bytes 221192 | tf_op jit(solution)/shard_map/ppermute | solution.py:21
  27.0 5.7 %copy-start.1 = (f32[8,2,12,6,2,12,6]{2,5,6,4,3,1,0:T(8,128)}, f32[8,2,12,6,2,12,6]{2,5,6,4,3,1,0:T(8,128)S(1)}, u32[]{:S(2)}) copy-start(f32[8,2,12,6,2,12,6]{2,5,6,4,3,1,0:T(8,128)S(1)} %get-tuple-element.26) | copy-start | bytes 1990660
  30.1 6.2 %copy-start.6 = (f32[8,2,12,6]{2,3,1,0:T(8,128)}, f32[8,2,12,6]{2,3,1,0:T(8,128)S(1)}, u32[]{:S(2)}) copy-start(f32[8,2,12,6]{2,3,1,0:T(8,128)S(1)} %fusion.2) | copy-start | bytes 13828
  30.1 4.8 %copy-start.3 = (bf16[2,12,6,8,64]{4,3,2,1,0:T(8,128)(2,1)S(1)}, bf16[2,12,6,8,64]{4,3,2,1,0:T(8,128)(2,1)}, u32[]{:S(2)}) copy-start(bf16[2,12,6,8,64]{4,3,2,1,0:T(8,128)(2,1)} %reshape.217) | copy-start | bytes 442372
  30.1 28.9 %copy-start.4 = (bf16[2,12,6,512]{3,0,2,1:T(2,128)(2,1)S(1)}, bf16[2,12,6,512]{3,0,2,1:T(2,128)(2,1)}, u32[]{:S(2)}) copy-start(bf16[2,12,6,512]{3,0,2,1:T(2,128)(2,1)} %param.6) | copy-start | bytes 442372
  32.7 2.2 %copy-start.2 = (bf16[8,2,12,6,2,12,6]{2,5,6,4,3,1,0:T(8,128)(2,1)}, bf16[8,2,12,6,2,12,6]{2,5,6,4,3,1,0:T(8,128)(2,1)S(1)}, u32[]{:S(2)}) copy-start(bf16[8,2,12,6,2,12,6]{2,5,6,4,3,1,0:T(8,128)(2,1)S(1)} %fusion.79) | copy-start | bytes 995332
  43.7 8.5 %collective-permute-start.2 = (bf16[2,6,6,512]{3,2,1,0:T(8,128)(2,1)S(1)}, bf16[2,6,6,512]{3,2,1,0:T(8,128)(2,1)S(1)}, u32[]{:S(2)}, u32[]{:S(2)}) collective-permute-start(bf16[2,6,6,512]{3,2,1,0:T(8,128)(2,1)S(1)} %get-tuple-element.19), channel_id=1, source_target_pairs={{0,32},{32,64},{64,96},{96,128},{128,160},{160,192},{192,224},{224... | collective-permute-start | bytes 221192 | tf_op jit(solution)/shard_map/ppermute | solution.py:21
  52.3 6.2 %collective-permute-start.3 = (bf16[2,12,3,512]{3,2,1,0:T(4,128)(2,1)S(1)}, bf16[2,12,3,512]{3,2,1,0:T(4,128)(2,1)S(1)}, u32[]{:S(2)}, u32[]{:S(2)}) collective-permute-start(bf16[2,12,3,512]{3,2,1,0:T(4,128)(2,1)S(1)} %fusion.76), channel_id=1, source_target_pairs={{0,1},{1,2},{2,3},{3,4},{4,5},{5,6},{6,7},{7,8},{8,9},{9,10},{10,1... | collective-permute-start | bytes 221192 | tf_op jit(solution)/shard_map/ppermute | solution.py:21
  61.7 6.2 %collective-permute-start.4 = (bf16[2,6,6,512]{3,2,1,0:T(8,128)(2,1)S(1)}, bf16[2,6,6,512]{3,2,1,0:T(8,128)(2,1)S(1)}, u32[]{:S(2)}, u32[]{:S(2)}) collective-permute-start(bf16[2,6,6,512]{3,2,1,0:T(8,128)(2,1)S(1)} %get-tuple-element.18), channel_id=1, source_target_pairs={{0,224},{32,0},{64,32},{96,64},{128,96},{160,128},{192,160},{224,1... | collective-permute-start | bytes 221192 | tf_op jit(solution)/shard_map/ppermute | solution.py:21
  68.0 2.3 %collective-permute-start.5 = (bf16[2,12,3,512]{3,2,1,0:T(4,128)(2,1)S(1)}, bf16[2,12,3,512]{3,2,1,0:T(4,128)(2,1)S(1)}, u32[]{:S(2)}, u32[]{:S(2)}) collective-permute-start(bf16[2,12,3,512]{3,2,1,0:T(4,128)(2,1)S(1)} %get-tuple-element.16), channel_id=1, source_target_pairs={{0,31},{1,0},{2,1},{3,2},{4,3},{5,4},{6,5},{7,6},{8,7},{9,8},{10,9... | collective-permute-start | bytes 221192 | tf_op jit(solution)/shard_map/ppermute | solution.py:21
  76.6 12.0 %slice-start = ((s8[9437184]{0:T(1024)(128)(4,1)}), s8[4194304]{0:T(1024)(128)(4,1)S(1)}, s32[]{:S(2)}) async-start(s8[9437184]{0:T(1024)(128)(4,1)} %bitcast.83), calls=%async_computation | async-start | bytes 8388608
  80.7 8.0 %slice-start.1 = ((s8[9437184]{0:T(1024)(128)(4,1)}), s8[4194304]{0:T(1024)(128)(4,1)S(1)}, s32[]{:S(2)}) async-start(s8[9437184]{0:T(1024)(128)(4,1)} %bitcast.83), calls=%async_computation.1 | async-start | bytes 8388608
  80.7 8.0 %slice-start.2 = ((s8[9437184]{0:T(1024)(128)(4,1)}), s8[1048576]{0:T(1024)(128)(4,1)S(1)}, s32[]{:S(2)}) async-start(s8[9437184]{0:T(1024)(128)(4,1)} %bitcast.83), calls=%async_computation.2 | async-start | bytes 2097152
  80.7 8.0 %copy-start.7 = (f32[8,2,12,6]{2,3,1,0:T(8,128)S(1)}, f32[8,2,12,6]{2,3,1,0:T(8,128)}, u32[]{:S(2)}) copy-start(f32[8,2,12,6]{2,3,1,0:T(8,128)} %copy-done.6) | copy-start | bytes 13828
  92.8 15.3 %copy-start.5 = (bf16[2,12,6,512]{3,2,1,0:T(8,128)(2,1)S(1)}, bf16[2,12,6,512]{3,2,1,0:T(8,128)(2,1)}, u32[]{:S(2)}) copy-start(bf16[2,12,6,512]{3,2,1,0:T(8,128)(2,1)} %get-tuple-element.12) | copy-start | bytes 442372
  99.5 8.3 %collective-permute-start.6 = (bf16[2,6,6,512]{3,2,1,0:T(8,128)(2,1)S(1)}, bf16[2,6,6,512]{3,2,1,0:T(8,128)(2,1)S(1)}, u32[]{:S(2)}, u32[]{:S(2)}) collective-permute-start(bf16[2,6,6,512]{3,2,1,0:T(8,128)(2,1)S(1)} %get-tuple-element.13), channel_id=1, source_target_pairs={{0,32},{32,64},{64,96},{96,128},{128,160},{160,192},{192,224},{224... | collective-permute-start | bytes 221192 | tf_op jit(solution)/shard_map/ppermute | solution.py:21
  107.9 6.2 %collective-permute-start.7 = (bf16[2,12,3,512]{3,2,1,0:T(4,128)(2,1)S(1)}, bf16[2,12,3,512]{3,2,1,0:T(4,128)(2,1)S(1)}, u32[]{:S(2)}, u32[]{:S(2)}) collective-permute-start(bf16[2,12,3,512]{3,2,1,0:T(4,128)(2,1)S(1)} %fusion.74), channel_id=1, source_target_pairs={{0,1},{1,2},{2,3},{3,4},{4,5},{5,6},{6,7},{7,8},{8,9},{9,10},{10,1... | collective-permute-start | bytes 221192 | tf_op jit(solution)/shard_map/ppermute | solution.py:21
where the time goes:
time: 116 us; the launch traced here: 115 us
  waiting for transfers between devices  35.3 us (30%)
  matrix products  25.1 us (22%)
  local copies, waits for them, and re-layouts  23.6 us (20%)
  starting transfers between devices  15.4 us (13%)
  other arithmetic  14.6 us (13%)
    ppermute x8, waiting for transfers between devices, passed_along(): lax.ppermute(shard, axis, [(i, (i + by) % devices) for i in range(devices)])  35.3 us
    ppermute x8, starting transfers between devices, passed_along(): lax.ppermute(shard, axis, [(i, (i + by) % devices) for i in range(devices)])  15.4 us
    dot_general x1, matrix products, attend_back(): jnp.einsum('larbchd,masbehd->abhlrcmse', grad_mixed, value_grid, preferre...  7.95 us
    another operation x3, local copies, waits for them, and re-layouts  4.75 us
    dot_general x1, matrix products, attend_back(): jnp.einsum('abhlrcmse,larbchd->masbehd', probs_grid, grad_mixed, preferre...  4.08 us
    convert_element_type x1, other arithmetic, attend_back(): grad_scores = grad_scores.astype(jnp.bfloat16).reshape(probs_grid.shape)  4.01 us
    unnamed x24, local copies, waits for them, and re-layouts  3.91 us
    reduce_sum x1, other arithmetic, attend(): probs = jax.nn.softmax(scores, axis=-1)  3.06 us
  transfers between devices with their start and end apart: 8, of which 8 were waited for; matrix products, arithmetic and copies ran while one was open for 1% of the time, Pallas kernels for 0%

commit v1 on v0

v1 whole, which is shorter than its diff:
```python
import math

import jax
import jax.numpy as jnp
from jax import lax
from jax.experimental import pallas as pl
from jax.experimental.pallas import tpu as pltpu
from jax.sharding import PartitionSpec as P

HEADS = 8
WLAT = 12
WLON = 6
SLAT = 6
SLON = 3

NORM_EPS = 1e-05
MASK_FILL = -1000000000.0


def neighbour(piece, lat_by, lon_by):
    lats, lons = lax.axis_size("lat"), lax.axis_size("lon")
    pairs = [
        (i * lons + j, (i + lat_by) % lats * lons + (j + lon_by) % lons)
        for i in range(lats)
        for j in range(lons)
    ]
    return lax.ppermute(piece, ("lat", "lon"), pairs)


def row_slices(rows, cols):
    late_rows, late_cols = pl.ds(SLAT, rows - SLAT), pl.ds(SLON, cols - SLON)
    early_rows, early_cols = pl.ds(0, SLAT), pl.ds(0, SLON)
    return (
        (late_rows, late_cols),
        (late_rows, early_cols),
        (early_rows, late_cols),
        (early_rows, early_cols),
    )


def cut_kernel(latent, cotangent, *rest):
    quarters, sems = rest[:4], rest[4]
    copies = []
    for k, (rows, cols) in enumerate(row_slices(latent.shape[0], latent.shape[1])):
        for f, field in enumerate((latent, cotangent)):
            copies.append(
                pltpu.make_async_copy(field.at[rows, cols], quarters[k].at[f], sems.at[k, f])
            )
    for copy in copies:
        copy.start()
    for copy in copies:
        copy.wait()


def join_kernel(*refs):
    quarters, outs, sems = refs[:4], refs[4:6], refs[6]
    copies = []
    for k, (rows, cols) in enumerate(row_slices(outs[0].shape[0], outs[0].shape[1])):
        for f, field in enumerate(outs):
            copies.append(
                pltpu.make_async_copy(quarters[k].at[f], field.at[rows, cols], sems.at[k, f])
            )
    for copy in copies:
        copy.start()
    for copy in copies:
        copy.wait()


def across(a, b):
    return lax.dot_general(a, b, (((1,), (1,)), ((), ())), preferred_element_type=jnp.float32)


def down(a, b):
    return lax.dot_general(a, b, (((0,), (0,)), ((), ())), preferred_element_type=jnp.float32)


def matmul(a, b):
    return jnp.dot(a, b, preferred_element_type=jnp.float32)


def window_kernel(
    own, ahead_lon, ahead_lat, ahead_both, gain_ref, qkv_ref, out_ref,
    own_out, lon_out, lat_out, both_out,
    tokens, cots, probs_ref, low_ref, proj_ref, mixed_ref, grad_ref,
):
    quarters = (own, ahead_lon, ahead_lat, ahead_both)
    results = (own_out, lon_out, lat_out, both_out)
    _, rows, cols, levels, features = own.shape
    quarter = rows * cols * levels
    window = 4 * quarter
    head_dim = features // HEADS
    scale = 1.0 / math.sqrt(head_dim)

    for k, ref in enumerate(quarters):
        for f, into in enumerate((tokens, cots)):
            for r in range(rows):
                for c in range(cols):
                    at = k * quarter + (r * cols + c) * levels
                    into[at : at + levels, :] = ref[f, r, c].astype(jnp.float32)

    proj_ref[...] = matmul(tokens[...].astype(jnp.bfloat16), qkv_ref[...]).astype(jnp.bfloat16)

    last = lax.axis_index("lat") == lax.axis_size("lat") - 1
    first_half = lambda d: lax.broadcasted_iota(jnp.int32, (window, window), d) < 2 * quarter
    fill = jnp.where(last, MASK_FILL, 0.0).astype(jnp.float32)
    bias = jnp.where(first_half(0) != first_half(1), fill, 0.0)
    lane = lax.broadcasted_iota(jnp.int32, (window, 2 * head_dim), 1)

    def masked(x, e):
        return jnp.where((lane >= head_dim) == bool(e), x, jnp.zeros_like(x))

    for pair in range(HEADS // 2):
        at = 2 * head_dim * pair
        wide = slice(at, at + 2 * head_dim)
        query = proj_ref[:, wide]
        key = proj_ref[:, features + at : features + at + 2 * head_dim]
        value = proj_ref[:, 2 * features + at : 2 * features + at + 2 * head_dim]
        mixed = None
        for e in range(2):
            scores = across(query, masked(key, e)) * scale + bias
            top = jnp.max(scores, axis=-1, keepdims=True)
            grown = jnp.exp(scores - top)
            probs = grown / jnp.sum(grown, axis=-1, keepdims=True)
            low = probs.astype(jnp.bfloat16)
            probs_ref[2 * pair + e] = probs
            low_ref[2 * pair + e] = low
            part = matmul(low, masked(value, e))
            mixed = part if mixed is None else mixed + part
        mixed_ref[:, wide] = mixed.astype(jnp.bfloat16)

    branch = matmul(mixed_ref[...], out_ref[...]).astype(jnp.bfloat16).astype(jnp.float32)
    gain = gain_ref[...]
    centred = branch - jnp.mean(branch, axis=-1, keepdims=True)
    inverse = lax.rsqrt(jnp.mean(centred * centred, axis=-1, keepdims=True) + NORM_EPS)
    normed = centred * inverse
    tokens[...] = tokens[...] + gain * normed
    upstream = gain * cots[...]
    centre_up = jnp.mean(upstream, axis=-1, keepdims=True)
    along = jnp.mean(upstream * normed, axis=-1, keepdims=True)
    grad_branch = (inverse * (upstream - centre_up - normed * along)).astype(jnp.bfloat16)
    mixed_ref[...] = across(grad_branch, out_ref[...]).astype(jnp.bfloat16)

    for pair in range(HEADS // 2):
        at = 2 * head_dim * pair
        wide = slice(at, at + 2 * head_dim)
        query = proj_ref[:, wide]
        key = proj_ref[:, features + at : features + at + 2 * head_dim]
        value = proj_ref[:, 2 * features + at : 2 * features + at + 2 * head_dim]
        grad_mixed = mixed_ref[:, wide]
        sums = [None, None, None]
        for e in range(2):
            probs = probs_ref[2 * pair + e]
            grad_probs = across(grad_mixed, masked(value, e))
            along = jnp.sum(grad_probs * probs, axis=-1, keepdims=True)
            grad_scores = (probs * (grad_probs - along) * scale).astype(jnp.bfloat16)
            parts = (
                matmul(grad_scores, masked(key, e)),
                down(grad_scores, masked(query, e)),
                down(low_ref[2 * pair + e], masked(grad_mixed, e)),
            )
            sums = [p if s is None else s + p for s, p in zip(sums, parts)]
        for part, total in enumerate(sums):
            grad_ref[:, part * features + at : part * features + at + 2 * head_dim] = total.astype(
                jnp.bfloat16
            )

    grad_tokens = across(grad_ref[...], qkv_ref[...]).astype(jnp.bfloat16).astype(jnp.float32)
    cots[...] = cots[...] + grad_tokens

    for k, ref in enumerate(results):
        for f, source in enumerate((tokens, cots)):
            for r in range(rows):
                for c in range(cols):
                    at = k * quarter + (r * cols + c) * levels
                    ref[f, r, c] = source[at : at + levels, :].astype(jnp.bfloat16)


def body(latent, cotangent, norm_gain, qkv_weight, out_weight):
    levels, rows, cols, features = latent.shape
    assert (rows, cols) == (WLAT, WLON) and (2 * SLAT, 2 * SLON) == (WLAT, WLON)
    window = levels * rows * cols
    quarter = (2, SLAT, SLON, levels, features)
    in_vmem = pl.BlockSpec(memory_space=pltpu.VMEM)
    anywhere = pl.BlockSpec(memory_space=pl.ANY)
    copies = pltpu.SemaphoreType.DMA((4, 2))

    own, to_lon, to_lat, to_both = pl.pallas_call(
        cut_kernel,
        in_specs=[anywhere] * 2,
        out_specs=[in_vmem] * 4,
        out_shape=[jax.ShapeDtypeStruct(quarter, jnp.bfloat16)] * 4,
        scratch_shapes=[copies],
        name="cut",
    )(latent.transpose(1, 2, 0, 3), cotangent.transpose(1, 2, 0, 3))

    from_both = neighbour(to_both, -1, -1)
    from_lat = neighbour(to_lat, -1, 0)
    from_lon = neighbour(to_lon, 0, -1)

    own, to_lon, to_lat, to_both = pl.pallas_call(
        window_kernel,
        in_specs=[in_vmem] * 7,
        out_specs=[in_vmem] * 4,
        out_shape=[jax.ShapeDtypeStruct(quarter, jnp.bfloat16)] * 4,
        scratch_shapes=[
            pltpu.VMEM((window, features), jnp.float32),
            pltpu.VMEM((window, features), jnp.float32),
            pltpu.VMEM((HEADS, window, window), jnp.float32),
            pltpu.VMEM((HEADS, window, window), jnp.bfloat16),
            pltpu.VMEM((window, 3 * features), jnp.bfloat16),
            pltpu.VMEM((window, features), jnp.bfloat16),
            pltpu.VMEM((window, 3 * features), jnp.bfloat16),
        ],
        compiler_params=pltpu.CompilerParams(vmem_limit_bytes=32 * 1024 * 1024),
        name="window",
    )(own, from_lon, from_lat, from_both, norm_gain.reshape(1, features), qkv_weight, out_weight)

    from_both = neighbour(to_both, 1, 1)
    from_lat = neighbour(to_lat, 1, 0)
    from_lon = neighbour(to_lon, 0, 1)

    updated, latent_grad = pl.pallas_call(
        join_kernel,
        in_specs=[in_vmem] * 4,
        out_specs=[anywhere] * 2,
        out_shape=[jax.ShapeDtypeStruct((rows, cols, levels, features), jnp.bfloat16)] * 2,
        scratch_shapes=[copies],
        name="join",
    )(own, from_lon, from_lat, from_both)
    return (updated.transpose(2, 0, 1, 3), latent_grad.transpose(2, 0, 1, 3))


def solution(mesh):
    placed = (P(None, "lat", "lon", None), P(None, "lat", "lon", None), P(), P(), P())
    return jax.shard_map(
        body,
        mesh=mesh,
        in_specs=placed,
        out_specs=(P(None, "lat", "lon", None), P(None, "lat", "lon", None)),
        check_vma=False,
    )
```

time: 116 us -> 41.7 us (0.36)
  the two profiles are of different devices: /device:TPU:2 before, /device:TPU:1 now
where the time goes in v1:
time: 41.7 us; the launch traced here: 41.3 us
  starting transfers between devices  15.4 us (37%)
  waiting for transfers between devices  11.9 us (29%)
  Pallas kernels  8.03 us (19%)
  local copies, waits for them, and re-layouts  5.28 us (13%)
  between operations  0.67 us (2%)
    ppermute x6, starting transfers between devices, neighbour(): return lax.ppermute(piece, ('lat', 'lon'), pairs)  15.4 us
    ppermute x6, waiting for transfers between devices, neighbour(): return lax.ppermute(piece, ('lat', 'lon'), pairs)  11.9 us
    unnamed x16, local copies, waits for them, and re-layouts  5.28 us
    pallas_call x1, Pallas kernels, body(): pl.pallas_call(window_kernel, in_specs=[in_vmem] * 7, out_specs=[in_vmem]...  4.59 us
    pallas_call x1, Pallas kernels, body(): pl.pallas_call(join_kernel, in_specs=[in_vmem] * 4, out_specs=[anywhere]...  1.76 us
    pallas_call x1, Pallas kernels, body(): pl.pallas_call(cut_kernel, in_specs=[anywhere] * 2, out_specs=[in_vmem] *...  1.68 us
  transfers between devices with their start and end apart: 6, of which 4 were waited for; matrix products, arithmetic and copies ran while one was open for 0% of the time, Pallas kernels for 0%

profile of v1, /device:TPU:1, one launch (start us, length us, event | category | flops | bytes accessed | tf_op | source)
XLA Modules:
  0.0 41.3 jit_solution(6643741297594141417)
XLA Ops:
  0.6 1.7 %cut.1 = (bf16[2,6,3,2,512]{4,3,2,1,0:T(2,128)(2,1)}, bf16[2,6,3,2,512]{4,3,2,1,0:T(2,128)(2,1)}, bf16[2,6,3,2,512]{4,3,2,1,0:T(2,128)(2,1)}, bf16[2,6,3,2,512]{4,3,2,1,0:T(2,128)(2,1)}) custom-call(bf16[12,6,2,512]{3,2,1,0:T(2,128)(2,1)} %bitcast.6, bf16[12,6,2,512]{3,2,1,0:T(2,128)(2,1)} %bitcast.7), custom_call_target="tpu_custom_call" | custom-call | tf_op jit(solution)/shard_map/cut/pallas_call | solution.py:187
  2.3 3.3 %collective-permute-start = (bf16[2,6,3,2,512]{4,3,2,1,0:T(2,128)(2,1)}, bf16[2,6,3,2,512]{4,3,2,1,0:T(2,128)(2,1)S(1)}, u32[]{:S(2)}, u32[]{:S(2)}) collective-permute-start(bf16[2,6,3,2,512]{4,3,2,1,0:T(2,128)(2,1)} %get-tuple-element.13), channel_id=1, source_target_pairs={{0,31},{1,0},{2,1},{3,2},{4,3},{5,4},{6,5},{7,6},{8,7},{9,8},{10,9... | collective-permute-start | bytes 221192 | tf_op jit(solution)/shard_map/ppermute | solution.py:27
  5.6 3.5 %collective-permute-start.1 = (bf16[2,6,3,2,512]{4,3,2,1,0:T(2,128)(2,1)}, bf16[2,6,3,2,512]{4,3,2,1,0:T(2,128)(2,1)S(1)}, u32[]{:S(2)}, u32[]{:S(2)}) collective-permute-start(bf16[2,6,3,2,512]{4,3,2,1,0:T(2,128)(2,1)} %get-tuple-element.14), channel_id=1, source_target_pairs={{0,224},{1,225},{2,226},{3,227},{4,228},{5,229},{6,230},{7,231},{8... | collective-permute-start | bytes 221192 | tf_op jit(solution)/shard_map/ppermute | solution.py:27
  9.1 6.6 %collective-permute-start.2 = (bf16[2,6,3,2,512]{4,3,2,1,0:T(2,128)(2,1)}, bf16[2,6,3,2,512]{4,3,2,1,0:T(2,128)(2,1)S(1)}, u32[]{:S(2)}, u32[]{:S(2)}) collective-permute-start(bf16[2,6,3,2,512]{4,3,2,1,0:T(2,128)(2,1)} %get-tuple-element.15), channel_id=1, source_target_pairs={{0,255},{1,224},{2,225},{3,226},{4,227},{5,228},{6,229},{7,230},{8... | collective-permute-start | bytes 221192 | tf_op jit(solution)/shard_map/ppermute | solution.py:27
  15.7 0.0 collective-permute-done.ahead_lon
  15.7 0.0 collective-permute-done.1.ahead_lat
  15.7 2.2 %collective-permute-done.2.ahead_both = bf16[2,6,3,2,512]{4,3,2,1,0:T(2,128)(2,1)S(1)} collective-permute-done((bf16[2,6,3,2,512]{4,3,2,1,0:T(2,128)(2,1)}, bf16[2,6,3,2,512]{4,3,2,1,0:T(2,128)(2,1)S(1)}, u32[]{:S(2)}, u32[]{:S(2)}) %collective-permute-start.2) | collective-permute-done | bytes 73760 | tf_op jit(solution)/shard_map/ppermute | solution.py:27
  17.9 0.0 copy-start
  17.9 1.4 %copy-done = bf16[512,1536]{1,0:T(8,128)(2,1)S(1)} copy-done((bf16[512,1536]{1,0:T(8,128)(2,1)S(1)}, bf16[512,1536]{1,0:T(8,128)(2,1)}, u32[]{:S(2)}) %copy-start) | copy-done | bytes 1572888
  19.3 0.0 copy-start.1
  19.3 1.0 %copy-done.1 = bf16[512,512]{1,0:T(8,128)(2,1)S(1)} copy-done((bf16[512,512]{1,0:T(8,128)(2,1)S(1)}, bf16[512,512]{1,0:T(8,128)(2,1)}, u32[]{:S(2)}) %copy-start.1) | copy-done | bytes 524312
  20.3 0.0 copy-start.2
  20.3 0.9 %copy-done.2 = bf16[2,6,3,2,512]{4,3,2,1,0:T(2,128)(2,1)S(1)} copy-done((bf16[2,6,3,2,512]{4,3,2,1,0:T(2,128)(2,1)S(1)}, bf16[2,6,3,2,512]{4,3,2,1,0:T(2,128)(2,1)}, u32[]{:S(2)}) %copy-start.2) | copy-done | bytes 73752
  21.2 0.0 copy-start.4
  21.2 0.7 %copy-done.4 = f32[512]{0:T(512)S(1)} copy-done((f32[512]{0:T(512)S(1)}, f32[512]{0:T(512)}, u32[]{:S(2)}) %copy-start.4) | copy-done | bytes 2072
  21.9 4.6 %window.1 = (bf16[2,6,3,2,512]{4,3,2,1,0:T(2,128)(2,1)S(1)}, bf16[2,6,3,2,512]{4,3,2,1,0:T(2,128)(2,1)S(1)}, bf16[2,6,3,2,512]{4,3,2,1,0:T(2,128)(2,1)S(1)}, bf16[2,6,3,2,512]{4,3,2,1,0:T(2,128)(2,1)S(1)}) custom-call(bf16[2,6,3,2,512]{4,3,2,1,0:T(2,128)(2,1)S(1)} %copy-done.2, bf16[2,6,3,2,512]{4,3,2,1,0:T(2,128)(2,1)S(1)} %collective-permute-done.ahead_lon, ...), custom_call_target="tpu_custom_call" | custom-call | tf_op jit(solution)/shard_map/window/pallas_call | solution.py:200
  26.5 0.0 copy-start.3
  26.5 0.6 %copy-done.3 = bf16[2,6,3,2,512]{4,3,2,1,0:T(2,128)(2,1)} copy-done((bf16[2,6,3,2,512]{4,3,2,1,0:T(2,128)(2,1)}, bf16[2,6,3,2,512]{4,3,2,1,0:T(2,128)(2,1)S(1)}, u32[]{:S(2)}) %copy-start.3) | copy-done | bytes 73752
  27.1 0.0 collective-permute-start.3
  27.1 2.0 %collective-permute-start.4 = (bf16[2,6,3,2,512]{4,3,2,1,0:T(2,128)(2,1)S(1)}, bf16[2,6,3,2,512]{4,3,2,1,0:T(2,128)(2,1)S(1)}, u32[]{:S(2)}, u32[]{:S(2)}) collective-permute-start(bf16[2,6,3,2,512]{4,3,2,1,0:T(2,128)(2,1)S(1)} %get-tuple-element.18), channel_id=1, source_target_pairs={{0,32},{1,33},{2,34},{3,35},{4,36},{5,37},{6,38},{7,39},{8,40},{9,... | collective-permute-start | bytes 221192 | tf_op jit(solution)/shard_map/ppermute | solution.py:27
  29.1 0.0 collective-permute-start.5
  29.1 1.7 %collective-permute-done.3.refs_1_ = bf16[2,6,3,2,512]{4,3,2,1,0:T(2,128)(2,1)S(1)} collective-permute-done((bf16[2,6,3,2,512]{4,3,2,1,0:T(2,128)(2,1)S(1)}, bf16[2,6,3,2,512]{4,3,2,1,0:T(2,128)(2,1)S(1)}, u32[]{:S(2)}, u32[]{:S(2)}) %collective-permute-start.3) | collective-permute-done | bytes 73760 | tf_op jit(solution)/shard_map/ppermute | solution.py:27
  30.8 0.0 copy-start.5
  30.8 3.2 %collective-permute-done.4.refs_2_ = bf16[2,6,3,2,512]{4,3,2,1,0:T(2,128)(2,1)S(1)} collective-permute-done((bf16[2,6,3,2,512]{4,3,2,1,0:T(2,128)(2,1)S(1)}, bf16[2,6,3,2,512]{4,3,2,1,0:T(2,128)(2,1)S(1)}, u32[]{:S(2)}, u32[]{:S(2)}) %collective-permute-start.4) | collective-permute-done | bytes 73760 | tf_op jit(solution)/shard_map/ppermute | solution.py:27
  34.0 0.0 copy-start.6
  34.0 4.9 %collective-permute-done.5.refs_3_ = bf16[2,6,3,2,512]{4,3,2,1,0:T(2,128)(2,1)S(1)} collective-permute-done((bf16[2,6,3,2,512]{4,3,2,1,0:T(2,128)(2,1)S(1)}, bf16[2,6,3,2,512]{4,3,2,1,0:T(2,128)(2,1)S(1)}, u32[]{:S(2)}, u32[]{:S(2)}) %collective-permute-start.5) | collective-permute-done | bytes 73760 | tf_op jit(solution)/shard_map/ppermute | solution.py:27
  38.9 0.0 copy-start.7
  38.9 0.0 copy-done.5
  38.9 0.0 copy-done.6
  38.9 0.6 %copy-done.7 = bf16[2,6,3,2,512]{4,3,2,1,0:T(2,128)(2,1)} copy-done((bf16[2,6,3,2,512]{4,3,2,1,0:T(2,128)(2,1)}, bf16[2,6,3,2,512]{4,3,2,1,0:T(2,128)(2,1)S(1)}, u32[]{:S(2)}) %copy-start.7) | copy-done | bytes 73752
  39.5 1.8 %join.1 = (bf16[12,6,2,512]{3,2,1,0:T(2,128)(2,1)}, bf16[12,6,2,512]{3,2,1,0:T(2,128)(2,1)}) custom-call(bf16[2,6,3,2,512]{4,3,2,1,0:T(2,128)(2,1)} %copy-done.3, bf16[2,6,3,2,512]{4,3,2,1,0:T(2,128)(2,1)} %copy-done.5, bf16[2,6,3,2,512]{4,3,2,1,0:T(2,128)(2,1)} %copy-done.6, bf16[2,6,3,2,512]{4,3,2,1,0:T(2,128)(2,1)} %copy-done.7), custom_call_target="tpu_custom_call" | custom-call | tf_op jit(solution)/shard_map/join/pallas_call | solution.py:222
Async XLA Ops:
  2.3 13.4 %collective-permute-start = (bf16[2,6,3,2,512]{4,3,2,1,0:T(2,128)(2,1)}, bf16[2,6,3,2,512]{4,3,2,1,0:T(2,128)(2,1)S(1)}, u32[]{:S(2)}, u32[]{:S(2)}) collective-permute-start(bf16[2,6,3,2,512]{4,3,2,1,0:T(2,128)(2,1)} %get-tuple-element.13), channel_id=1, source_target_pairs={{0,31},{1,0},{2,1},{3,2},{4,3},{5,4},{6,5},{7,6},{8,7},{9,8},{10,9... | collective-permute-start | bytes 221192 | tf_op jit(solution)/shard_map/ppermute | solution.py:27
  5.6 10.1 %collective-permute-start.1 = (bf16[2,6,3,2,512]{4,3,2,1,0:T(2,128)(2,1)}, bf16[2,6,3,2,512]{4,3,2,1,0:T(2,128)(2,1)S(1)}, u32[]{:S(2)}, u32[]{:S(2)}) collective-permute-start(bf16[2,6,3,2,512]{4,3,2,1,0:T(2,128)(2,1)} %get-tuple-element.14), channel_id=1, source_target_pairs={{0,224},{1,225},{2,226},{3,227},{4,228},{5,229},{6,230},{7,231},{8... | collective-permute-start | bytes 221192 | tf_op jit(solution)/shard_map/ppermute | solution.py:27
  9.1 8.8 %collective-permute-start.2 = (bf16[2,6,3,2,512]{4,3,2,1,0:T(2,128)(2,1)}, bf16[2,6,3,2,512]{4,3,2,1,0:T(2,128)(2,1)S(1)}, u32[]{:S(2)}, u32[]{:S(2)}) collective-permute-start(bf16[2,6,3,2,512]{4,3,2,1,0:T(2,128)(2,1)} %get-tuple-element.15), channel_id=1, source_target_pairs={{0,255},{1,224},{2,225},{3,226},{4,227},{5,228},{6,229},{7,230},{8... | collective-permute-start | bytes 221192 | tf_op jit(solution)/shard_map/ppermute | solution.py:27
  17.9 1.4 %copy-start = (bf16[512,1536]{1,0:T(8,128)(2,1)S(1)}, bf16[512,1536]{1,0:T(8,128)(2,1)}, u32[]{:S(2)}) copy-start(bf16[512,1536]{1,0:T(8,128)(2,1)} %qkv_ref.1) | copy-start | bytes 4718596
  19.3 1.0 %copy-start.1 = (bf16[512,512]{1,0:T(8,128)(2,1)S(1)}, bf16[512,512]{1,0:T(8,128)(2,1)}, u32[]{:S(2)}) copy-start(bf16[512,512]{1,0:T(8,128)(2,1)} %out_ref.1) | copy-start | bytes 1572868
  20.3 0.9 %copy-start.2 = (bf16[2,6,3,2,512]{4,3,2,1,0:T(2,128)(2,1)S(1)}, bf16[2,6,3,2,512]{4,3,2,1,0:T(2,128)(2,1)}, u32[]{:S(2)}) copy-start(bf16[2,6,3,2,512]{4,3,2,1,0:T(2,128)(2,1)} %get-tuple-element.12.own) | copy-start | bytes 221188
  21.2 0.7 %copy-start.4 = (f32[512]{0:T(512)S(1)}, f32[512]{0:T(512)}, u32[]{:S(2)}) copy-start(f32[512]{0:T(512)} %param.7) | copy-start | bytes 6148
  26.5 0.6 %copy-start.3 = (bf16[2,6,3,2,512]{4,3,2,1,0:T(2,128)(2,1)}, bf16[2,6,3,2,512]{4,3,2,1,0:T(2,128)(2,1)S(1)}, u32[]{:S(2)}) copy-start(bf16[2,6,3,2,512]{4,3,2,1,0:T(2,128)(2,1)S(1)} %get-tuple-element.16.refs_0_) | copy-start | bytes 221188
  27.1 3.7 %collective-permute-start.3 = (bf16[2,6,3,2,512]{4,3,2,1,0:T(2,128)(2,1)S(1)}, bf16[2,6,3,2,512]{4,3,2,1,0:T(2,128)(2,1)S(1)}, u32[]{:S(2)}, u32[]{:S(2)}) collective-permute-start(bf16[2,6,3,2,512]{4,3,2,1,0:T(2,128)(2,1)S(1)} %get-tuple-element.17), channel_id=1, source_target_pairs={{0,1},{1,2},{2,3},{3,4},{4,5},{5,6},{6,7},{7,8},{8,9},{9,10},{10,1... | collective-permute-start | bytes 221192 | tf_op jit(solution)/shard_map/ppermute | solution.py:27
  27.1 6.8 %collective-permute-start.4 = (bf16[2,6,3,2,512]{4,3,2,1,0:T(2,128)(2,1)S(1)}, bf16[2,6,3,2,512]{4,3,2,1,0:T(2,128)(2,1)S(1)}, u32[]{:S(2)}, u32[]{:S(2)}) collective-permute-start(bf16[2,6,3,2,512]{4,3,2,1,0:T(2,128)(2,1)S(1)} %get-tuple-element.18), channel_id=1, source_target_pairs={{0,32},{1,33},{2,34},{3,35},{4,36},{5,37},{6,38},{7,39},{8,40},{9,... | collective-permute-start | bytes 221192 | tf_op jit(solution)/shard_map/ppermute | solution.py:27
  29.1 9.8 %collective-permute-start.5 = (bf16[2,6,3,2,512]{4,3,2,1,0:T(2,128)(2,1)S(1)}, bf16[2,6,3,2,512]{4,3,2,1,0:T(2,128)(2,1)S(1)}, u32[]{:S(2)}, u32[]{:S(2)}) collective-permute-start(bf16[2,6,3,2,512]{4,3,2,1,0:T(2,128)(2,1)S(1)} %get-tuple-element.19), channel_id=1, source_target_pairs={{0,33},{1,34},{2,35},{3,36},{4,37},{5,38},{6,39},{7,40},{8,41},{9,... | collective-permute-start | bytes 221192 | tf_op jit(solution)/shard_map/ppermute | solution.py:27
  30.8 8.1 %copy-start.5 = (bf16[2,6,3,2,512]{4,3,2,1,0:T(2,128)(2,1)}, bf16[2,6,3,2,512]{4,3,2,1,0:T(2,128)(2,1)S(1)}, u32[]{:S(2)}) copy-start(bf16[2,6,3,2,512]{4,3,2,1,0:T(2,128)(2,1)S(1)} %collective-permute-done.3.refs_1_) | copy-start | bytes 221188
  34.0 5.0 %copy-start.6 = (bf16[2,6,3,2,512]{4,3,2,1,0:T(2,128)(2,1)}, bf16[2,6,3,2,512]{4,3,2,1,0:T(2,128)(2,1)S(1)}, u32[]{:S(2)}) copy-start(bf16[2,6,3,2,512]{4,3,2,1,0:T(2,128)(2,1)S(1)} %collective-permute-done.4.refs_2_) | copy-start | bytes 221188
  38.9 0.6 %copy-start.7 = (bf16[2,6,3,2,512]{4,3,2,1,0:T(2,128)(2,1)}, bf16[2,6,3,2,512]{4,3,2,1,0:T(2,128)(2,1)S(1)}, u32[]{:S(2)}) copy-start(bf16[2,6,3,2,512]{4,3,2,1,0:T(2,128)(2,1)S(1)} %collective-permute-done.5.refs_3_) | copy-start | bytes 221188

commit v2 on v1

--- a/solution.py
+++ b/solution.py
@@ -13,6 +13,7 @@
 SLAT = 6
 SLON = 3
 
+MIB = 1 << 20
 NORM_EPS = 1e-05
 MASK_FILL = -1000000000.0
 
@@ -38,13 +39,17 @@
     )
 
 
+def stay(x):
+    return pltpu.with_memory_space_constraint(x, pltpu.HBM)
+
+
 def cut_kernel(latent, cotangent, *rest):
-    quarters, sems = rest[:4], rest[4]
+    pieces, sems = rest[:3], rest[3]
     copies = []
-    for k, (rows, cols) in enumerate(row_slices(latent.shape[0], latent.shape[1])):
+    for k, (rows, cols) in enumerate(row_slices(latent.shape[0], latent.shape[1])[1:]):
         for f, field in enumerate((latent, cotangent)):
             copies.append(
-                pltpu.make_async_copy(field.at[rows, cols], quarters[k].at[f], sems.at[k, f])
+                pltpu.make_async_copy(field.at[rows, cols], pieces[k].at[f], sems.at[k, f])
             )
     for copy in copies:
         copy.start()
@@ -52,8 +57,23 @@
         copy.wait()
 
 
+def fetch_kernel(latent, cotangent, gain, qkv, out, own, gain_to, qkv_to, out_to, sems):
+    rows, cols = row_slices(latent.shape[0], latent.shape[1])[0]
+    copies = [
+        pltpu.make_async_copy(qkv, qkv_to, sems.at[0]),
+        pltpu.make_async_copy(out, out_to, sems.at[1]),
+        pltpu.make_async_copy(gain, gain_to, sems.at[2]),
+        pltpu.make_async_copy(latent.at[rows, cols], own.at[0], sems.at[3]),
+        pltpu.make_async_copy(cotangent.at[rows, cols], own.at[1], sems.at[4]),
+    ]
+    for copy in copies:
+        copy.start()
+    for copy in copies:
+        copy.wait()
+
+
 def join_kernel(*refs):
-    quarters, outs, sems = refs[:4], refs[4:6], refs[6]
+    quarters, outs, sems = refs[3::-1], refs[4:6], refs[6]
     copies = []
     for k, (rows, cols) in enumerate(row_slices(outs[0].shape[0], outs[0].shape[1])):
         for f, field in enumerate(outs):
@@ -79,8 +99,8 @@
 
 
 def window_kernel(
-    own, ahead_lon, ahead_lat, ahead_both, gain_ref, qkv_ref, out_ref,
-    own_out, lon_out, lat_out, both_out,
+    ahead_both, ahead_lat, ahead_lon, own, gain_ref, qkv_ref, out_ref,
+    both_out, lat_out, lon_out, own_out,
     tokens, cots, probs_ref, low_ref, proj_ref, mixed_ref, grad_ref,
 ):
     quarters = (own, ahead_lon, ahead_lat, ahead_both)
@@ -181,27 +201,46 @@
     window = levels * rows * cols
     quarter = (2, SLAT, SLON, levels, features)
     in_vmem = pl.BlockSpec(memory_space=pltpu.VMEM)
-    anywhere = pl.BlockSpec(memory_space=pl.ANY)
-    copies = pltpu.SemaphoreType.DMA((4, 2))
-
-    own, to_lon, to_lat, to_both = pl.pallas_call(
+    in_hbm = pl.BlockSpec(memory_space=pltpu.HBM)
+    piece = pltpu.VMEM(quarter, jnp.bfloat16)
+    few = pltpu.CompilerParams(vmem_limit_bytes=MIB)
+    latent, cotangent = latent.transpose(1, 2, 0, 3), cotangent.transpose(1, 2, 0, 3)
+
+    to_lon, to_lat, to_both = pl.pallas_call(
         cut_kernel,
-        in_specs=[anywhere] * 2,
-        out_specs=[in_vmem] * 4,
-        out_shape=[jax.ShapeDtypeStruct(quarter, jnp.bfloat16)] * 4,
-        scratch_shapes=[copies],
+        in_specs=[in_hbm] * 2,
+        out_specs=[in_vmem] * 3,
+        out_shape=[piece] * 3,
+        scratch_shapes=[pltpu.SemaphoreType.DMA((3, 2))],
+        compiler_params=few,
         name="cut",
-    )(latent.transpose(1, 2, 0, 3), cotangent.transpose(1, 2, 0, 3))
+    )(stay(latent), stay(cotangent))
 
     from_both = neighbour(to_both, -1, -1)
     from_lat = neighbour(to_lat, -1, 0)
     from_lon = neighbour(to_lon, 0, -1)
 
-    own, to_lon, to_lat, to_both = pl.pallas_call(
+    own, gain, qkv, out = pl.pallas_call(
+        fetch_kernel,
+        in_specs=[in_hbm] * 5,
+        out_specs=[in_vmem] * 4,
+        out_shape=[
+            piece,
+            pltpu.VMEM((1, features), jnp.float32),
+            pltpu.VMEM(qkv_weight.shape, jnp.bfloat16),
+            pltpu.VMEM(out_weight.shape, jnp.bfloat16),
+        ],
+        scratch_shapes=[pltpu.SemaphoreType.DMA((5,))],
+        compiler_params=few,
+        cost_estimate=pl.CostEstimate(flops=0, bytes_accessed=4 * MIB, transcendentals=0),
+        name="fetch",
+    )(*map(stay, (latent, cotangent, norm_gain.reshape(1, features), qkv_weight, out_weight)))
+
+    to_both, to_lat, to_lon, own = pl.pallas_call(
         window_kernel,
         in_specs=[in_vmem] * 7,
         out_specs=[in_vmem] * 4,
-        out_shape=[jax.ShapeDtypeStruct(quarter, jnp.bfloat16)] * 4,
+        out_shape=[piece] * 4,
         scratch_shapes=[
             pltpu.VMEM((window, features), jnp.float32),
             pltpu.VMEM((window, features), jnp.float32),
@@ -211,9 +250,9 @@
             pltpu.VMEM((window, features), jnp.bfloat16),
             pltpu.VMEM((window, 3 * features), jnp.bfloat16),
         ],
-        compiler_params=pltpu.CompilerParams(vmem_limit_bytes=32 * 1024 * 1024),
+        compiler_params=pltpu.CompilerParams(vmem_limit_bytes=12 * MIB),
         name="window",
-    )(own, from_lon, from_lat, from_both, norm_gain.reshape(1, features), qkv_weight, out_weight)
+    )(from_both, from_lat, from_lon, own, gain, qkv, out)
 
     from_both = neighbour(to_both, 1, 1)
     from_lat = neighbour(to_lat, 1, 0)
@@ -222,11 +261,12 @@
     updated, latent_grad = pl.pallas_call(
         join_kernel,
         in_specs=[in_vmem] * 4,
-        out_specs=[anywhere] * 2,
+        out_specs=[in_hbm] * 2,
         out_shape=[jax.ShapeDtypeStruct((rows, cols, levels, features), jnp.bfloat16)] * 2,
-        scratch_shapes=[copies],
+        scratch_shapes=[pltpu.SemaphoreType.DMA((4, 2))],
+        compiler_params=few,
         name="join",
-    )(own, from_lon, from_lat, from_both)
+    )(from_both, from_lat, from_lon, own)
     return (updated.transpose(2, 0, 1, 3), latent_grad.transpose(2, 0, 1, 3))
 
 

time: 41.7 us -> 30.6 us (0.73)
  the two profiles are of different devices: /device:TPU:1 before, /device:TPU:2 now
where the time goes in v2:
time: 30.6 us; the launch traced here: 30.4 us
  starting transfers between devices  12.6 us (41%)
  waiting for transfers between devices  9.28 us (30%)
  Pallas kernels  7.83 us (26%)
  between operations  0.67 us (2%)
    ppermute x6, starting transfers between devices, neighbour(): return lax.ppermute(piece, ('lat', 'lon'), pairs)  12.6 us
    ppermute x6, waiting for transfers between devices, neighbour(): return lax.ppermute(piece, ('lat', 'lon'), pairs)  9.28 us
    pallas_call x1, Pallas kernels, body(): pl.pallas_call(window_kernel, in_specs=[in_vmem] * 7, out_specs=[in_vmem]...  4.58 us
    pallas_call x1, Pallas kernels, body(): pl.pallas_call(fetch_kernel, in_specs=[in_hbm] * 5, out_specs=[in_vmem] *...  1.56 us
    pallas_call x1, Pallas kernels, body(): pl.pallas_call(cut_kernel, in_specs=[in_hbm] * 2, out_specs=[in_vmem] * 3...  0.91 us
    pallas_call x1, Pallas kernels, body(): pl.pallas_call(join_kernel, in_specs=[in_vmem] * 4, out_specs=[in_hbm] *...  0.77 us
  transfers between devices with their start and end apart: 6, of which 3 were waited for; matrix products, arithmetic and copies ran while one was open for 0% of the time, Pallas kernels for 5%

profile of v2, /device:TPU:2, one launch (start us, length us, event | category | flops | bytes accessed | tf_op | source)
XLA Modules:
  0.0 30.4 jit_solution(10989794762402297281)
XLA Ops:
  0.6 0.9 %cut.1 = (bf16[2,6,3,2,512]{4,3,2,1,0:T(2,128)(2,1)S(1)}, bf16[2,6,3,2,512]{4,3,2,1,0:T(2,128)(2,1)S(1)}, bf16[2,6,3,2,512]{4,3,2,1,0:T(2,128)(2,1)S(1)}) custom-call(bf16[12,6,2,512]{3,2,1,0:T(2,128)(2,1)} %bitcast.5, bf16[12,6,2,512]{3,2,1,0:T(2,128)(2,1)} %bitcast.7), custom_call_target="tpu_custom_call" | custom-call | tf_op jit(solution)/shard_map/cut/pallas_call | solution.py:209
  1.6 8.8 %collective-permute-start = (bf16[2,6,3,2,512]{4,3,2,1,0:T(2,128)(2,1)S(1)}, bf16[2,6,3,2,512]{4,3,2,1,0:T(2,128)(2,1)S(1)}, u32[]{:S(2)}, u32[]{:S(2)}) collective-permute-start(bf16[2,6,3,2,512]{4,3,2,1,0:T(2,128)(2,1)S(1)} %get-tuple-element.15), channel_id=1, source_target_pairs={{0,255},{1,224},{2,225},{3,226},{4,227},{5,228},{6,229},{7,230},{8... | collective-permute-start | bytes 221192 | tf_op jit(solution)/shard_map/ppermute | solution.py:28
  10.3 1.1 %collective-permute-start.1 = (bf16[2,6,3,2,512]{4,3,2,1,0:T(2,128)(2,1)S(1)}, bf16[2,6,3,2,512]{4,3,2,1,0:T(2,128)(2,1)S(1)}, u32[]{:S(2)}, u32[]{:S(2)}) collective-permute-start(bf16[2,6,3,2,512]{4,3,2,1,0:T(2,128)(2,1)S(1)} %get-tuple-element.16), channel_id=1, source_target_pairs={{0,224},{1,225},{2,226},{3,227},{4,228},{5,229},{6,230},{7,231},{8... | collective-permute-start | bytes 221192 | tf_op jit(solution)/shard_map/ppermute | solution.py:28
  11.4 1.5 %collective-permute-start.2 = (bf16[2,6,3,2,512]{4,3,2,1,0:T(2,128)(2,1)S(1)}, bf16[2,6,3,2,512]{4,3,2,1,0:T(2,128)(2,1)S(1)}, u32[]{:S(2)}, u32[]{:S(2)}) collective-permute-start(bf16[2,6,3,2,512]{4,3,2,1,0:T(2,128)(2,1)S(1)} %get-tuple-element.17), channel_id=1, source_target_pairs={{0,31},{1,0},{2,1},{3,2},{4,3},{5,4},{6,5},{7,6},{8,7},{9,8},{10,9... | collective-permute-start | bytes 221192 | tf_op jit(solution)/shard_map/ppermute | solution.py:28
  12.9 1.6 %fetch.1 = (bf16[2,6,3,2,512]{4,3,2,1,0:T(2,128)(2,1)S(1)}, f32[1,512]{1,0:T(1,128)S(1)}, bf16[512,1536]{1,0:T(8,128)(2,1)S(1)}, bf16[512,512]{1,0:T(8,128)(2,1)S(1)}) custom-call(bf16[12,6,2,512]{3,2,1,0:T(2,128)(2,1)} %bitcast.6, bf16[12,6,2,512]{3,2,1,0:T(2,128)(2,1)} %bitcast.8, f32[1,512]{1,0:T(1,128)} %bitcast.9, bf16[512,1536]{1,0:T(8,128)(2,1)} %qkv.1, ...), custom_call_target="tpu_custom_call" | custom-call | bytes 4194304 | tf_op jit(solution)/shard_map/fetch/pallas_call | solution.py:223
  14.4 0.0 collective-permute-done.ahead_both
  14.5 1.7 %collective-permute-done.1.ahead_lat = bf16[2,6,3,2,512]{4,3,2,1,0:T(2,128)(2,1)S(1)} collective-permute-done((bf16[2,6,3,2,512]{4,3,2,1,0:T(2,128)(2,1)S(1)}, bf16[2,6,3,2,512]{4,3,2,1,0:T(2,128)(2,1)S(1)}, u32[]{:S(2)}, u32[]{:S(2)}) %collective-permute-start.1) | collective-permute-done | bytes 73760 | tf_op jit(solution)/shard_map/ppermute | solution.py:28
  16.2 0.0 collective-permute-done.2.ahead_lon
  16.2 4.6 %window.1 = (bf16[2,6,3,2,512]{4,3,2,1,0:T(2,128)(2,1)S(1)}, bf16[2,6,3,2,512]{4,3,2,1,0:T(2,128)(2,1)S(1)}, bf16[2,6,3,2,512]{4,3,2,1,0:T(2,128)(2,1)S(1)}, bf16[2,6,3,2,512]{4,3,2,1,0:T(2,128)(2,1)S(1)}) custom-call(bf16[2,6,3,2,512]{4,3,2,1,0:T(2,128)(2,1)S(1)} %collective-permute-done.ahead_both, ...), custom_call_target="tpu_custom_call" | custom-call | tf_op jit(solution)/shard_map/window/pallas_call | solution.py:239
  20.7 0.1 collective-permute-start.3
  20.8 1.2 %collective-permute-start.4 = (bf16[2,6,3,2,512]{4,3,2,1,0:T(2,128)(2,1)S(1)}, bf16[2,6,3,2,512]{4,3,2,1,0:T(2,128)(2,1)S(1)}, u32[]{:S(2)}, u32[]{:S(2)}) collective-permute-start(bf16[2,6,3,2,512]{4,3,2,1,0:T(2,128)(2,1)S(1)} %get-tuple-element.23), channel_id=1, source_target_pairs={{0,32},{1,33},{2,34},{3,35},{4,36},{5,37},{6,38},{7,39},{8,40},{9,... | collective-permute-start | bytes 221192 | tf_op jit(solution)/shard_map/ppermute | solution.py:28
  22.0 0.0 collective-permute-start.5
  22.0 7.5 %collective-permute-done.3.refs_0_ = bf16[2,6,3,2,512]{4,3,2,1,0:T(2,128)(2,1)S(1)} collective-permute-done((bf16[2,6,3,2,512]{4,3,2,1,0:T(2,128)(2,1)S(1)}, bf16[2,6,3,2,512]{4,3,2,1,0:T(2,128)(2,1)S(1)}, u32[]{:S(2)}, u32[]{:S(2)}) %collective-permute-start.3) | collective-permute-done | bytes 73760 | tf_op jit(solution)/shard_map/ppermute | solution.py:28
  29.5 0.1 collective-permute-done.4.refs_1_
  29.6 0.0 collective-permute-done.5.refs_2_
  29.6 0.8 %join.1 = (bf16[12,6,2,512]{3,2,1,0:T(2,128)(2,1)}, bf16[12,6,2,512]{3,2,1,0:T(2,128)(2,1)}) custom-call(bf16[2,6,3,2,512]{4,3,2,1,0:T(2,128)(2,1)S(1)} %collective-permute-done.3.refs_0_, bf16[2,6,3,2,512]{4,3,2,1,0:T(2,128)(2,1)S(1)} %collective-permute-done.4.refs_1_, bf16[2,6,3,2,512]{4,3,2,1,0:T(2,128)(2,1)S(1)} %collective-permute-done.5.refs_2_, ...), custom_call_target="tpu_custom_call" | custom-call | tf_op jit(solution)/shard_map/join/pallas_call | solution.py:261
Async XLA Ops:
  1.6 12.9 %collective-permute-start = (bf16[2,6,3,2,512]{4,3,2,1,0:T(2,128)(2,1)S(1)}, bf16[2,6,3,2,512]{4,3,2,1,0:T(2,128)(2,1)S(1)}, u32[]{:S(2)}, u32[]{:S(2)}) collective-permute-start(bf16[2,6,3,2,512]{4,3,2,1,0:T(2,128)(2,1)S(1)} %get-tuple-element.15), channel_id=1, source_target_pairs={{0,255},{1,224},{2,225},{3,226},{4,227},{5,228},{6,229},{7,230},{8... | collective-permute-start | bytes 221192 | tf_op jit(solution)/shard_map/ppermute | solution.py:28
  10.3 5.9 %collective-permute-start.1 = (bf16[2,6,3,2,512]{4,3,2,1,0:T(2,128)(2,1)S(1)}, bf16[2,6,3,2,512]{4,3,2,1,0:T(2,128)(2,1)S(1)}, u32[]{:S(2)}, u32[]{:S(2)}) collective-permute-start(bf16[2,6,3,2,512]{4,3,2,1,0:T(2,128)(2,1)S(1)} %get-tuple-element.16), channel_id=1, source_target_pairs={{0,224},{1,225},{2,226},{3,227},{4,228},{5,229},{6,230},{7,231},{8... | collective-permute-start | bytes 221192 | tf_op jit(solution)/shard_map/ppermute | solution.py:28
  11.4 4.7 %collective-permute-start.2 = (bf16[2,6,3,2,512]{4,3,2,1,0:T(2,128)(2,1)S(1)}, bf16[2,6,3,2,512]{4,3,2,1,0:T(2,128)(2,1)S(1)}, u32[]{:S(2)}, u32[]{:S(2)}) collective-permute-start(bf16[2,6,3,2,512]{4,3,2,1,0:T(2,128)(2,1)S(1)} %get-tuple-element.17), channel_id=1, source_target_pairs={{0,31},{1,0},{2,1},{3,2},{4,3},{5,4},{6,5},{7,6},{8,7},{9,8},{10,9... | collective-permute-start | bytes 221192 | tf_op jit(solution)/shard_map/ppermute | solution.py:28
  20.7 8.8 %collective-permute-start.3 = (bf16[2,6,3,2,512]{4,3,2,1,0:T(2,128)(2,1)S(1)}, bf16[2,6,3,2,512]{4,3,2,1,0:T(2,128)(2,1)S(1)}, u32[]{:S(2)}, u32[]{:S(2)}) collective-permute-start(bf16[2,6,3,2,512]{4,3,2,1,0:T(2,128)(2,1)S(1)} %get-tuple-element.22), channel_id=1, source_target_pairs={{0,33},{1,34},{2,35},{3,36},{4,37},{5,38},{6,39},{7,40},{8,41},{9,... | collective-permute-start | bytes 221192 | tf_op jit(solution)/shard_map/ppermute | solution.py:28
  20.8 8.8 %collective-permute-start.4 = (bf16[2,6,3,2,512]{4,3,2,1,0:T(2,128)(2,1)S(1)}, bf16[2,6,3,2,512]{4,3,2,1,0:T(2,128)(2,1)S(1)}, u32[]{:S(2)}, u32[]{:S(2)}) collective-permute-start(bf16[2,6,3,2,512]{4,3,2,1,0:T(2,128)(2,1)S(1)} %get-tuple-element.23), channel_id=1, source_target_pairs={{0,32},{1,33},{2,34},{3,35},{4,36},{5,37},{6,38},{7,39},{8,40},{9,... | collective-permute-start | bytes 221192 | tf_op jit(solution)/shard_map/ppermute | solution.py:28
  22.0 7.6 %collective-permute-start.5 = (bf16[2,6,3,2,512]{4,3,2,1,0:T(2,128)(2,1)S(1)}, bf16[2,6,3,2,512]{4,3,2,1,0:T(2,128)(2,1)S(1)}, u32[]{:S(2)}, u32[]{:S(2)}) collective-permute-start(bf16[2,6,3,2,512]{4,3,2,1,0:T(2,128)(2,1)S(1)} %get-tuple-element.24), channel_id=1, source_target_pairs={{0,1},{1,2},{2,3},{3,4},{4,5},{5,6},{6,7},{7,8},{8,9},{9,10},{10,1... | collective-permute-start | bytes 221192 | tf_op jit(solution)/shard_map/ppermute | solution.py:28

commit v3 on v2

v3 whole, which is shorter than its diff:
```python
import math

import jax
import jax.numpy as jnp
from jax import lax
from jax.experimental import pallas as pl
from jax.experimental.pallas import tpu as pltpu
from jax.sharding import PartitionSpec as P

HEADS = 8
WLAT = 12
WLON = 6
SLAT = 6
SLON = 3

MIB = 1 << 20
NORM_EPS = 1e-05
MASK_FILL = -1000000000.0

LAT_STEP = 1
LON_STEP = 1


def neighbour(piece, lat_by, lon_by):
    lats, lons = lax.axis_size("lat"), lax.axis_size("lon")
    pairs = [
        (i * lons + j, (i + lat_by) % lats * lons + (j + lon_by) % lons)
        for i in range(lats)
        for j in range(lons)
    ]
    return lax.ppermute(piece, ("lat", "lon"), pairs)


def corners(rows, cols):
    early_rows, late_rows = pl.ds(0, SLAT), pl.ds(SLAT, rows - SLAT)
    early_cols, late_cols = pl.ds(0, SLON), pl.ds(SLON, cols - SLON)
    go_rows, stay_rows = (early_rows, late_rows) if LAT_STEP < 0 else (late_rows, early_rows)
    go_cols, stay_cols = (early_cols, late_cols) if LON_STEP < 0 else (late_cols, early_cols)
    return (
        (go_rows, go_cols), (go_rows, stay_cols), (stay_rows, go_cols), (stay_rows, stay_cols)
    )


def stay(x):
    return pltpu.with_memory_space_constraint(x, pltpu.HBM)


def cut_kernel(latent, cotangent, *rest):
    pieces, sems = rest[:3], rest[3]
    copies = []
    for k, (rows, cols) in enumerate(corners(*latent.shape[:2])[:3]):
        for f, field in enumerate((latent, cotangent)):
            copies.append(
                pltpu.make_async_copy(field.at[rows, cols], pieces[k].at[f], sems.at[k, f])
            )
    for copy in copies:
        copy.start()
    for copy in copies:
        copy.wait()


def fetch_kernel(
    latent, cotangent, gain, qkv, out, own, gain_to, qkv_to, out_to, qkv_turned, out_turned, sems
):
    rows, cols = corners(*latent.shape[:2])[3]
    copies = [
        pltpu.make_async_copy(qkv, qkv_to, sems.at[0]),
        pltpu.make_async_copy(out, out_to, sems.at[1]),
        pltpu.make_async_copy(gain, gain_to, sems.at[2]),
        pltpu.make_async_copy(latent.at[rows, cols], own.at[0], sems.at[3]),
        pltpu.make_async_copy(cotangent.at[rows, cols], own.at[1], sems.at[4]),
    ]
    for copy in copies:
        copy.start()
    copies[1].wait()
    out_turned[...] = out_to[...].T
    copies[0].wait()
    qkv_turned[...] = qkv_to[...].T
    for copy in copies[2:]:
        copy.wait()


def join_kernel(*refs):
    quarters, outs, sems = refs[:4], refs[4:6], refs[6]
    copies = []
    for k, (rows, cols) in enumerate(corners(*outs[0].shape[:2])):
        for f, field in enumerate(outs):
            copies.append(
                pltpu.make_async_copy(quarters[k].at[f], field.at[rows, cols], sems.at[k, f])
            )
    for copy in copies:
        copy.start()
    for copy in copies:
        copy.wait()


def across(a, b):
    return lax.dot_general(a, b, (((1,), (1,)), ((), ())), preferred_element_type=jnp.float32)


def down(a, b):
    return lax.dot_general(a, b, (((0,), (0,)), ((), ())), preferred_element_type=jnp.float32)


def matmul(a, b):
    return jnp.dot(a, b, preferred_element_type=jnp.float32)


def window_kernel(
    ahead_both, ahead_lat, ahead_lon, own, gain_ref, qkv_ref, out_ref, qkv_turned, out_turned,
    both_out, lat_out, lon_out, own_out,
    tokens, cots, scores_ref, low_ref, slopes_ref, proj_ref, mixed_ref, grad_ref,
):
    quarters = (ahead_both, ahead_lat, ahead_lon, own)
    results = (both_out, lat_out, lon_out, own_out)
    _, rows, cols, levels, features = own.shape
    quarter = rows * cols * levels
    window = 4 * quarter
    head_dim = features // HEADS
    wide = 2 * head_dim
    scale = 1.0 / math.sqrt(head_dim)

    for k, ref in enumerate(quarters):
        for f, into in enumerate((tokens, cots)):
            for r in range(rows):
                for c in range(cols):
                    at = k * quarter + (r * cols + c) * levels
                    into[at : at + levels, :] = ref[f, r, c].astype(jnp.float32)

    proj = matmul(tokens[...].astype(jnp.bfloat16), qkv_ref[...]).astype(jnp.bfloat16)
    proj_ref[:, features:] = proj[:, features:]
    proj_ref[:, :features] = proj[:, :features] * jnp.asarray(scale, jnp.bfloat16)

    last = lax.axis_index("lat") == (lax.axis_size("lat") - 1 if LAT_STEP < 0 else 0)
    first_half = lambda d: lax.broadcasted_iota(jnp.int32, (window, window), d) < 2 * quarter
    fill = jnp.where(last, MASK_FILL, 0.0).astype(jnp.float32)
    bias = jnp.where(first_half(0) != first_half(1), fill, 0.0)
    lane = lax.broadcasted_iota(jnp.int32, (1, wide), 1)
    only = [(lane // head_dim == e).astype(jnp.float32).astype(jnp.bfloat16) for e in range(2)]
    second = lax.broadcasted_iota(jnp.int32, (window, wide), 1) >= head_dim

    def part(ref, which, pair):
        at = which * features + wide * pair
        return ref[:, at : at + wide]

    for head in range(HEADS):
        pair, e = divmod(head, 2)
        scores_ref[head] = across(part(proj_ref, 0, pair), part(proj_ref, 1, pair) * only[e])

    for head in range(HEADS):
        scores = scores_ref[head] + bias
        grown = jnp.exp(scores - jnp.max(scores, axis=-1, keepdims=True))
        probs = grown * (1.0 / jnp.sum(grown, axis=-1, keepdims=True))
        scores_ref[head] = probs
        low_ref[head] = probs.astype(jnp.bfloat16)

    for pair in range(HEADS // 2):
        value = part(proj_ref, 2, pair)
        mixed = [matmul(low_ref[2 * pair + e], value) for e in range(2)]
        at = wide * pair
        mixed_ref[:, at : at + wide] = jnp.where(second, mixed[1], mixed[0]).astype(jnp.bfloat16)

    branch = matmul(mixed_ref[...], out_ref[...]).astype(jnp.bfloat16).astype(jnp.float32)
    gain = gain_ref[...]
    centred = branch - jnp.mean(branch, axis=-1, keepdims=True)
    inverse = lax.rsqrt(jnp.mean(centred * centred, axis=-1, keepdims=True) + NORM_EPS)
    normed = centred * inverse
    tokens[...] = tokens[...] + gain * normed
    upstream = gain * cots[...]
    centre_up = jnp.mean(upstream, axis=-1, keepdims=True)
    along = jnp.mean(upstream * normed, axis=-1, keepdims=True)
    grad_branch = (inverse * (upstream - centre_up - normed * along)).astype(jnp.bfloat16)
    mixed_ref[...] = matmul(grad_branch, out_turned[...]).astype(jnp.bfloat16)

    for head in range(HEADS):
        pair, e = divmod(head, 2)
        slopes_ref[head] = across(part(mixed_ref, 0, pair), part(proj_ref, 2, pair) * only[e])

    def put(which, pair, two):
        at = which * features + wide * pair
        grad_ref[:, at : at + wide] = jnp.where(second, two[1], two[0]).astype(jnp.bfloat16)

    for pair in range(HEADS // 2):
        grad_mixed = part(mixed_ref, 0, pair)
        put(2, pair, [down(low_ref[2 * pair + e], grad_mixed) for e in range(2)])

    for head in range(HEADS):
        probs, grad_probs = scores_ref[head], slopes_ref[head]
        along = jnp.sum(grad_probs * probs, axis=-1, keepdims=True)
        low_ref[head] = (probs * (grad_probs - along)).astype(jnp.bfloat16)

    for pair in range(HEADS // 2):
        query, key = part(proj_ref, 0, pair), part(proj_ref, 1, pair)
        put(0, pair, [matmul(low_ref[2 * pair + e], key) * scale for e in range(2)])
        put(1, pair, [down(low_ref[2 * pair + e], query) for e in range(2)])

    grad_tokens = matmul(grad_ref[...], qkv_turned[...]).astype(jnp.bfloat16).astype(jnp.float32)
    cots[...] = cots[...] + grad_tokens

    for k, ref in enumerate(results):
        for f, source in enumerate((tokens, cots)):
            for r in range(rows):
                for c in range(cols):
                    at = k * quarter + (r * cols + c) * levels
                    ref[f, r, c] = source[at : at + levels, :].astype(jnp.bfloat16)


def body(latent, cotangent, norm_gain, qkv_weight, out_weight):
    levels, rows, cols, features = latent.shape
    assert (rows, cols) == (WLAT, WLON) and (2 * SLAT, 2 * SLON) == (WLAT, WLON)
    window = levels * rows * cols
    quarter = (2, SLAT, SLON, levels, features)
    in_vmem = pl.BlockSpec(memory_space=pltpu.VMEM)
    in_hbm = pl.BlockSpec(memory_space=pltpu.HBM)
    piece = pltpu.VMEM(quarter, jnp.bfloat16)
    few = pltpu.CompilerParams(vmem_limit_bytes=MIB)
    latent, cotangent = latent.transpose(1, 2, 0, 3), cotangent.transpose(1, 2, 0, 3)

    to_both, to_lat, to_lon = pl.pallas_call(
        cut_kernel,
        in_specs=[in_hbm] * 2,
        out_specs=[in_vmem] * 3,
        out_shape=[piece] * 3,
        scratch_shapes=[pltpu.SemaphoreType.DMA((3, 2))],
        compiler_params=few,
        name="cut",
    )(stay(latent), stay(cotangent))

    from_both = neighbour(to_both, LAT_STEP, LON_STEP)
    from_lat = neighbour(to_lat, LAT_STEP, 0)
    from_lon = neighbour(to_lon, 0, LON_STEP)

    own, *parameters = pl.pallas_call(
        fetch_kernel,
        in_specs=[in_hbm] * 5,
        out_specs=[in_vmem] * 6,
        out_shape=[
            piece,
            pltpu.VMEM((1, features), jnp.float32),
            pltpu.VMEM(qkv_weight.shape, jnp.bfloat16),
            pltpu.VMEM(out_weight.shape, jnp.bfloat16),
            pltpu.VMEM(qkv_weight.shape[::-1], jnp.bfloat16),
            pltpu.VMEM(out_weight.shape[::-1], jnp.bfloat16),
        ],
        scratch_shapes=[pltpu.SemaphoreType.DMA((5,))],
        compiler_params=few,
        cost_estimate=pl.CostEstimate(flops=0, bytes_accessed=4 * MIB, transcendentals=0),
        name="fetch",
    )(*map(stay, (latent, cotangent, norm_gain.reshape(1, features), qkv_weight, out_weight)))

    to_both, to_lat, to_lon, own = pl.pallas_call(
        window_kernel,
        in_specs=[in_vmem] * 9,
        out_specs=[in_vmem] * 4,
        out_shape=[piece] * 4,
        scratch_shapes=[
            pltpu.VMEM((window, features), jnp.float32),
            pltpu.VMEM((window, features), jnp.float32),
            pltpu.VMEM((HEADS, window, window), jnp.float32),
            pltpu.VMEM((HEADS, window, window), jnp.bfloat16),
            pltpu.VMEM((HEADS, window, window), jnp.float32),
            pltpu.VMEM((window, 3 * features), jnp.bfloat16),
            pltpu.VMEM((window, features), jnp.bfloat16),
            pltpu.VMEM((window, 3 * features), jnp.bfloat16),
        ],
        compiler_params=pltpu.CompilerParams(vmem_limit_bytes=12 * MIB),
        name="window",
    )(from_both, from_lat, from_lon, own, *parameters)

    from_both = neighbour(to_both, -LAT_STEP, -LON_STEP)
    from_lat = neighbour(to_lat, -LAT_STEP, 0)
    from_lon = neighbour(to_lon, 0, -LON_STEP)

    updated, latent_grad = pl.pallas_call(
        join_kernel,
        in_specs=[in_vmem] * 4,
        out_specs=[in_hbm] * 2,
        out_shape=[jax.ShapeDtypeStruct((rows, cols, levels, features), jnp.bfloat16)] * 2,
        scratch_shapes=[pltpu.SemaphoreType.DMA((4, 2))],
        compiler_params=few,
        name="join",
    )(from_both, from_lat, from_lon, own)
    return (updated.transpose(2, 0, 1, 3), latent_grad.transpose(2, 0, 1, 3))


def solution(mesh):
    placed = (P(None, "lat", "lon", None), P(None, "lat", "lon", None), P(), P(), P())
    return jax.shard_map(
        body,
        mesh=mesh,
        in_specs=placed,
        out_specs=(P(None, "lat", "lon", None), P(None, "lat", "lon", None)),
        check_vma=False,
    )
```

time: 30.6 us -> 28.3 us (0.925)
  waiting for transfers between devices: 9.28 us -> 5.41 us
  starting transfers between devices: 12.6 us -> 15 us
  Pallas kernels: 7.83 us -> 7.12 us
    ppermute x6, waiting for transfers between devices: 9.28 us -> 5.41 us  [neighbour(): return lax.ppermute(piece, ('lat', 'lon'), pairs)]
    ppermute x6, starting transfers between devices: 12.6 us -> 15 us  [neighbour(): return lax.ppermute(piece, ('lat', 'lon'), pairs)]
    pallas_call x1, Pallas kernels: 4.58 us -> 3.22 us  [body(): pl.pallas_call(window_kernel, in_specs=[in_vmem] * 9, out_specs=[in_vmem]...]
    pallas_call x1, Pallas kernels: 1.56 us -> 2.22 us  [body(): pl.pallas_call(fetch_kernel, in_specs=[in_hbm] * 5, out_specs=[in_vmem] *...]
  transfers between devices with their start and end apart: 6 -> 6, of which waited for: 3 -> 3; matrix products, arithmetic and copies ran while one was open for 0% -> 0% of each run, Pallas kernels for 5% -> 8%
where the time goes in v3:
time: 28.3 us; the launch traced here: 28.1 us
  starting transfers between devices  15 us (53%)
  Pallas kernels  7.12 us (25%)
  waiting for transfers between devices  5.41 us (19%)
  between operations  0.66 us (2%)
    ppermute x6, starting transfers between devices, neighbour(): return lax.ppermute(piece, ('lat', 'lon'), pairs)  15 us
    ppermute x6, waiting for transfers between devices, neighbour(): return lax.ppermute(piece, ('lat', 'lon'), pairs)  5.41 us
    pallas_call x1, Pallas kernels, body(): pl.pallas_call(window_kernel, in_specs=[in_vmem] * 9, out_specs=[in_vmem]...  3.22 us
    pallas_call x1, Pallas kernels, body(): pl.pallas_call(fetch_kernel, in_specs=[in_hbm] * 5, out_specs=[in_vmem] *...  2.22 us
    pallas_call x1, Pallas kernels, body(): pl.pallas_call(cut_kernel, in_specs=[in_hbm] * 2, out_specs=[in_vmem] * 3...  0.91 us
    pallas_call x1, Pallas kernels, body(): pl.pallas_call(join_kernel, in_specs=[in_vmem] * 4, out_specs=[in_hbm] *...  0.77 us
  transfers between devices with their start and end apart: 6, of which 3 were waited for; matrix products, arithmetic and copies ran while one was open for 0% of the time, Pallas kernels for 8%

profile of v3, /device:TPU:2, one launch (start us, length us, event | category | flops | bytes accessed | tf_op | source)
XLA Modules:
  0.0 28.1 jit_solution(13316014757027438777)
XLA Ops:
  0.6 0.9 %cut.1 = (bf16[2,6,3,2,512]{4,3,2,1,0:T(2,128)(2,1)S(1)}, bf16[2,6,3,2,512]{4,3,2,1,0:T(2,128)(2,1)S(1)}, bf16[2,6,3,2,512]{4,3,2,1,0:T(2,128)(2,1)S(1)}) custom-call(bf16[12,6,2,512]{3,2,1,0:T(2,128)(2,1)} %bitcast.5, bf16[12,6,2,512]{3,2,1,0:T(2,128)(2,1)} %bitcast.7), custom_call_target="tpu_custom_call" | custom-call | tf_op jit(solution)/shard_map/cut/pallas_call | solution.py:219
  1.6 1.6 %collective-permute-start = (bf16[2,6,3,2,512]{4,3,2,1,0:T(2,128)(2,1)S(1)}, bf16[2,6,3,2,512]{4,3,2,1,0:T(2,128)(2,1)S(1)}, u32[]{:S(2)}, u32[]{:S(2)}) collective-permute-start(bf16[2,6,3,2,512]{4,3,2,1,0:T(2,128)(2,1)S(1)} %get-tuple-element.17), channel_id=1, source_target_pairs={{0,33},{1,34},{2,35},{3,36},{4,37},{5,38},{6,39},{7,40},{8,41},{9,... | collective-permute-start | bytes 221192 | tf_op jit(solution)/shard_map/ppermute | solution.py:31
  3.2 2.4 %collective-permute-start.1 = (bf16[2,6,3,2,512]{4,3,2,1,0:T(2,128)(2,1)S(1)}, bf16[2,6,3,2,512]{4,3,2,1,0:T(2,128)(2,1)S(1)}, u32[]{:S(2)}, u32[]{:S(2)}) collective-permute-start(bf16[2,6,3,2,512]{4,3,2,1,0:T(2,128)(2,1)S(1)} %get-tuple-element.18), channel_id=1, source_target_pairs={{0,32},{1,33},{2,34},{3,35},{4,36},{5,37},{6,38},{7,39},{8,40},{9,... | collective-permute-start | bytes 221192 | tf_op jit(solution)/shard_map/ppermute | solution.py:31
  5.6 1.7 %collective-permute-start.2 = (bf16[2,6,3,2,512]{4,3,2,1,0:T(2,128)(2,1)S(1)}, bf16[2,6,3,2,512]{4,3,2,1,0:T(2,128)(2,1)S(1)}, u32[]{:S(2)}, u32[]{:S(2)}) collective-permute-start(bf16[2,6,3,2,512]{4,3,2,1,0:T(2,128)(2,1)S(1)} %get-tuple-element.19), channel_id=1, source_target_pairs={{0,1},{1,2},{2,3},{3,4},{4,5},{5,6},{6,7},{7,8},{8,9},{9,10},{10,1... | collective-permute-start | bytes 221192 | tf_op jit(solution)/shard_map/ppermute | solution.py:31
  7.4 2.2 %fetch.1 = (bf16[2,6,3,2,512]{4,3,2,1,0:T(2,128)(2,1)S(1)}, f32[1,512]{1,0:T(1,128)S(1)}, bf16[512,1536]{1,0:T(8,128)(2,1)S(1)}, bf16[512,512]{1,0:T(8,128)(2,1)...) custom-call(bf16[12,6,2,512]{3,2,1,0:T(2,128)(2,1)} %bitcast.6, bf16[12,6,2,512]{3,2,1,0:T(2,128)(2,1)} %bitcast.8, ...), custom_call_target="tpu_custom_call" | custom-call | bytes 4194304 | tf_op jit(solution)/shard_map/fetch/pallas_call | solution.py:233
  9.6 3.4 %collective-permute-done.ahead_both = bf16[2,6,3,2,512]{4,3,2,1,0:T(2,128)(2,1)S(1)} collective-permute-done((bf16[2,6,3,2,512]{4,3,2,1,0:T(2,128)(2,1)S(1)}, bf16[2,6,3,2,512]{4,3,2,1,0:T(2,128)(2,1)S(1)}, u32[]{:S(2)}, u32[]{:S(2)}) %collective-permute-start) | collective-permute-done | bytes 73760 | tf_op jit(solution)/shard_map/ppermute | solution.py:31
  13.0 0.0 collective-permute-done.1.ahead_lat
  13.0 0.0 collective-permute-done.2.ahead_lon
  13.0 3.2 %window.1 = (bf16[2,6,3,2,512]{4,3,2,1,0:T(2,128)(2,1)S(1)}, bf16[2,6,3,2,512]{4,3,2,1,0:T(2,128)(2,1)S(1)}, bf16[2,6,3,2,512]{4,3,2,1,0:T(2,128)(2,1)S(1)}, bf16[2,6,3,2,512]{4,3,2,1,0:T(2,128)(2,1)S(1)}) custom-call(bf16[2,6,3,2,512]{4,3,2,1,0:T(2,128)(2,1)S(1)} %collective-permute-done.ahead_both, ...), custom_call_target="tpu_custom_call" | custom-call | tf_op jit(solution)/shard_map/window/pallas_call | solution.py:251
  16.2 3.8 %collective-permute-start.3 = (bf16[2,6,3,2,512]{4,3,2,1,0:T(2,128)(2,1)S(1)}, bf16[2,6,3,2,512]{4,3,2,1,0:T(2,128)(2,1)S(1)}, u32[]{:S(2)}, u32[]{:S(2)}) collective-permute-start(bf16[2,6,3,2,512]{4,3,2,1,0:T(2,128)(2,1)S(1)} %get-tuple-element.26), channel_id=1, source_target_pairs={{0,255},{1,224},{2,225},{3,226},{4,227},{5,228},{6,229},{7,230},{8... | collective-permute-start | bytes 221192 | tf_op jit(solution)/shard_map/ppermute | solution.py:31
  20.1 2.0 %collective-permute-start.4 = (bf16[2,6,3,2,512]{4,3,2,1,0:T(2,128)(2,1)S(1)}, bf16[2,6,3,2,512]{4,3,2,1,0:T(2,128)(2,1)S(1)}, u32[]{:S(2)}, u32[]{:S(2)}) collective-permute-start(bf16[2,6,3,2,512]{4,3,2,1,0:T(2,128)(2,1)S(1)} %get-tuple-element.27), channel_id=1, source_target_pairs={{0,224},{1,225},{2,226},{3,227},{4,228},{5,229},{6,230},{7,231},{8... | collective-permute-start | bytes 221192 | tf_op jit(solution)/shard_map/ppermute | solution.py:31
  22.1 3.3 %collective-permute-start.5 = (bf16[2,6,3,2,512]{4,3,2,1,0:T(2,128)(2,1)S(1)}, bf16[2,6,3,2,512]{4,3,2,1,0:T(2,128)(2,1)S(1)}, u32[]{:S(2)}, u32[]{:S(2)}) collective-permute-start(bf16[2,6,3,2,512]{4,3,2,1,0:T(2,128)(2,1)S(1)} %get-tuple-element.28), channel_id=1, source_target_pairs={{0,31},{1,0},{2,1},{3,2},{4,3},{5,4},{6,5},{7,6},{8,7},{9,8},{10,9... | collective-permute-start | bytes 221192 | tf_op jit(solution)/shard_map/ppermute | solution.py:31
  25.4 0.0 collective-permute-done.3.refs_0_
  25.4 0.5 %collective-permute-done.4.refs_1_ = bf16[2,6,3,2,512]{4,3,2,1,0:T(2,128)(2,1)S(1)} collective-permute-done((bf16[2,6,3,2,512]{4,3,2,1,0:T(2,128)(2,1)S(1)}, bf16[2,6,3,2,512]{4,3,2,1,0:T(2,128)(2,1)S(1)}, u32[]{:S(2)}, u32[]{:S(2)}) %collective-permute-start.4) | collective-permute-done | bytes 73760 | tf_op jit(solution)/shard_map/ppermute | solution.py:31
  25.9 1.4 %collective-permute-done.5.refs_2_ = bf16[2,6,3,2,512]{4,3,2,1,0:T(2,128)(2,1)S(1)} collective-permute-done((bf16[2,6,3,2,512]{4,3,2,1,0:T(2,128)(2,1)S(1)}, bf16[2,6,3,2,512]{4,3,2,1,0:T(2,128)(2,1)S(1)}, u32[]{:S(2)}, u32[]{:S(2)}) %collective-permute-start.5) | collective-permute-done | bytes 73760 | tf_op jit(solution)/shard_map/ppermute | solution.py:31
  27.4 0.8 %join.1 = (bf16[12,6,2,512]{3,2,1,0:T(2,128)(2,1)}, bf16[12,6,2,512]{3,2,1,0:T(2,128)(2,1)}) custom-call(bf16[2,6,3,2,512]{4,3,2,1,0:T(2,128)(2,1)S(1)} %collective-permute-done.3.refs_0_, bf16[2,6,3,2,512]{4,3,2,1,0:T(2,128)(2,1)S(1)} %collective-permute-done.4.refs_1_, bf16[2,6,3,2,512]{4,3,2,1,0:T(2,128)(2,1)S(1)} %collective-permute-done.5.refs_2_, ...), custom_call_target="tpu_custom_call" | custom-call | tf_op jit(solution)/shard_map/join/pallas_call | solution.py:274
Async XLA Ops:
  1.6 11.5 %collective-permute-start = (bf16[2,6,3,2,512]{4,3,2,1,0:T(2,128)(2,1)S(1)}, bf16[2,6,3,2,512]{4,3,2,1,0:T(2,128)(2,1)S(1)}, u32[]{:S(2)}, u32[]{:S(2)}) collective-permute-start(bf16[2,6,3,2,512]{4,3,2,1,0:T(2,128)(2,1)S(1)} %get-tuple-element.17), channel_id=1, source_target_pairs={{0,33},{1,34},{2,35},{3,36},{4,37},{5,38},{6,39},{7,40},{8,41},{9,... | collective-permute-start | bytes 221192 | tf_op jit(solution)/shard_map/ppermute | solution.py:31
  3.2 9.8 %collective-permute-start.1 = (bf16[2,6,3,2,512]{4,3,2,1,0:T(2,128)(2,1)S(1)}, bf16[2,6,3,2,512]{4,3,2,1,0:T(2,128)(2,1)S(1)}, u32[]{:S(2)}, u32[]{:S(2)}) collective-permute-start(bf16[2,6,3,2,512]{4,3,2,1,0:T(2,128)(2,1)S(1)} %get-tuple-element.18), channel_id=1, source_target_pairs={{0,32},{1,33},{2,34},{3,35},{4,36},{5,37},{6,38},{7,39},{8,40},{9,... | collective-permute-start | bytes 221192 | tf_op jit(solution)/shard_map/ppermute | solution.py:31
  5.6 7.4 %collective-permute-start.2 = (bf16[2,6,3,2,512]{4,3,2,1,0:T(2,128)(2,1)S(1)}, bf16[2,6,3,2,512]{4,3,2,1,0:T(2,128)(2,1)S(1)}, u32[]{:S(2)}, u32[]{:S(2)}) collective-permute-start(bf16[2,6,3,2,512]{4,3,2,1,0:T(2,128)(2,1)S(1)} %get-tuple-element.19), channel_id=1, source_target_pairs={{0,1},{1,2},{2,3},{3,4},{4,5},{5,6},{6,7},{7,8},{8,9},{9,10},{10,1... | collective-permute-start | bytes 221192 | tf_op jit(solution)/shard_map/ppermute | solution.py:31
  16.2 9.2 %collective-permute-start.3 = (bf16[2,6,3,2,512]{4,3,2,1,0:T(2,128)(2,1)S(1)}, bf16[2,6,3,2,512]{4,3,2,1,0:T(2,128)(2,1)S(1)}, u32[]{:S(2)}, u32[]{:S(2)}) collective-permute-start(bf16[2,6,3,2,512]{4,3,2,1,0:T(2,128)(2,1)S(1)} %get-tuple-element.26), channel_id=1, source_target_pairs={{0,255},{1,224},{2,225},{3,226},{4,227},{5,228},{6,229},{7,230},{8... | collective-permute-start | bytes 221192 | tf_op jit(solution)/shard_map/ppermute | solution.py:31
  20.1 5.9 %collective-permute-start.4 = (bf16[2,6,3,2,512]{4,3,2,1,0:T(2,128)(2,1)S(1)}, bf16[2,6,3,2,512]{4,3,2,1,0:T(2,128)(2,1)S(1)}, u32[]{:S(2)}, u32[]{:S(2)}) collective-permute-start(bf16[2,6,3,2,512]{4,3,2,1,0:T(2,128)(2,1)S(1)} %get-tuple-element.27), channel_id=1, source_target_pairs={{0,224},{1,225},{2,226},{3,227},{4,228},{5,229},{6,230},{7,231},{8... | collective-permute-start | bytes 221192 | tf_op jit(solution)/shard_map/ppermute | solution.py:31
  22.1 5.3 %collective-permute-start.5 = (bf16[2,6,3,2,512]{4,3,2,1,0:T(2,128)(2,1)S(1)}, bf16[2,6,3,2,512]{4,3,2,1,0:T(2,128)(2,1)S(1)}, u32[]{:S(2)}, u32[]{:S(2)}) collective-permute-start(bf16[2,6,3,2,512]{4,3,2,1,0:T(2,128)(2,1)S(1)} %get-tuple-element.28), channel_id=1, source_target_pairs={{0,31},{1,0},{2,1},{3,2},{4,3},{5,4},{6,5},{7,6},{8,7},{9,8},{10,9... | collective-permute-start | bytes 221192 | tf_op jit(solution)/shard_map/ppermute | solution.py:31

commit v4 on v3

--- a/solution.py
+++ b/solution.py
@@ -12,6 +12,7 @@
 WLON = 6
 SLAT = 6
 SLON = 3
+GROUP = 4
 
 MIB = 1 << 20
 NORM_EPS = 1e-05
@@ -109,7 +110,7 @@
 def window_kernel(
     ahead_both, ahead_lat, ahead_lon, own, gain_ref, qkv_ref, out_ref, qkv_turned, out_turned,
     both_out, lat_out, lon_out, own_out,
-    tokens, cots, scores_ref, low_ref, slopes_ref, proj_ref, mixed_ref, grad_ref,
+    tokens, cots, scores_ref, low_ref, slopes_ref, wide_query, proj_ref, mixed_ref, grad_ref,
 ):
     quarters = (ahead_both, ahead_lat, ahead_lon, own)
     results = (both_out, lat_out, lon_out, own_out)
@@ -117,7 +118,6 @@
     quarter = rows * cols * levels
     window = 4 * quarter
     head_dim = features // HEADS
-    wide = 2 * head_dim
     scale = 1.0 / math.sqrt(head_dim)
 
     for k, ref in enumerate(quarters):
@@ -132,67 +132,75 @@
     proj_ref[:, :features] = proj[:, :features] * jnp.asarray(scale, jnp.bfloat16)
 
     last = lax.axis_index("lat") == (lax.axis_size("lat") - 1 if LAT_STEP < 0 else 0)
-    first_half = lambda d: lax.broadcasted_iota(jnp.int32, (window, window), d) < 2 * quarter
+    wide = GROUP * head_dim
+    packed = GROUP * window
+    key_row = lax.broadcasted_iota(jnp.int32, (window, packed), 0)
+    query_row = lax.rem(lax.broadcasted_iota(jnp.int32, (window, packed), 1), window)
     fill = jnp.where(last, MASK_FILL, 0.0).astype(jnp.float32)
-    bias = jnp.where(first_half(0) != first_half(1), fill, 0.0)
+    bias = jnp.where((key_row < 2 * quarter) != (query_row < 2 * quarter), fill, 0.0)
     lane = lax.broadcasted_iota(jnp.int32, (1, wide), 1)
-    only = [(lane // head_dim == e).astype(jnp.float32).astype(jnp.bfloat16) for e in range(2)]
-    second = lax.broadcasted_iota(jnp.int32, (window, wide), 1) >= head_dim
-
-    def part(ref, which, pair):
-        at = which * features + wide * pair
+    only = [(lane // head_dim == e).astype(jnp.float32).astype(jnp.bfloat16) for e in range(GROUP)]
+    mine = [lax.broadcasted_iota(jnp.int32, (window, wide), 1) < head_dim * e for e in range(1, GROUP)]
+
+    def part(ref, which, group):
+        at = which * features + wide * group
         return ref[:, at : at + wide]
 
-    for head in range(HEADS):
-        pair, e = divmod(head, 2)
-        scores_ref[head] = across(part(proj_ref, 0, pair), part(proj_ref, 1, pair) * only[e])
-
-    for head in range(HEADS):
-        scores = scores_ref[head] + bias
-        grown = jnp.exp(scores - jnp.max(scores, axis=-1, keepdims=True))
-        probs = grown * (1.0 / jnp.sum(grown, axis=-1, keepdims=True))
-        scores_ref[head] = probs
-        low_ref[head] = probs.astype(jnp.bfloat16)
-
-    for pair in range(HEADS // 2):
-        value = part(proj_ref, 2, pair)
-        mixed = [matmul(low_ref[2 * pair + e], value) for e in range(2)]
-        at = wide * pair
-        mixed_ref[:, at : at + wide] = jnp.where(second, mixed[1], mixed[0]).astype(jnp.bfloat16)
+    def fanned(x):
+        return jnp.concatenate([x * only[e] for e in range(GROUP)], axis=0)
+
+    def gathered(x):
+        out = x[(GROUP - 1) * window :]
+        for e in range(GROUP - 2, -1, -1):
+            out = jnp.where(mine[e], x[e * window : (e + 1) * window], out)
+        return out
+
+    for group in range(HEADS // GROUP):
+        wide_query[group] = fanned(part(proj_ref, 0, group))
+        scores_ref[group] = across(part(proj_ref, 1, group), wide_query[group])
+
+    for group in range(HEADS // GROUP):
+        scores = scores_ref[group] + bias
+        grown = jnp.exp(scores - jnp.max(scores, axis=0, keepdims=True))
+        probs = grown * (1.0 / jnp.sum(grown, axis=0, keepdims=True))
+        scores_ref[group] = probs
+        low_ref[group] = probs.astype(jnp.bfloat16)
+
+    for group in range(HEADS // GROUP):
+        at = wide * group
+        mixed = gathered(down(low_ref[group], part(proj_ref, 2, group)))
+        mixed_ref[:, at : at + wide] = mixed.astype(jnp.bfloat16)
 
     branch = matmul(mixed_ref[...], out_ref[...]).astype(jnp.bfloat16).astype(jnp.float32)
     gain = gain_ref[...]
+    upstream = gain * cots[...]
+    centre_up = jnp.mean(upstream, axis=-1, keepdims=True)
     centred = branch - jnp.mean(branch, axis=-1, keepdims=True)
-    inverse = lax.rsqrt(jnp.mean(centred * centred, axis=-1, keepdims=True) + NORM_EPS)
+    spread = jnp.mean(centred * centred, axis=-1, keepdims=True)
+    along = jnp.mean(upstream * centred, axis=-1, keepdims=True)
+    inverse = lax.rsqrt(spread + NORM_EPS)
     normed = centred * inverse
     tokens[...] = tokens[...] + gain * normed
-    upstream = gain * cots[...]
-    centre_up = jnp.mean(upstream, axis=-1, keepdims=True)
-    along = jnp.mean(upstream * normed, axis=-1, keepdims=True)
-    grad_branch = (inverse * (upstream - centre_up - normed * along)).astype(jnp.bfloat16)
+    grad_branch = (inverse * (upstream - centre_up - normed * (along * inverse))).astype(jnp.bfloat16)
     mixed_ref[...] = matmul(grad_branch, out_turned[...]).astype(jnp.bfloat16)
 
-    for head in range(HEADS):
-        pair, e = divmod(head, 2)
-        slopes_ref[head] = across(part(mixed_ref, 0, pair), part(proj_ref, 2, pair) * only[e])
-
-    def put(which, pair, two):
-        at = which * features + wide * pair
-        grad_ref[:, at : at + wide] = jnp.where(second, two[1], two[0]).astype(jnp.bfloat16)
-
-    for pair in range(HEADS // 2):
-        grad_mixed = part(mixed_ref, 0, pair)
-        put(2, pair, [down(low_ref[2 * pair + e], grad_mixed) for e in range(2)])
-
-    for head in range(HEADS):
-        probs, grad_probs = scores_ref[head], slopes_ref[head]
-        along = jnp.sum(grad_probs * probs, axis=-1, keepdims=True)
-        low_ref[head] = (probs * (grad_probs - along)).astype(jnp.bfloat16)
-
-    for pair in range(HEADS // 2):
-        query, key = part(proj_ref, 0, pair), part(proj_ref, 1, pair)
-        put(0, pair, [matmul(low_ref[2 * pair + e], key) * scale for e in range(2)])
-        put(1, pair, [down(low_ref[2 * pair + e], query) for e in range(2)])
+    def put(which, group, x):
+        at = which * features + wide * group
+        grad_ref[:, at : at + wide] = x.astype(jnp.bfloat16)
+
+    for group in range(HEADS // GROUP):
+        grad_mixed = fanned(part(mixed_ref, 0, group))
+        slopes_ref[group] = across(part(proj_ref, 2, group), grad_mixed)
+        put(2, group, matmul(low_ref[group], grad_mixed))
+
+    for group in range(HEADS // GROUP):
+        probs, grad_probs = scores_ref[group], slopes_ref[group]
+        along = jnp.sum(grad_probs * probs, axis=0, keepdims=True)
+        low_ref[group] = (probs * (grad_probs - along)).astype(jnp.bfloat16)
+
+    for group in range(HEADS // GROUP):
+        put(0, group, gathered(down(low_ref[group], part(proj_ref, 1, group))) * scale)
+        put(1, group, matmul(low_ref[group], wide_query[group]))
 
     grad_tokens = matmul(grad_ref[...], qkv_turned[...]).astype(jnp.bfloat16).astype(jnp.float32)
     cots[...] = cots[...] + grad_tokens
@@ -210,6 +218,7 @@
     assert (rows, cols) == (WLAT, WLON) and (2 * SLAT, 2 * SLON) == (WLAT, WLON)
     window = levels * rows * cols
     quarter = (2, SLAT, SLON, levels, features)
+    packed = (HEADS // GROUP, window, GROUP * window)
     in_vmem = pl.BlockSpec(memory_space=pltpu.VMEM)
     in_hbm = pl.BlockSpec(memory_space=pltpu.HBM)
     piece = pltpu.VMEM(quarter, jnp.bfloat16)
@@ -256,9 +265,10 @@
         scratch_shapes=[
             pltpu.VMEM((window, features), jnp.float32),
             pltpu.VMEM((window, features), jnp.float32),
-            pltpu.VMEM((HEADS, window, window), jnp.float32),
-            pltpu.VMEM((HEADS, window, window), jnp.bfloat16),
-            pltpu.VMEM((HEADS, window, window), jnp.float32),
+            pltpu.VMEM(packed, jnp.float32),
+            pltpu.VMEM(packed, jnp.bfloat16),
+            pltpu.VMEM(packed, jnp.float32),
+            pltpu.VMEM((HEADS // GROUP, GROUP * window, features * GROUP // HEADS), jnp.bfloat16),
             pltpu.VMEM((window, 3 * features), jnp.bfloat16),
             pltpu.VMEM((window, features), jnp.bfloat16),
             pltpu.VMEM((window, 3 * features), jnp.bfloat16),

time: 28.3 us -> 27.9 us (0.986)
  Pallas kernels: 7.12 us -> 6.71 us
    pallas_call x1, Pallas kernels: 3.22 us -> 2.81 us  [body(): pl.pallas_call(window_kernel, in_specs=[in_vmem] * 9, out_specs=[in_vmem]...]
where the time goes in v4:
time: 27.9 us; the launch traced here: 27.8 us
  starting transfers between devices  15 us (54%)
  Pallas kernels  6.71 us (24%)
  waiting for transfers between devices  5.41 us (19%)
  between operations  0.66 us (2%)
    ppermute x6, starting transfers between devices, neighbour(): return lax.ppermute(piece, ('lat', 'lon'), pairs)  15 us
    ppermute x6, waiting for transfers between devices, neighbour(): return lax.ppermute(piece, ('lat', 'lon'), pairs)  5.41 us
    pallas_call x1, Pallas kernels, body(): pl.pallas_call(window_kernel, in_specs=[in_vmem] * 9, out_specs=[in_vmem]...  2.81 us
    pallas_call x1, Pallas kernels, body(): pl.pallas_call(fetch_kernel, in_specs=[in_hbm] * 5, out_specs=[in_vmem] *...  2.22 us
    pallas_call x1, Pallas kernels, body(): pl.pallas_call(cut_kernel, in_specs=[in_hbm] * 2, out_specs=[in_vmem] * 3...  0.91 us
    pallas_call x1, Pallas kernels, body(): pl.pallas_call(join_kernel, in_specs=[in_vmem] * 4, out_specs=[in_hbm] *...  0.77 us
  transfers between devices with their start and end apart: 6, of which 3 were waited for; matrix products, arithmetic and copies ran while one was open for 0% of the time, Pallas kernels for 8%

profile of v4, /device:TPU:2, one launch (start us, length us, event | category | flops | bytes accessed | tf_op | source)
XLA Modules:
  0.0 27.8 jit_solution(10052295071690019033)
XLA Ops:
  0.6 0.9 %cut.1 = (bf16[2,6,3,2,512]{4,3,2,1,0:T(2,128)(2,1)S(1)}, bf16[2,6,3,2,512]{4,3,2,1,0:T(2,128)(2,1)S(1)}, bf16[2,6,3,2,512]{4,3,2,1,0:T(2,128)(2,1)S(1)}) custom-call(bf16[12,6,2,512]{3,2,1,0:T(2,128)(2,1)} %bitcast.5, bf16[12,6,2,512]{3,2,1,0:T(2,128)(2,1)} %bitcast.7), custom_call_target="tpu_custom_call" | custom-call | tf_op jit(solution)/shard_map/cut/pallas_call | solution.py:228
  1.6 1.6 %collective-permute-start = (bf16[2,6,3,2,512]{4,3,2,1,0:T(2,128)(2,1)S(1)}, bf16[2,6,3,2,512]{4,3,2,1,0:T(2,128)(2,1)S(1)}, u32[]{:S(2)}, u32[]{:S(2)}) collective-permute-start(bf16[2,6,3,2,512]{4,3,2,1,0:T(2,128)(2,1)S(1)} %get-tuple-element.17), channel_id=1, source_target_pairs={{0,33},{1,34},{2,35},{3,36},{4,37},{5,38},{6,39},{7,40},{8,41},{9,... | collective-permute-start | bytes 221192 | tf_op jit(solution)/shard_map/ppermute | solution.py:32
  3.2 2.4 %collective-permute-start.1 = (bf16[2,6,3,2,512]{4,3,2,1,0:T(2,128)(2,1)S(1)}, bf16[2,6,3,2,512]{4,3,2,1,0:T(2,128)(2,1)S(1)}, u32[]{:S(2)}, u32[]{:S(2)}) collective-permute-start(bf16[2,6,3,2,512]{4,3,2,1,0:T(2,128)(2,1)S(1)} %get-tuple-element.18), channel_id=1, source_target_pairs={{0,32},{1,33},{2,34},{3,35},{4,36},{5,37},{6,38},{7,39},{8,40},{9,... | collective-permute-start | bytes 221192 | tf_op jit(solution)/shard_map/ppermute | solution.py:32
  5.6 1.7 %collective-permute-start.2 = (bf16[2,6,3,2,512]{4,3,2,1,0:T(2,128)(2,1)S(1)}, bf16[2,6,3,2,512]{4,3,2,1,0:T(2,128)(2,1)S(1)}, u32[]{:S(2)}, u32[]{:S(2)}) collective-permute-start(bf16[2,6,3,2,512]{4,3,2,1,0:T(2,128)(2,1)S(1)} %get-tuple-element.19), channel_id=1, source_target_pairs={{0,1},{1,2},{2,3},{3,4},{4,5},{5,6},{6,7},{7,8},{8,9},{9,10},{10,1... | collective-permute-start | bytes 221192 | tf_op jit(solution)/shard_map/ppermute | solution.py:32
  7.4 2.2 %fetch.1 = (bf16[2,6,3,2,512]{4,3,2,1,0:T(2,128)(2,1)S(1)}, f32[1,512]{1,0:T(1,128)S(1)}, bf16[512,1536]{1,0:T(8,128)(2,1)S(1)}, bf16[512,512]{1,0:T(8,128)(2,1)...) custom-call(bf16[12,6,2,512]{3,2,1,0:T(2,128)(2,1)} %bitcast.6, bf16[12,6,2,512]{3,2,1,0:T(2,128)(2,1)} %bitcast.8, ...), custom_call_target="tpu_custom_call" | custom-call | bytes 4194304 | tf_op jit(solution)/shard_map/fetch/pallas_call | solution.py:242
  9.6 3.4 %collective-permute-done.ahead_both = bf16[2,6,3,2,512]{4,3,2,1,0:T(2,128)(2,1)S(1)} collective-permute-done((bf16[2,6,3,2,512]{4,3,2,1,0:T(2,128)(2,1)S(1)}, bf16[2,6,3,2,512]{4,3,2,1,0:T(2,128)(2,1)S(1)}, u32[]{:S(2)}, u32[]{:S(2)}) %collective-permute-start) | collective-permute-done | bytes 73760 | tf_op jit(solution)/shard_map/ppermute | solution.py:32
  13.0 0.0 collective-permute-done.1.ahead_lat
  13.0 0.0 collective-permute-done.2.ahead_lon
  13.0 2.8 %window.1 = (bf16[2,6,3,2,512]{4,3,2,1,0:T(2,128)(2,1)S(1)}, bf16[2,6,3,2,512]{4,3,2,1,0:T(2,128)(2,1)S(1)}, bf16[2,6,3,2,512]{4,3,2,1,0:T(2,128)(2,1)S(1)}, bf16[2,6,3,2,512]{4,3,2,1,0:T(2,128)(2,1)S(1)}) custom-call(bf16[2,6,3,2,512]{4,3,2,1,0:T(2,128)(2,1)S(1)} %collective-permute-done.ahead_both, ...), custom_call_target="tpu_custom_call" | custom-call | tf_op jit(solution)/shard_map/window/pallas_call | solution.py:260
  15.8 3.8 %collective-permute-start.3 = (bf16[2,6,3,2,512]{4,3,2,1,0:T(2,128)(2,1)S(1)}, bf16[2,6,3,2,512]{4,3,2,1,0:T(2,128)(2,1)S(1)}, u32[]{:S(2)}, u32[]{:S(2)}) collective-permute-start(bf16[2,6,3,2,512]{4,3,2,1,0:T(2,128)(2,1)S(1)} %get-tuple-element.26), channel_id=1, source_target_pairs={{0,255},{1,224},{2,225},{3,226},{4,227},{5,228},{6,229},{7,230},{8... | collective-permute-start | bytes 221192 | tf_op jit(solution)/shard_map/ppermute | solution.py:32
  19.7 2.0 %collective-permute-start.4 = (bf16[2,6,3,2,512]{4,3,2,1,0:T(2,128)(2,1)S(1)}, bf16[2,6,3,2,512]{4,3,2,1,0:T(2,128)(2,1)S(1)}, u32[]{:S(2)}, u32[]{:S(2)}) collective-permute-start(bf16[2,6,3,2,512]{4,3,2,1,0:T(2,128)(2,1)S(1)} %get-tuple-element.27), channel_id=1, source_target_pairs={{0,224},{1,225},{2,226},{3,227},{4,228},{5,229},{6,230},{7,231},{8... | collective-permute-start | bytes 221192 | tf_op jit(solution)/shard_map/ppermute | solution.py:32
  21.7 3.3 %collective-permute-start.5 = (bf16[2,6,3,2,512]{4,3,2,1,0:T(2,128)(2,1)S(1)}, bf16[2,6,3,2,512]{4,3,2,1,0:T(2,128)(2,1)S(1)}, u32[]{:S(2)}, u32[]{:S(2)}) collective-permute-start(bf16[2,6,3,2,512]{4,3,2,1,0:T(2,128)(2,1)S(1)} %get-tuple-element.28), channel_id=1, source_target_pairs={{0,31},{1,0},{2,1},{3,2},{4,3},{5,4},{6,5},{7,6},{8,7},{9,8},{10,9... | collective-permute-start | bytes 221192 | tf_op jit(solution)/shard_map/ppermute | solution.py:32
  25.0 0.0 collective-permute-done.3.refs_0_
  25.0 0.5 %collective-permute-done.4.refs_1_ = bf16[2,6,3,2,512]{4,3,2,1,0:T(2,128)(2,1)S(1)} collective-permute-done((bf16[2,6,3,2,512]{4,3,2,1,0:T(2,128)(2,1)S(1)}, bf16[2,6,3,2,512]{4,3,2,1,0:T(2,128)(2,1)S(1)}, u32[]{:S(2)}, u32[]{:S(2)}) %collective-permute-start.4) | collective-permute-done | bytes 73760 | tf_op jit(solution)/shard_map/ppermute | solution.py:32
  25.5 1.5 %collective-permute-done.5.refs_2_ = bf16[2,6,3,2,512]{4,3,2,1,0:T(2,128)(2,1)S(1)} collective-permute-done((bf16[2,6,3,2,512]{4,3,2,1,0:T(2,128)(2,1)S(1)}, bf16[2,6,3,2,512]{4,3,2,1,0:T(2,128)(2,1)S(1)}, u32[]{:S(2)}, u32[]{:S(2)}) %collective-permute-start.5) | collective-permute-done | bytes 73760 | tf_op jit(solution)/shard_map/ppermute | solution.py:32
  27.0 0.8 %join.1 = (bf16[12,6,2,512]{3,2,1,0:T(2,128)(2,1)}, bf16[12,6,2,512]{3,2,1,0:T(2,128)(2,1)}) custom-call(bf16[2,6,3,2,512]{4,3,2,1,0:T(2,128)(2,1)S(1)} %collective-permute-done.3.refs_0_, bf16[2,6,3,2,512]{4,3,2,1,0:T(2,128)(2,1)S(1)} %collective-permute-done.4.refs_1_, bf16[2,6,3,2,512]{4,3,2,1,0:T(2,128)(2,1)S(1)} %collective-permute-done.5.refs_2_, ...), custom_call_target="tpu_custom_call" | custom-call | tf_op jit(solution)/shard_map/join/pallas_call | solution.py:284
Async XLA Ops:
  1.6 11.5 %collective-permute-start = (bf16[2,6,3,2,512]{4,3,2,1,0:T(2,128)(2,1)S(1)}, bf16[2,6,3,2,512]{4,3,2,1,0:T(2,128)(2,1)S(1)}, u32[]{:S(2)}, u32[]{:S(2)}) collective-permute-start(bf16[2,6,3,2,512]{4,3,2,1,0:T(2,128)(2,1)S(1)} %get-tuple-element.17), channel_id=1, source_target_pairs={{0,33},{1,34},{2,35},{3,36},{4,37},{5,38},{6,39},{7,40},{8,41},{9,... | collective-permute-start | bytes 221192 | tf_op jit(solution)/shard_map/ppermute | solution.py:32
  3.2 9.8 %collective-permute-start.1 = (bf16[2,6,3,2,512]{4,3,2,1,0:T(2,128)(2,1)S(1)}, bf16[2,6,3,2,512]{4,3,2,1,0:T(2,128)(2,1)S(1)}, u32[]{:S(2)}, u32[]{:S(2)}) collective-permute-start(bf16[2,6,3,2,512]{4,3,2,1,0:T(2,128)(2,1)S(1)} %get-tuple-element.18), channel_id=1, source_target_pairs={{0,32},{1,33},{2,34},{3,35},{4,36},{5,37},{6,38},{7,39},{8,40},{9,... | collective-permute-start | bytes 221192 | tf_op jit(solution)/shard_map/ppermute | solution.py:32
  5.6 7.4 %collective-permute-start.2 = (bf16[2,6,3,2,512]{4,3,2,1,0:T(2,128)(2,1)S(1)}, bf16[2,6,3,2,512]{4,3,2,1,0:T(2,128)(2,1)S(1)}, u32[]{:S(2)}, u32[]{:S(2)}) collective-permute-start(bf16[2,6,3,2,512]{4,3,2,1,0:T(2,128)(2,1)S(1)} %get-tuple-element.19), channel_id=1, source_target_pairs={{0,1},{1,2},{2,3},{3,4},{4,5},{5,6},{6,7},{7,8},{8,9},{9,10},{10,1... | collective-permute-start | bytes 221192 | tf_op jit(solution)/shard_map/ppermute | solution.py:32
  15.8 9.2 %collective-permute-start.3 = (bf16[2,6,3,2,512]{4,3,2,1,0:T(2,128)(2,1)S(1)}, bf16[2,6,3,2,512]{4,3,2,1,0:T(2,128)(2,1)S(1)}, u32[]{:S(2)}, u32[]{:S(2)}) collective-permute-start(bf16[2,6,3,2,512]{4,3,2,1,0:T(2,128)(2,1)S(1)} %get-tuple-element.26), channel_id=1, source_target_pairs={{0,255},{1,224},{2,225},{3,226},{4,227},{5,228},{6,229},{7,230},{8... | collective-permute-start | bytes 221192 | tf_op jit(solution)/shard_map/ppermute | solution.py:32
  19.7 5.9 %collective-permute-start.4 = (bf16[2,6,3,2,512]{4,3,2,1,0:T(2,128)(2,1)S(1)}, bf16[2,6,3,2,512]{4,3,2,1,0:T(2,128)(2,1)S(1)}, u32[]{:S(2)}, u32[]{:S(2)}) collective-permute-start(bf16[2,6,3,2,512]{4,3,2,1,0:T(2,128)(2,1)S(1)} %get-tuple-element.27), channel_id=1, source_target_pairs={{0,224},{1,225},{2,226},{3,227},{4,228},{5,229},{6,230},{7,231},{8... | collective-permute-start | bytes 221192 | tf_op jit(solution)/shard_map/ppermute | solution.py:32
  21.7 5.3 %collective-permute-start.5 = (bf16[2,6,3,2,512]{4,3,2,1,0:T(2,128)(2,1)S(1)}, bf16[2,6,3,2,512]{4,3,2,1,0:T(2,128)(2,1)S(1)}, u32[]{:S(2)}, u32[]{:S(2)}) collective-permute-start(bf16[2,6,3,2,512]{4,3,2,1,0:T(2,128)(2,1)S(1)} %get-tuple-element.28), channel_id=1, source_target_pairs={{0,31},{1,0},{2,1},{3,2},{4,3},{5,4},{6,5},{7,6},{8,7},{9,8},{10,9... | collective-permute-start | bytes 221192 | tf_op jit(solution)/shard_map/ppermute | solution.py:32

commit v5 on v4

--- a/solution.py
+++ b/solution.py
@@ -82,7 +82,7 @@
 
 
 def join_kernel(*refs):
-    quarters, outs, sems = refs[:4], refs[4:6], refs[6]
+    quarters, outs, sems = (*refs[2::-1], refs[3]), refs[4:6], refs[6]
     copies = []
     for k, (rows, cols) in enumerate(corners(*outs[0].shape[:2])):
         for f, field in enumerate(outs):
@@ -289,7 +289,7 @@
         scratch_shapes=[pltpu.SemaphoreType.DMA((4, 2))],
         compiler_params=few,
         name="join",
-    )(from_both, from_lat, from_lon, own)
+    )(from_lon, from_lat, from_both, own)
     return (updated.transpose(2, 0, 1, 3), latent_grad.transpose(2, 0, 1, 3))
 
 

time: 27.9 us -> 27.6 us (0.989)
  starting transfers between devices: 15 us -> 13.3 us
  waiting for transfers between devices: 5.41 us -> 6.51 us
    ppermute x6, starting transfers between devices: 15 us -> 13.3 us  [neighbour(): return lax.ppermute(piece, ('lat', 'lon'), pairs)]
    ppermute x6, waiting for transfers between devices: 5.41 us -> 6.51 us  [neighbour(): return lax.ppermute(piece, ('lat', 'lon'), pairs)]
where the time goes in v5:
time: 27.6 us; the launch traced here: 27.2 us
  starting transfers between devices  13.3 us (48%)
  Pallas kernels  6.72 us (24%)
  waiting for transfers between devices  6.51 us (24%)
  between operations  0.66 us (2%)
    ppermute x6, starting transfers between devices, neighbour(): return lax.ppermute(piece, ('lat', 'lon'), pairs)  13.3 us
    ppermute x6, waiting for transfers between devices, neighbour(): return lax.ppermute(piece, ('lat', 'lon'), pairs)  6.51 us
    pallas_call x1, Pallas kernels, body(): pl.pallas_call(window_kernel, in_specs=[in_vmem] * 9, out_specs=[in_vmem]...  2.81 us
    pallas_call x1, Pallas kernels, body(): pl.pallas_call(fetch_kernel, in_specs=[in_hbm] * 5, out_specs=[in_vmem] *...  2.22 us
    pallas_call x1, Pallas kernels, body(): pl.pallas_call(cut_kernel, in_specs=[in_hbm] * 2, out_specs=[in_vmem] * 3...  0.91 us
    pallas_call x1, Pallas kernels, body(): pl.pallas_call(join_kernel, in_specs=[in_vmem] * 4, out_specs=[in_hbm] *...  0.77 us
  transfers between devices with their start and end apart: 6, of which 3 were waited for; matrix products, arithmetic and copies ran while one was open for 0% of the time, Pallas kernels for 8%

profile of v5, /device:TPU:2, one launch (start us, length us, event | category | flops | bytes accessed | tf_op | source)
XLA Modules:
  0.0 27.2 jit_solution(18058879464952558360)
XLA Ops:
  0.6 0.9 %cut.1 = (bf16[2,6,3,2,512]{4,3,2,1,0:T(2,128)(2,1)S(1)}, bf16[2,6,3,2,512]{4,3,2,1,0:T(2,128)(2,1)S(1)}, bf16[2,6,3,2,512]{4,3,2,1,0:T(2,128)(2,1)S(1)}) custom-call(bf16[12,6,2,512]{3,2,1,0:T(2,128)(2,1)} %bitcast.5, bf16[12,6,2,512]{3,2,1,0:T(2,128)(2,1)} %bitcast.7), custom_call_target="tpu_custom_call" | custom-call | tf_op jit(solution)/shard_map/cut/pallas_call | solution.py:228
  1.6 1.6 %collective-permute-start = (bf16[2,6,3,2,512]{4,3,2,1,0:T(2,128)(2,1)S(1)}, bf16[2,6,3,2,512]{4,3,2,1,0:T(2,128)(2,1)S(1)}, u32[]{:S(2)}, u32[]{:S(2)}) collective-permute-start(bf16[2,6,3,2,512]{4,3,2,1,0:T(2,128)(2,1)S(1)} %get-tuple-element.17), channel_id=1, source_target_pairs={{0,33},{1,34},{2,35},{3,36},{4,37},{5,38},{6,39},{7,40},{8,41},{9,... | collective-permute-start | bytes 221192 | tf_op jit(solution)/shard_map/ppermute | solution.py:32
  3.2 2.4 %collective-permute-start.1 = (bf16[2,6,3,2,512]{4,3,2,1,0:T(2,128)(2,1)S(1)}, bf16[2,6,3,2,512]{4,3,2,1,0:T(2,128)(2,1)S(1)}, u32[]{:S(2)}, u32[]{:S(2)}) collective-permute-start(bf16[2,6,3,2,512]{4,3,2,1,0:T(2,128)(2,1)S(1)} %get-tuple-element.18), channel_id=1, source_target_pairs={{0,32},{1,33},{2,34},{3,35},{4,36},{5,37},{6,38},{7,39},{8,40},{9,... | collective-permute-start | bytes 221192 | tf_op jit(solution)/shard_map/ppermute | solution.py:32
  5.6 1.7 %collective-permute-start.2 = (bf16[2,6,3,2,512]{4,3,2,1,0:T(2,128)(2,1)S(1)}, bf16[2,6,3,2,512]{4,3,2,1,0:T(2,128)(2,1)S(1)}, u32[]{:S(2)}, u32[]{:S(2)}) collective-permute-start(bf16[2,6,3,2,512]{4,3,2,1,0:T(2,128)(2,1)S(1)} %get-tuple-element.19), channel_id=1, source_target_pairs={{0,1},{1,2},{2,3},{3,4},{4,5},{5,6},{6,7},{7,8},{8,9},{9,10},{10,1... | collective-permute-start | bytes 221192 | tf_op jit(solution)/shard_map/ppermute | solution.py:32
  7.4 2.2 %fetch.1 = (bf16[2,6,3,2,512]{4,3,2,1,0:T(2,128)(2,1)S(1)}, f32[1,512]{1,0:T(1,128)S(1)}, bf16[512,1536]{1,0:T(8,128)(2,1)S(1)}, bf16[512,512]{1,0:T(8,128)(2,1)...) custom-call(bf16[12,6,2,512]{3,2,1,0:T(2,128)(2,1)} %bitcast.6, bf16[12,6,2,512]{3,2,1,0:T(2,128)(2,1)} %bitcast.8, ...), custom_call_target="tpu_custom_call" | custom-call | bytes 4194304 | tf_op jit(solution)/shard_map/fetch/pallas_call | solution.py:242
  9.6 3.4 %collective-permute-done.ahead_both = bf16[2,6,3,2,512]{4,3,2,1,0:T(2,128)(2,1)S(1)} collective-permute-done((bf16[2,6,3,2,512]{4,3,2,1,0:T(2,128)(2,1)S(1)}, bf16[2,6,3,2,512]{4,3,2,1,0:T(2,128)(2,1)S(1)}, u32[]{:S(2)}, u32[]{:S(2)}) %collective-permute-start) | collective-permute-done | bytes 73760 | tf_op jit(solution)/shard_map/ppermute | solution.py:32
  13.0 0.0 collective-permute-done.1.ahead_lat
  13.0 0.0 collective-permute-done.2.ahead_lon
  13.0 2.8 %window.1 = (bf16[2,6,3,2,512]{4,3,2,1,0:T(2,128)(2,1)S(1)}, bf16[2,6,3,2,512]{4,3,2,1,0:T(2,128)(2,1)S(1)}, bf16[2,6,3,2,512]{4,3,2,1,0:T(2,128)(2,1)S(1)}, bf16[2,6,3,2,512]{4,3,2,1,0:T(2,128)(2,1)S(1)}) custom-call(bf16[2,6,3,2,512]{4,3,2,1,0:T(2,128)(2,1)S(1)} %collective-permute-done.ahead_both, ...), custom_call_target="tpu_custom_call" | custom-call | tf_op jit(solution)/shard_map/window/pallas_call | solution.py:260
  15.8 2.6 %collective-permute-start.3 = (bf16[2,6,3,2,512]{4,3,2,1,0:T(2,128)(2,1)S(1)}, bf16[2,6,3,2,512]{4,3,2,1,0:T(2,128)(2,1)S(1)}, u32[]{:S(2)}, u32[]{:S(2)}) collective-permute-start(bf16[2,6,3,2,512]{4,3,2,1,0:T(2,128)(2,1)S(1)} %get-tuple-element.26), channel_id=1, source_target_pairs={{0,31},{1,0},{2,1},{3,2},{4,3},{5,4},{6,5},{7,6},{8,7},{9,8},{10,9... | collective-permute-start | bytes 221192 | tf_op jit(solution)/shard_map/ppermute | solution.py:32
  18.4 2.7 %collective-permute-start.4 = (bf16[2,6,3,2,512]{4,3,2,1,0:T(2,128)(2,1)S(1)}, bf16[2,6,3,2,512]{4,3,2,1,0:T(2,128)(2,1)S(1)}, u32[]{:S(2)}, u32[]{:S(2)}) collective-permute-start(bf16[2,6,3,2,512]{4,3,2,1,0:T(2,128)(2,1)S(1)} %get-tuple-element.27), channel_id=1, source_target_pairs={{0,224},{1,225},{2,226},{3,227},{4,228},{5,229},{6,230},{7,231},{8... | collective-permute-start | bytes 221192 | tf_op jit(solution)/shard_map/ppermute | solution.py:32
  21.1 2.2 %collective-permute-start.5 = (bf16[2,6,3,2,512]{4,3,2,1,0:T(2,128)(2,1)S(1)}, bf16[2,6,3,2,512]{4,3,2,1,0:T(2,128)(2,1)S(1)}, u32[]{:S(2)}, u32[]{:S(2)}) collective-permute-start(bf16[2,6,3,2,512]{4,3,2,1,0:T(2,128)(2,1)S(1)} %get-tuple-element.28), channel_id=1, source_target_pairs={{0,255},{1,224},{2,225},{3,226},{4,227},{5,228},{6,229},{7,230},{8... | collective-permute-start | bytes 221192 | tf_op jit(solution)/shard_map/ppermute | solution.py:32
  23.3 0.0 collective-permute-done.3.refs_0_
  23.3 1.7 %collective-permute-done.4.refs_1_ = bf16[2,6,3,2,512]{4,3,2,1,0:T(2,128)(2,1)S(1)} collective-permute-done((bf16[2,6,3,2,512]{4,3,2,1,0:T(2,128)(2,1)S(1)}, bf16[2,6,3,2,512]{4,3,2,1,0:T(2,128)(2,1)S(1)}, u32[]{:S(2)}, u32[]{:S(2)}) %collective-permute-start.4) | collective-permute-done | bytes 73760 | tf_op jit(solution)/shard_map/ppermute | solution.py:32
  25.0 1.4 %collective-permute-done.5.refs_2_ = bf16[2,6,3,2,512]{4,3,2,1,0:T(2,128)(2,1)S(1)} collective-permute-done((bf16[2,6,3,2,512]{4,3,2,1,0:T(2,128)(2,1)S(1)}, bf16[2,6,3,2,512]{4,3,2,1,0:T(2,128)(2,1)S(1)}, u32[]{:S(2)}, u32[]{:S(2)}) %collective-permute-start.5) | collective-permute-done | bytes 73760 | tf_op jit(solution)/shard_map/ppermute | solution.py:32
  26.4 0.8 %join.1 = (bf16[12,6,2,512]{3,2,1,0:T(2,128)(2,1)}, bf16[12,6,2,512]{3,2,1,0:T(2,128)(2,1)}) custom-call(bf16[2,6,3,2,512]{4,3,2,1,0:T(2,128)(2,1)S(1)} %collective-permute-done.3.refs_0_, bf16[2,6,3,2,512]{4,3,2,1,0:T(2,128)(2,1)S(1)} %collective-permute-done.4.refs_1_, bf16[2,6,3,2,512]{4,3,2,1,0:T(2,128)(2,1)S(1)} %collective-permute-done.5.refs_2_, ...), custom_call_target="tpu_custom_call" | custom-call | tf_op jit(solution)/shard_map/join/pallas_call | solution.py:284
Async XLA Ops:
  1.6 11.5 %collective-permute-start = (bf16[2,6,3,2,512]{4,3,2,1,0:T(2,128)(2,1)S(1)}, bf16[2,6,3,2,512]{4,3,2,1,0:T(2,128)(2,1)S(1)}, u32[]{:S(2)}, u32[]{:S(2)}) collective-permute-start(bf16[2,6,3,2,512]{4,3,2,1,0:T(2,128)(2,1)S(1)} %get-tuple-element.17), channel_id=1, source_target_pairs={{0,33},{1,34},{2,35},{3,36},{4,37},{5,38},{6,39},{7,40},{8,41},{9,... | collective-permute-start | bytes 221192 | tf_op jit(solution)/shard_map/ppermute | solution.py:32
  3.2 9.8 %collective-permute-start.1 = (bf16[2,6,3,2,512]{4,3,2,1,0:T(2,128)(2,1)S(1)}, bf16[2,6,3,2,512]{4,3,2,1,0:T(2,128)(2,1)S(1)}, u32[]{:S(2)}, u32[]{:S(2)}) collective-permute-start(bf16[2,6,3,2,512]{4,3,2,1,0:T(2,128)(2,1)S(1)} %get-tuple-element.18), channel_id=1, source_target_pairs={{0,32},{1,33},{2,34},{3,35},{4,36},{5,37},{6,38},{7,39},{8,40},{9,... | collective-permute-start | bytes 221192 | tf_op jit(solution)/shard_map/ppermute | solution.py:32
  5.6 7.4 %collective-permute-start.2 = (bf16[2,6,3,2,512]{4,3,2,1,0:T(2,128)(2,1)S(1)}, bf16[2,6,3,2,512]{4,3,2,1,0:T(2,128)(2,1)S(1)}, u32[]{:S(2)}, u32[]{:S(2)}) collective-permute-start(bf16[2,6,3,2,512]{4,3,2,1,0:T(2,128)(2,1)S(1)} %get-tuple-element.19), channel_id=1, source_target_pairs={{0,1},{1,2},{2,3},{3,4},{4,5},{5,6},{6,7},{7,8},{8,9},{9,10},{10,1... | collective-permute-start | bytes 221192 | tf_op jit(solution)/shard_map/ppermute | solution.py:32
  15.8 7.5 %collective-permute-start.3 = (bf16[2,6,3,2,512]{4,3,2,1,0:T(2,128)(2,1)S(1)}, bf16[2,6,3,2,512]{4,3,2,1,0:T(2,128)(2,1)S(1)}, u32[]{:S(2)}, u32[]{:S(2)}) collective-permute-start(bf16[2,6,3,2,512]{4,3,2,1,0:T(2,128)(2,1)S(1)} %get-tuple-element.26), channel_id=1, source_target_pairs={{0,31},{1,0},{2,1},{3,2},{4,3},{5,4},{6,5},{7,6},{8,7},{9,8},{10,9... | collective-permute-start | bytes 221192 | tf_op jit(solution)/shard_map/ppermute | solution.py:32
  18.4 6.6 %collective-permute-start.4 = (bf16[2,6,3,2,512]{4,3,2,1,0:T(2,128)(2,1)S(1)}, bf16[2,6,3,2,512]{4,3,2,1,0:T(2,128)(2,1)S(1)}, u32[]{:S(2)}, u32[]{:S(2)}) collective-permute-start(bf16[2,6,3,2,512]{4,3,2,1,0:T(2,128)(2,1)S(1)} %get-tuple-element.27), channel_id=1, source_target_pairs={{0,224},{1,225},{2,226},{3,227},{4,228},{5,229},{6,230},{7,231},{8... | collective-permute-start | bytes 221192 | tf_op jit(solution)/shard_map/ppermute | solution.py:32
  21.1 5.3 %collective-permute-start.5 = (bf16[2,6,3,2,512]{4,3,2,1,0:T(2,128)(2,1)S(1)}, bf16[2,6,3,2,512]{4,3,2,1,0:T(2,128)(2,1)S(1)}, u32[]{:S(2)}, u32[]{:S(2)}) collective-permute-start(bf16[2,6,3,2,512]{4,3,2,1,0:T(2,128)(2,1)S(1)} %get-tuple-element.28), channel_id=1, source_target_pairs={{0,255},{1,224},{2,225},{3,226},{4,227},{5,228},{6,229},{7,230},{8... | collective-permute-start | bytes 221192 | tf_op jit(solution)/shard_map/ppermute | solution.py:32

commit v6 on v5

--- a/solution.py
+++ b/solution.py
@@ -13,13 +13,14 @@
 SLAT = 6
 SLON = 3
 GROUP = 4
+STRIP = 256
 
 MIB = 1 << 20
 NORM_EPS = 1e-05
 MASK_FILL = -1000000000.0
 
 LAT_STEP = 1
-LON_STEP = 1
+LON_STEP = -1
 
 
 def neighbour(piece, lat_by, lon_by):
@@ -64,25 +65,30 @@
     latent, cotangent, gain, qkv, out, own, gain_to, qkv_to, out_to, qkv_turned, out_turned, sems
 ):
     rows, cols = corners(*latent.shape[:2])[3]
-    copies = [
-        pltpu.make_async_copy(qkv, qkv_to, sems.at[0]),
-        pltpu.make_async_copy(out, out_to, sems.at[1]),
-        pltpu.make_async_copy(gain, gain_to, sems.at[2]),
-        pltpu.make_async_copy(latent.at[rows, cols], own.at[0], sems.at[3]),
-        pltpu.make_async_copy(cotangent.at[rows, cols], own.at[1], sems.at[4]),
+    pieces = []
+    for source, into, turned in ((out, out_to, out_turned), (qkv, qkv_to, qkv_turned)):
+        for at in range(0, source.shape[0], STRIP):
+            pieces.append((source, into, turned, pl.ds(at, STRIP)))
+    strips = [
+        pltpu.make_async_copy(source.at[at], into.at[at], sems.at[k])
+        for k, (source, into, _, at) in enumerate(pieces)
     ]
-    for copy in copies:
+    others = [
+        pltpu.make_async_copy(gain, gain_to, sems.at[len(strips)]),
+        pltpu.make_async_copy(latent.at[rows, cols], own.at[0], sems.at[len(strips) + 1]),
+        pltpu.make_async_copy(cotangent.at[rows, cols], own.at[1], sems.at[len(strips) + 2]),
+    ]
+    for copy in strips + others:
         copy.start()
-    copies[1].wait()
-    out_turned[...] = out_to[...].T
-    copies[0].wait()
-    qkv_turned[...] = qkv_to[...].T
-    for copy in copies[2:]:
+    for copy, (_, into, turned, at) in zip(strips, pieces):
         copy.wait()
+        turned[:, at] = into[at].T
+    for copy in others:
+        copy.wait()
 
 
 def join_kernel(*refs):
-    quarters, outs, sems = (*refs[2::-1], refs[3]), refs[4:6], refs[6]
+    quarters, outs, sems = (refs[0], refs[2], refs[1], refs[3]), refs[4:6], refs[6]
     copies = []
     for k, (rows, cols) in enumerate(corners(*outs[0].shape[:2])):
         for f, field in enumerate(outs):
@@ -108,7 +114,7 @@
 
 
 def window_kernel(
-    ahead_both, ahead_lat, ahead_lon, own, gain_ref, qkv_ref, out_ref, qkv_turned, out_turned,
+    ahead_lat, ahead_both, ahead_lon, own, gain_ref, qkv_ref, out_ref, qkv_turned, out_turned,
     both_out, lat_out, lon_out, own_out,
     tokens, cots, scores_ref, low_ref, slopes_ref, wide_query, proj_ref, mixed_ref, grad_ref,
 ):
@@ -251,7 +257,7 @@
             pltpu.VMEM(qkv_weight.shape[::-1], jnp.bfloat16),
             pltpu.VMEM(out_weight.shape[::-1], jnp.bfloat16),
         ],
-        scratch_shapes=[pltpu.SemaphoreType.DMA((5,))],
+        scratch_shapes=[pltpu.SemaphoreType.DMA((2 * features // STRIP + 3,))],
         compiler_params=few,
         cost_estimate=pl.CostEstimate(flops=0, bytes_accessed=4 * MIB, transcendentals=0),
         name="fetch",
@@ -275,7 +281,7 @@
         ],
         compiler_params=pltpu.CompilerParams(vmem_limit_bytes=12 * MIB),
         name="window",
-    )(from_both, from_lat, from_lon, own, *parameters)
+    )(from_lat, from_both, from_lon, own, *parameters)
 
     from_both = neighbour(to_both, -LAT_STEP, -LON_STEP)
     from_lat = neighbour(to_lat, -LAT_STEP, 0)
@@ -289,7 +295,7 @@
         scratch_shapes=[pltpu.SemaphoreType.DMA((4, 2))],
         compiler_params=few,
         name="join",
-    )(from_lon, from_lat, from_both, own)
+    )(from_both, from_lon, from_lat, own)
     return (updated.transpose(2, 0, 1, 3), latent_grad.transpose(2, 0, 1, 3))
 
 

time: 27.6 us -> 26.9 us (0.975)
  waiting for transfers between devices: 6.51 us -> 4.94 us
  starting transfers between devices: 13.3 us -> 14.7 us
  Pallas kernels: 6.72 us -> 6.37 us
    ppermute x6, waiting for transfers between devices: 6.51 us -> 4.94 us  [neighbour(): return lax.ppermute(piece, ('lat', 'lon'), pairs)]
    ppermute x6, starting transfers between devices: 13.3 us -> 14.7 us  [neighbour(): return lax.ppermute(piece, ('lat', 'lon'), pairs)]
    pallas_call x1, Pallas kernels: 2.22 us -> 1.88 us  [body(): pl.pallas_call(fetch_kernel, in_specs=[in_hbm] * 5, out_specs=[in_vmem] *...]
  transfers between devices with their start and end apart: 6 -> 6, of which waited for: 3 -> 3; matrix products, arithmetic and copies ran while one was open for 0% -> 0% of each run, Pallas kernels for 8% -> 7%
where the time goes in v6:
time: 26.9 us; the launch traced here: 26.7 us
  starting transfers between devices  14.7 us (55%)
  Pallas kernels  6.37 us (24%)
  waiting for transfers between devices  4.94 us (18%)
  between operations  0.67 us (2%)
    ppermute x6, starting transfers between devices, neighbour(): return lax.ppermute(piece, ('lat', 'lon'), pairs)  14.7 us
    ppermute x6, waiting for transfers between devices, neighbour(): return lax.ppermute(piece, ('lat', 'lon'), pairs)  4.94 us
    pallas_call x1, Pallas kernels, body(): pl.pallas_call(window_kernel, in_specs=[in_vmem] * 9, out_specs=[in_vmem]...  2.81 us
    pallas_call x1, Pallas kernels, body(): pl.pallas_call(fetch_kernel, in_specs=[in_hbm] * 5, out_specs=[in_vmem] *...  1.88 us
    pallas_call x1, Pallas kernels, body(): pl.pallas_call(cut_kernel, in_specs=[in_hbm] * 2, out_specs=[in_vmem] * 3...  0.91 us
    pallas_call x1, Pallas kernels, body(): pl.pallas_call(join_kernel, in_specs=[in_vmem] * 4, out_specs=[in_hbm] *...  0.77 us
  transfers between devices with their start and end apart: 6, of which 3 were waited for; matrix products, arithmetic and copies ran while one was open for 0% of the time, Pallas kernels for 7%

profile of v6, /device:TPU:2, one launch (start us, length us, event | category | flops | bytes accessed | tf_op | source)
XLA Modules:
  0.0 26.7 jit_solution(11655073141490590487)
XLA Ops:
  0.6 0.9 %cut.1 = (bf16[2,6,3,2,512]{4,3,2,1,0:T(2,128)(2,1)S(1)}, bf16[2,6,3,2,512]{4,3,2,1,0:T(2,128)(2,1)S(1)}, bf16[2,6,3,2,512]{4,3,2,1,0:T(2,128)(2,1)S(1)}) custom-call(bf16[12,6,2,512]{3,2,1,0:T(2,128)(2,1)} %bitcast.5, bf16[12,6,2,512]{3,2,1,0:T(2,128)(2,1)} %bitcast.7), custom_call_target="tpu_custom_call" | custom-call | tf_op jit(solution)/shard_map/cut/pallas_call | solution.py:234
  1.6 2.2 %collective-permute-start = (bf16[2,6,3,2,512]{4,3,2,1,0:T(2,128)(2,1)S(1)}, bf16[2,6,3,2,512]{4,3,2,1,0:T(2,128)(2,1)S(1)}, u32[]{:S(2)}, u32[]{:S(2)}) collective-permute-start(bf16[2,6,3,2,512]{4,3,2,1,0:T(2,128)(2,1)S(1)} %get-tuple-element.17), channel_id=1, source_target_pairs={{0,32},{1,33},{2,34},{3,35},{4,36},{5,37},{6,38},{7,39},{8,40},{9,... | collective-permute-start | bytes 221192 | tf_op jit(solution)/shard_map/ppermute | solution.py:33
  3.8 5.3 %collective-permute-start.1 = (bf16[2,6,3,2,512]{4,3,2,1,0:T(2,128)(2,1)S(1)}, bf16[2,6,3,2,512]{4,3,2,1,0:T(2,128)(2,1)S(1)}, u32[]{:S(2)}, u32[]{:S(2)}) collective-permute-start(bf16[2,6,3,2,512]{4,3,2,1,0:T(2,128)(2,1)S(1)} %get-tuple-element.18), channel_id=1, source_target_pairs={{0,63},{1,32},{2,33},{3,34},{4,35},{5,36},{6,37},{7,38},{8,39},{9,... | collective-permute-start | bytes 221192 | tf_op jit(solution)/shard_map/ppermute | solution.py:33
  9.1 2.6 %collective-permute-start.2 = (bf16[2,6,3,2,512]{4,3,2,1,0:T(2,128)(2,1)S(1)}, bf16[2,6,3,2,512]{4,3,2,1,0:T(2,128)(2,1)S(1)}, u32[]{:S(2)}, u32[]{:S(2)}) collective-permute-start(bf16[2,6,3,2,512]{4,3,2,1,0:T(2,128)(2,1)S(1)} %get-tuple-element.19), channel_id=1, source_target_pairs={{0,31},{1,0},{2,1},{3,2},{4,3},{5,4},{6,5},{7,6},{8,7},{9,8},{10,9... | collective-permute-start | bytes 221192 | tf_op jit(solution)/shard_map/ppermute | solution.py:33
  11.7 1.9 %fetch.1 = (bf16[2,6,3,2,512]{4,3,2,1,0:T(2,128)(2,1)S(1)}, f32[1,512]{1,0:T(1,128)S(1)}, bf16[512,1536]{1,0:T(8,128)(2,1)S(1)}, bf16[512,512]{1,0:T(8,128)(2,1)...) custom-call(bf16[12,6,2,512]{3,2,1,0:T(2,128)(2,1)} %bitcast.6, bf16[12,6,2,512]{3,2,1,0:T(2,128)(2,1)} %bitcast.8, ...), custom_call_target="tpu_custom_call" | custom-call | bytes 4194304 | tf_op jit(solution)/shard_map/fetch/pallas_call | solution.py:248
  13.6 0.0 collective-permute-done.ahead_lat
  13.6 0.0 collective-permute-done.1.ahead_both
  13.6 0.1 collective-permute-done.2.ahead_lon
  13.7 2.8 %window.1 = (bf16[2,6,3,2,512]{4,3,2,1,0:T(2,128)(2,1)S(1)}, bf16[2,6,3,2,512]{4,3,2,1,0:T(2,128)(2,1)S(1)}, bf16[2,6,3,2,512]{4,3,2,1,0:T(2,128)(2,1)S(1)}, bf16[2,6,3,2,512]{4,3,2,1,0:T(2,128)(2,1)S(1)}) custom-call(bf16[2,6,3,2,512]{4,3,2,1,0:T(2,128)(2,1)S(1)} %collective-permute-done.ahead_lat, ...), custom_call_target="tpu_custom_call" | custom-call | tf_op jit(solution)/shard_map/window/pallas_call | solution.py:266
  16.5 2.2 %collective-permute-start.3 = (bf16[2,6,3,2,512]{4,3,2,1,0:T(2,128)(2,1)S(1)}, bf16[2,6,3,2,512]{4,3,2,1,0:T(2,128)(2,1)S(1)}, u32[]{:S(2)}, u32[]{:S(2)}) collective-permute-start(bf16[2,6,3,2,512]{4,3,2,1,0:T(2,128)(2,1)S(1)} %get-tuple-element.26), channel_id=1, source_target_pairs={{0,225},{1,226},{2,227},{3,228},{4,229},{5,230},{6,231},{7,232},{8... | collective-permute-start | bytes 221192 | tf_op jit(solution)/shard_map/ppermute | solution.py:33
  18.7 0.0 collective-permute-start.4
  18.7 2.3 %collective-permute-start.5 = (bf16[2,6,3,2,512]{4,3,2,1,0:T(2,128)(2,1)S(1)}, bf16[2,6,3,2,512]{4,3,2,1,0:T(2,128)(2,1)S(1)}, u32[]{:S(2)}, u32[]{:S(2)}) collective-permute-start(bf16[2,6,3,2,512]{4,3,2,1,0:T(2,128)(2,1)S(1)} %get-tuple-element.28), channel_id=1, source_target_pairs={{0,224},{1,225},{2,226},{3,227},{4,228},{5,229},{6,230},{7,231},{8... | collective-permute-start | bytes 221192 | tf_op jit(solution)/shard_map/ppermute | solution.py:33
  21.1 2.7 %collective-permute-done.3.refs_0_ = bf16[2,6,3,2,512]{4,3,2,1,0:T(2,128)(2,1)S(1)} collective-permute-done((bf16[2,6,3,2,512]{4,3,2,1,0:T(2,128)(2,1)S(1)}, bf16[2,6,3,2,512]{4,3,2,1,0:T(2,128)(2,1)S(1)}, u32[]{:S(2)}, u32[]{:S(2)}) %collective-permute-start.3) | collective-permute-done | bytes 73760 | tf_op jit(solution)/shard_map/ppermute | solution.py:33
  23.8 2.1 %collective-permute-done.4.refs_1_ = bf16[2,6,3,2,512]{4,3,2,1,0:T(2,128)(2,1)S(1)} collective-permute-done((bf16[2,6,3,2,512]{4,3,2,1,0:T(2,128)(2,1)S(1)}, bf16[2,6,3,2,512]{4,3,2,1,0:T(2,128)(2,1)S(1)}, u32[]{:S(2)}, u32[]{:S(2)}) %collective-permute-start.4) | collective-permute-done | bytes 73760 | tf_op jit(solution)/shard_map/ppermute | solution.py:33
  25.9 0.0 collective-permute-done.5.refs_2_
  25.9 0.8 %join.1 = (bf16[12,6,2,512]{3,2,1,0:T(2,128)(2,1)}, bf16[12,6,2,512]{3,2,1,0:T(2,128)(2,1)}) custom-call(bf16[2,6,3,2,512]{4,3,2,1,0:T(2,128)(2,1)S(1)} %collective-permute-done.3.refs_0_, bf16[2,6,3,2,512]{4,3,2,1,0:T(2,128)(2,1)S(1)} %collective-permute-done.4.refs_1_, bf16[2,6,3,2,512]{4,3,2,1,0:T(2,128)(2,1)S(1)} %collective-permute-done.5.refs_2_, ...), custom_call_target="tpu_custom_call" | custom-call | tf_op jit(solution)/shard_map/join/pallas_call | solution.py:290
Async XLA Ops:
  1.6 12.1 %collective-permute-start = (bf16[2,6,3,2,512]{4,3,2,1,0:T(2,128)(2,1)S(1)}, bf16[2,6,3,2,512]{4,3,2,1,0:T(2,128)(2,1)S(1)}, u32[]{:S(2)}, u32[]{:S(2)}) collective-permute-start(bf16[2,6,3,2,512]{4,3,2,1,0:T(2,128)(2,1)S(1)} %get-tuple-element.17), channel_id=1, source_target_pairs={{0,32},{1,33},{2,34},{3,35},{4,36},{5,37},{6,38},{7,39},{8,40},{9,... | collective-permute-start | bytes 221192 | tf_op jit(solution)/shard_map/ppermute | solution.py:33
  3.8 9.9 %collective-permute-start.1 = (bf16[2,6,3,2,512]{4,3,2,1,0:T(2,128)(2,1)S(1)}, bf16[2,6,3,2,512]{4,3,2,1,0:T(2,128)(2,1)S(1)}, u32[]{:S(2)}, u32[]{:S(2)}) collective-permute-start(bf16[2,6,3,2,512]{4,3,2,1,0:T(2,128)(2,1)S(1)} %get-tuple-element.18), channel_id=1, source_target_pairs={{0,63},{1,32},{2,33},{3,34},{4,35},{5,36},{6,37},{7,38},{8,39},{9,... | collective-permute-start | bytes 221192 | tf_op jit(solution)/shard_map/ppermute | solution.py:33
  9.1 4.6 %collective-permute-start.2 = (bf16[2,6,3,2,512]{4,3,2,1,0:T(2,128)(2,1)S(1)}, bf16[2,6,3,2,512]{4,3,2,1,0:T(2,128)(2,1)S(1)}, u32[]{:S(2)}, u32[]{:S(2)}) collective-permute-start(bf16[2,6,3,2,512]{4,3,2,1,0:T(2,128)(2,1)S(1)} %get-tuple-element.19), channel_id=1, source_target_pairs={{0,31},{1,0},{2,1},{3,2},{4,3},{5,4},{6,5},{7,6},{8,7},{9,8},{10,9... | collective-permute-start | bytes 221192 | tf_op jit(solution)/shard_map/ppermute | solution.py:33
  16.5 7.3 %collective-permute-start.3 = (bf16[2,6,3,2,512]{4,3,2,1,0:T(2,128)(2,1)S(1)}, bf16[2,6,3,2,512]{4,3,2,1,0:T(2,128)(2,1)S(1)}, u32[]{:S(2)}, u32[]{:S(2)}) collective-permute-start(bf16[2,6,3,2,512]{4,3,2,1,0:T(2,128)(2,1)S(1)} %get-tuple-element.26), channel_id=1, source_target_pairs={{0,225},{1,226},{2,227},{3,228},{4,229},{5,230},{6,231},{7,232},{8... | collective-permute-start | bytes 221192 | tf_op jit(solution)/shard_map/ppermute | solution.py:33
  18.7 7.2 %collective-permute-start.4 = (bf16[2,6,3,2,512]{4,3,2,1,0:T(2,128)(2,1)S(1)}, bf16[2,6,3,2,512]{4,3,2,1,0:T(2,128)(2,1)S(1)}, u32[]{:S(2)}, u32[]{:S(2)}) collective-permute-start(bf16[2,6,3,2,512]{4,3,2,1,0:T(2,128)(2,1)S(1)} %get-tuple-element.27), channel_id=1, source_target_pairs={{0,1},{1,2},{2,3},{3,4},{4,5},{5,6},{6,7},{7,8},{8,9},{9,10},{10,1... | collective-permute-start | bytes 221192 | tf_op jit(solution)/shard_map/ppermute | solution.py:33
  18.7 7.2 %collective-permute-start.5 = (bf16[2,6,3,2,512]{4,3,2,1,0:T(2,128)(2,1)S(1)}, bf16[2,6,3,2,512]{4,3,2,1,0:T(2,128)(2,1)S(1)}, u32[]{:S(2)}, u32[]{:S(2)}) collective-permute-start(bf16[2,6,3,2,512]{4,3,2,1,0:T(2,128)(2,1)S(1)} %get-tuple-element.28), channel_id=1, source_target_pairs={{0,224},{1,225},{2,226},{3,227},{4,228},{5,229},{6,230},{7,231},{8... | collective-permute-start | bytes 221192 | tf_op jit(solution)/shard_map/ppermute | solution.py:33

commit v7 on v6

--- a/solution.py
+++ b/solution.py
@@ -1,3 +1,4 @@
+import functools
 import math
 
 import jax
@@ -65,6 +66,8 @@
     latent, cotangent, gain, qkv, out, own, gain_to, qkv_to, out_to, qkv_turned, out_turned, sems
 ):
     rows, cols = corners(*latent.shape[:2])[3]
+    width = out.shape[1]
+    scale = 1.0 / math.sqrt(width // HEADS)
     pieces = []
     for source, into, turned in ((out, out_to, out_turned), (qkv, qkv_to, qkv_turned)):
         for at in range(0, source.shape[0], STRIP):
@@ -82,16 +85,20 @@
         copy.start()
     for copy, (_, into, turned, at) in zip(strips, pieces):
         copy.wait()
+        if into is qkv_to:
+            into[at, :width] = into[at, :width] * jnp.asarray(scale, jnp.bfloat16)
         turned[:, at] = into[at].T
     for copy in others:
         copy.wait()
 
 
-def join_kernel(*refs):
-    quarters, outs, sems = (refs[0], refs[2], refs[1], refs[3]), refs[4:6], refs[6]
+def join_kernel(which, *refs):
+    quarters, outs, sems = refs[: len(which)], refs[-3:-1], refs[-1]
+    places = corners(*outs[0].shape[:2])
     copies = []
-    for k, (rows, cols) in enumerate(corners(*outs[0].shape[:2])):
+    for k, place in enumerate(which):
         for f, field in enumerate(outs):
+            rows, cols = places[place]
             copies.append(
                 pltpu.make_async_copy(quarters[k].at[f], field.at[rows, cols], sems.at[k, f])
             )
@@ -124,7 +131,6 @@
     quarter = rows * cols * levels
     window = 4 * quarter
     head_dim = features // HEADS
-    scale = 1.0 / math.sqrt(head_dim)
 
     for k, ref in enumerate(quarters):
         for f, into in enumerate((tokens, cots)):
@@ -133,9 +139,7 @@
                     at = k * quarter + (r * cols + c) * levels
                     into[at : at + levels, :] = ref[f, r, c].astype(jnp.float32)
 
-    proj = matmul(tokens[...].astype(jnp.bfloat16), qkv_ref[...]).astype(jnp.bfloat16)
-    proj_ref[:, features:] = proj[:, features:]
-    proj_ref[:, :features] = proj[:, :features] * jnp.asarray(scale, jnp.bfloat16)
+    proj_ref[...] = matmul(tokens[...].astype(jnp.bfloat16), qkv_ref[...]).astype(jnp.bfloat16)
 
     last = lax.axis_index("lat") == (lax.axis_size("lat") - 1 if LAT_STEP < 0 else 0)
     wide = GROUP * head_dim
@@ -146,7 +150,7 @@
     bias = jnp.where((key_row < 2 * quarter) != (query_row < 2 * quarter), fill, 0.0)
     lane = lax.broadcasted_iota(jnp.int32, (1, wide), 1)
     only = [(lane // head_dim == e).astype(jnp.float32).astype(jnp.bfloat16) for e in range(GROUP)]
-    mine = [lax.broadcasted_iota(jnp.int32, (window, wide), 1) < head_dim * e for e in range(1, GROUP)]
+    first = lax.broadcasted_iota(jnp.int32, (window, 2 * head_dim), 1) < head_dim
 
     def part(ref, which, group):
         at = which * features + wide * group
@@ -155,11 +159,13 @@
     def fanned(x):
         return jnp.concatenate([x * only[e] for e in range(GROUP)], axis=0)
 
-    def gathered(x):
-        out = x[(GROUP - 1) * window :]
-        for e in range(GROUP - 2, -1, -1):
-            out = jnp.where(mine[e], x[e * window : (e + 1) * window], out)
-        return out
+    def gathered(packed_rows, x):
+        rows_first, parts = packed_rows.T, []
+        for pair in range(GROUP // 2):
+            lanes = slice(2 * head_dim * pair, 2 * head_dim * (pair + 1))
+            both = matmul(rows_first[2 * window * pair : 2 * window * (pair + 1)], x[:, lanes])
+            parts.append(jnp.where(first, both[:window], both[window:]))
+        return jnp.concatenate(parts, axis=1)
 
     for group in range(HEADS // GROUP):
         wide_query[group] = fanned(part(proj_ref, 0, group))
@@ -174,7 +180,7 @@
 
     for group in range(HEADS // GROUP):
         at = wide * group
-        mixed = gathered(down(low_ref[group], part(proj_ref, 2, group)))
+        mixed = gathered(low_ref[group], part(proj_ref, 2, group))
         mixed_ref[:, at : at + wide] = mixed.astype(jnp.bfloat16)
 
     branch = matmul(mixed_ref[...], out_ref[...]).astype(jnp.bfloat16).astype(jnp.float32)
@@ -205,7 +211,7 @@
         low_ref[group] = (probs * (grad_probs - along)).astype(jnp.bfloat16)
 
     for group in range(HEADS // GROUP):
-        put(0, group, gathered(down(low_ref[group], part(proj_ref, 1, group))) * scale)
+        put(0, group, gathered(low_ref[group], part(proj_ref, 1, group)))
         put(1, group, matmul(low_ref[group], wide_query[group]))
 
     grad_tokens = matmul(grad_ref[...], qkv_turned[...]).astype(jnp.bfloat16).astype(jnp.float32)
@@ -287,15 +293,20 @@
     from_lat = neighbour(to_lat, -LAT_STEP, 0)
     from_lon = neighbour(to_lon, 0, -LON_STEP)
 
-    updated, latent_grad = pl.pallas_call(
-        join_kernel,
-        in_specs=[in_vmem] * 4,
-        out_specs=[in_hbm] * 2,
-        out_shape=[jax.ShapeDtypeStruct((rows, cols, levels, features), jnp.bfloat16)] * 2,
-        scratch_shapes=[pltpu.SemaphoreType.DMA((4, 2))],
-        compiler_params=few,
-        name="join",
-    )(from_both, from_lon, from_lat, own)
+    def join(which, quarters, outs=()):
+        return pl.pallas_call(
+            functools.partial(join_kernel, which),
+            in_specs=[in_vmem] * len(which) + [in_hbm] * len(outs),
+            out_specs=[in_hbm] * 2,
+            out_shape=[pltpu.HBM((rows, cols, levels, features), jnp.bfloat16)] * 2,
+            scratch_shapes=[pltpu.SemaphoreType.DMA((len(which), 2))],
+            input_output_aliases={len(which) + f: f for f in range(len(outs))},
+            compiler_params=few,
+            name="join",
+        )(*quarters, *outs)
+
+    outs = join((3,), (own,))
+    updated, latent_grad = join((0, 2, 1), (from_both, from_lon, from_lat), tuple(outs))
     return (updated.transpose(2, 0, 1, 3), latent_grad.transpose(2, 0, 1, 3))
 
 

time: 26.9 us -> 26.8 us (level)
  waiting for transfers between devices: 4.94 us -> 4.29 us
  Pallas kernels: 6.37 us -> 6.92 us
    ppermute x6, waiting for transfers between devices: 4.94 us -> 4.29 us  [neighbour(): return lax.ppermute(piece, ('lat', 'lon'), pairs)]
    pallas_call x1 -> x2, Pallas kernels: 0.77 us -> 1.37 us  [join(): pl.pallas_call(functools.partial(join_kernel, which), in_specs=[in_vmem]...]
  transfers between devices with their start and end apart: 6 -> 6, of which waited for: 3 -> 3; matrix products, arithmetic and copies ran while one was open for 0% -> 0% of each run, Pallas kernels for 7% -> 9%
where the time goes in v7:
time: 26.8 us; the launch traced here: 26.6 us
  starting transfers between devices  14.7 us (55%)
  Pallas kernels  6.92 us (26%)
  waiting for transfers between devices  4.29 us (16%)
  between operations  0.68 us (3%)
    ppermute x6, starting transfers between devices, neighbour(): return lax.ppermute(piece, ('lat', 'lon'), pairs)  14.7 us
    ppermute x6, waiting for transfers between devices, neighbour(): return lax.ppermute(piece, ('lat', 'lon'), pairs)  4.29 us
    pallas_call x1, Pallas kernels, body(): pl.pallas_call(window_kernel, in_specs=[in_vmem] * 9, out_specs=[in_vmem]...  2.75 us
    pallas_call x1, Pallas kernels, body(): pl.pallas_call(fetch_kernel, in_specs=[in_hbm] * 5, out_specs=[in_vmem] *...  1.88 us
    pallas_call x2, Pallas kernels, join(): pl.pallas_call(functools.partial(join_kernel, which), in_specs=[in_vmem]...  1.37 us
    pallas_call x1, Pallas kernels, body(): pl.pallas_call(cut_kernel, in_specs=[in_hbm] * 2, out_specs=[in_vmem] * 3...  0.91 us
  transfers between devices with their start and end apart: 6, of which 3 were waited for; matrix products, arithmetic and copies ran while one was open for 0% of the time, Pallas kernels for 9%

profile of v7, /device:TPU:2, one launch (start us, length us, event | category | flops | bytes accessed | tf_op | source)
XLA Modules:
  0.0 26.6 jit_solution(3939814050120237602)
XLA Ops:
  0.6 0.9 %cut.1 = (bf16[2,6,3,2,512]{4,3,2,1,0:T(2,128)(2,1)S(1)}, bf16[2,6,3,2,512]{4,3,2,1,0:T(2,128)(2,1)S(1)}, bf16[2,6,3,2,512]{4,3,2,1,0:T(2,128)(2,1)S(1)}) custom-call(bf16[12,6,2,512]{3,2,1,0:T(2,128)(2,1)} %bitcast.5, bf16[12,6,2,512]{3,2,1,0:T(2,128)(2,1)} %bitcast.7), custom_call_target="tpu_custom_call" | custom-call | tf_op jit(solution)/shard_map/cut/pallas_call | solution.py:240
  1.6 2.2 %collective-permute-start = (bf16[2,6,3,2,512]{4,3,2,1,0:T(2,128)(2,1)S(1)}, bf16[2,6,3,2,512]{4,3,2,1,0:T(2,128)(2,1)S(1)}, u32[]{:S(2)}, u32[]{:S(2)}) collective-permute-start(bf16[2,6,3,2,512]{4,3,2,1,0:T(2,128)(2,1)S(1)} %get-tuple-element.19), channel_id=1, source_target_pairs={{0,32},{1,33},{2,34},{3,35},{4,36},{5,37},{6,38},{7,39},{8,40},{9,... | collective-permute-start | bytes 221192 | tf_op jit(solution)/shard_map/ppermute | solution.py:34
  3.8 5.3 %collective-permute-start.1 = (bf16[2,6,3,2,512]{4,3,2,1,0:T(2,128)(2,1)S(1)}, bf16[2,6,3,2,512]{4,3,2,1,0:T(2,128)(2,1)S(1)}, u32[]{:S(2)}, u32[]{:S(2)}) collective-permute-start(bf16[2,6,3,2,512]{4,3,2,1,0:T(2,128)(2,1)S(1)} %get-tuple-element.20), channel_id=1, source_target_pairs={{0,63},{1,32},{2,33},{3,34},{4,35},{5,36},{6,37},{7,38},{8,39},{9,... | collective-permute-start | bytes 221192 | tf_op jit(solution)/shard_map/ppermute | solution.py:34
  9.1 2.6 %collective-permute-start.2 = (bf16[2,6,3,2,512]{4,3,2,1,0:T(2,128)(2,1)S(1)}, bf16[2,6,3,2,512]{4,3,2,1,0:T(2,128)(2,1)S(1)}, u32[]{:S(2)}, u32[]{:S(2)}) collective-permute-start(bf16[2,6,3,2,512]{4,3,2,1,0:T(2,128)(2,1)S(1)} %get-tuple-element.21), channel_id=1, source_target_pairs={{0,31},{1,0},{2,1},{3,2},{4,3},{5,4},{6,5},{7,6},{8,7},{9,8},{10,9... | collective-permute-start | bytes 221192 | tf_op jit(solution)/shard_map/ppermute | solution.py:34
  11.7 1.9 %fetch.1 = (bf16[2,6,3,2,512]{4,3,2,1,0:T(2,128)(2,1)S(1)}, f32[1,512]{1,0:T(1,128)S(1)}, bf16[512,1536]{1,0:T(8,128)(2,1)S(1)}, bf16[512,512]{1,0:T(8,128)(2,1)...) custom-call(bf16[12,6,2,512]{3,2,1,0:T(2,128)(2,1)} %bitcast.6, bf16[12,6,2,512]{3,2,1,0:T(2,128)(2,1)} %bitcast.8, ...), custom_call_target="tpu_custom_call" | custom-call | bytes 4194304 | tf_op jit(solution)/shard_map/fetch/pallas_call | solution.py:254
  13.6 0.0 collective-permute-done.ahead_lat
  13.6 0.0 collective-permute-done.1.ahead_both
  13.6 0.1 collective-permute-done.2.ahead_lon
  13.7 2.7 %window.1 = (bf16[2,6,3,2,512]{4,3,2,1,0:T(2,128)(2,1)S(1)}, bf16[2,6,3,2,512]{4,3,2,1,0:T(2,128)(2,1)S(1)}, bf16[2,6,3,2,512]{4,3,2,1,0:T(2,128)(2,1)S(1)}, bf16[2,6,3,2,512]{4,3,2,1,0:T(2,128)(2,1)S(1)}) custom-call(bf16[2,6,3,2,512]{4,3,2,1,0:T(2,128)(2,1)S(1)} %collective-permute-done.ahead_lat, ...), custom_call_target="tpu_custom_call" | custom-call | tf_op jit(solution)/shard_map/window/pallas_call | solution.py:272
  16.5 2.2 %collective-permute-start.3 = (bf16[2,6,3,2,512]{4,3,2,1,0:T(2,128)(2,1)S(1)}, bf16[2,6,3,2,512]{4,3,2,1,0:T(2,128)(2,1)S(1)}, u32[]{:S(2)}, u32[]{:S(2)}) collective-permute-start(bf16[2,6,3,2,512]{4,3,2,1,0:T(2,128)(2,1)S(1)} %get-tuple-element.28), channel_id=1, source_target_pairs={{0,225},{1,226},{2,227},{3,228},{4,229},{5,230},{6,231},{7,232},{8... | collective-permute-start | bytes 221192 | tf_op jit(solution)/shard_map/ppermute | solution.py:34
  18.7 0.0 collective-permute-start.4
  18.7 2.3 %collective-permute-start.5 = (bf16[2,6,3,2,512]{4,3,2,1,0:T(2,128)(2,1)S(1)}, bf16[2,6,3,2,512]{4,3,2,1,0:T(2,128)(2,1)S(1)}, u32[]{:S(2)}, u32[]{:S(2)}) collective-permute-start(bf16[2,6,3,2,512]{4,3,2,1,0:T(2,128)(2,1)S(1)} %get-tuple-element.30), channel_id=1, source_target_pairs={{0,224},{1,225},{2,226},{3,227},{4,228},{5,229},{6,230},{7,231},{8... | collective-permute-start | bytes 221192 | tf_op jit(solution)/shard_map/ppermute | solution.py:34
  21.0 0.6 %join.2 = (bf16[12,6,2,512]{3,2,1,0:T(2,128)(2,1)}, bf16[12,6,2,512]{3,2,1,0:T(2,128)(2,1)}) custom-call(bf16[2,6,3,2,512]{4,3,2,1,0:T(2,128)(2,1)S(1)} %get-tuple-element.31.refs_0_), custom_call_target="tpu_custom_call" | custom-call | tf_op jit(solution)/shard_map/join/pallas_call | solution.py:297
  21.7 2.1 %collective-permute-done.3.refs_0_ = bf16[2,6,3,2,512]{4,3,2,1,0:T(2,128)(2,1)S(1)} collective-permute-done((bf16[2,6,3,2,512]{4,3,2,1,0:T(2,128)(2,1)S(1)}, bf16[2,6,3,2,512]{4,3,2,1,0:T(2,128)(2,1)S(1)}, u32[]{:S(2)}, u32[]{:S(2)}) %collective-permute-start.3) | collective-permute-done | bytes 73760 | tf_op jit(solution)/shard_map/ppermute | solution.py:34
  23.7 2.1 %collective-permute-done.4.refs_1_ = bf16[2,6,3,2,512]{4,3,2,1,0:T(2,128)(2,1)S(1)} collective-permute-done((bf16[2,6,3,2,512]{4,3,2,1,0:T(2,128)(2,1)S(1)}, bf16[2,6,3,2,512]{4,3,2,1,0:T(2,128)(2,1)S(1)}, u32[]{:S(2)}, u32[]{:S(2)}) %collective-permute-start.4) | collective-permute-done | bytes 73760 | tf_op jit(solution)/shard_map/ppermute | solution.py:34
  25.9 0.0 collective-permute-done.5.refs_2_
  25.9 0.7 %join.3 = (bf16[12,6,2,512]{3,2,1,0:T(2,128)(2,1)}, bf16[12,6,2,512]{3,2,1,0:T(2,128)(2,1)}) custom-call(bf16[2,6,3,2,512]{4,3,2,1,0:T(2,128)(2,1)S(1)} %collective-permute-done.3.refs_0_, bf16[2,6,3,2,512]{4,3,2,1,0:T(2,128)(2,1)S(1)} %collective-permute-done.4.refs_1_, ...), custom_call_target="tpu_custom_call", output_to_operand_aliasing={{0}: (3, {}), {1}: (4, {})} | custom-call | tf_op jit(solution)/shard_map/join/pallas_call | solution.py:297
Async XLA Ops:
  1.6 12.1 %collective-permute-start = (bf16[2,6,3,2,512]{4,3,2,1,0:T(2,128)(2,1)S(1)}, bf16[2,6,3,2,512]{4,3,2,1,0:T(2,128)(2,1)S(1)}, u32[]{:S(2)}, u32[]{:S(2)}) collective-permute-start(bf16[2,6,3,2,512]{4,3,2,1,0:T(2,128)(2,1)S(1)} %get-tuple-element.19), channel_id=1, source_target_pairs={{0,32},{1,33},{2,34},{3,35},{4,36},{5,37},{6,38},{7,39},{8,40},{9,... | collective-permute-start | bytes 221192 | tf_op jit(solution)/shard_map/ppermute | solution.py:34
  3.8 9.9 %collective-permute-start.1 = (bf16[2,6,3,2,512]{4,3,2,1,0:T(2,128)(2,1)S(1)}, bf16[2,6,3,2,512]{4,3,2,1,0:T(2,128)(2,1)S(1)}, u32[]{:S(2)}, u32[]{:S(2)}) collective-permute-start(bf16[2,6,3,2,512]{4,3,2,1,0:T(2,128)(2,1)S(1)} %get-tuple-element.20), channel_id=1, source_target_pairs={{0,63},{1,32},{2,33},{3,34},{4,35},{5,36},{6,37},{7,38},{8,39},{9,... | collective-permute-start | bytes 221192 | tf_op jit(solution)/shard_map/ppermute | solution.py:34
  9.1 4.6 %collective-permute-start.2 = (bf16[2,6,3,2,512]{4,3,2,1,0:T(2,128)(2,1)S(1)}, bf16[2,6,3,2,512]{4,3,2,1,0:T(2,128)(2,1)S(1)}, u32[]{:S(2)}, u32[]{:S(2)}) collective-permute-start(bf16[2,6,3,2,512]{4,3,2,1,0:T(2,128)(2,1)S(1)} %get-tuple-element.21), channel_id=1, source_target_pairs={{0,31},{1,0},{2,1},{3,2},{4,3},{5,4},{6,5},{7,6},{8,7},{9,8},{10,9... | collective-permute-start | bytes 221192 | tf_op jit(solution)/shard_map/ppermute | solution.py:34
  16.5 7.3 %collective-permute-start.3 = (bf16[2,6,3,2,512]{4,3,2,1,0:T(2,128)(2,1)S(1)}, bf16[2,6,3,2,512]{4,3,2,1,0:T(2,128)(2,1)S(1)}, u32[]{:S(2)}, u32[]{:S(2)}) collective-permute-start(bf16[2,6,3,2,512]{4,3,2,1,0:T(2,128)(2,1)S(1)} %get-tuple-element.28), channel_id=1, source_target_pairs={{0,225},{1,226},{2,227},{3,228},{4,229},{5,230},{6,231},{7,232},{8... | collective-permute-start | bytes 221192 | tf_op jit(solution)/shard_map/ppermute | solution.py:34
  18.7 7.2 %collective-permute-start.4 = (bf16[2,6,3,2,512]{4,3,2,1,0:T(2,128)(2,1)S(1)}, bf16[2,6,3,2,512]{4,3,2,1,0:T(2,128)(2,1)S(1)}, u32[]{:S(2)}, u32[]{:S(2)}) collective-permute-start(bf16[2,6,3,2,512]{4,3,2,1,0:T(2,128)(2,1)S(1)} %get-tuple-element.29), channel_id=1, source_target_pairs={{0,1},{1,2},{2,3},{3,4},{4,5},{5,6},{6,7},{7,8},{8,9},{9,10},{10,1... | collective-permute-start | bytes 221192 | tf_op jit(solution)/shard_map/ppermute | solution.py:34
  18.7 7.2 %collective-permute-start.5 = (bf16[2,6,3,2,512]{4,3,2,1,0:T(2,128)(2,1)S(1)}, bf16[2,6,3,2,512]{4,3,2,1,0:T(2,128)(2,1)S(1)}, u32[]{:S(2)}, u32[]{:S(2)}) collective-permute-start(bf16[2,6,3,2,512]{4,3,2,1,0:T(2,128)(2,1)S(1)} %get-tuple-element.30), channel_id=1, source_target_pairs={{0,224},{1,225},{2,226},{3,227},{4,228},{5,229},{6,230},{7,231},{8... | collective-permute-start | bytes 221192 | tf_op jit(solution)/shard_map/ppermute | solution.py:34

commit v8 on v7

--- a/solution.py
+++ b/solution.py
@@ -14,7 +14,7 @@
 SLAT = 6
 SLON = 3
 GROUP = 4
-STRIP = 256
+STRIP = 512
 
 MIB = 1 << 20
 NORM_EPS = 1e-05

time: 26.8 us -> 26.9 us (level)
  transfers between devices with their start and end apart: 6 -> 6, of which waited for: 3 -> 2; matrix products, arithmetic and copies ran while one was open for 0% -> 0% of each run, Pallas kernels for 9% -> 10%
where the time goes in v8:
time: 26.9 us; the launch traced here: 26.8 us
  starting transfers between devices  14.6 us (54%)
  Pallas kernels  7.13 us (27%)
  waiting for transfers between devices  4.36 us (16%)
  between operations  0.69 us (3%)
    ppermute x6, starting transfers between devices, neighbour(): return lax.ppermute(piece, ('lat', 'lon'), pairs)  14.6 us
    ppermute x6, waiting for transfers between devices, neighbour(): return lax.ppermute(piece, ('lat', 'lon'), pairs)  4.36 us
    pallas_call x1, Pallas kernels, body(): pl.pallas_call(window_kernel, in_specs=[in_vmem] * 9, out_specs=[in_vmem]...  2.76 us
    pallas_call x1, Pallas kernels, body(): pl.pallas_call(fetch_kernel, in_specs=[in_hbm] * 5, out_specs=[in_vmem] *...  2.09 us
    pallas_call x2, Pallas kernels, join(): pl.pallas_call(functools.partial(join_kernel, which), in_specs=[in_vmem]...  1.37 us
    pallas_call x1, Pallas kernels, body(): pl.pallas_call(cut_kernel, in_specs=[in_hbm] * 2, out_specs=[in_vmem] * 3...  0.91 us
  transfers between devices with their start and end apart: 6, of which 2 were waited for; matrix products, arithmetic and copies ran while one was open for 0% of the time, Pallas kernels for 10%

profile of v8, /device:TPU:2, one launch (start us, length us, event | category | flops | bytes accessed | tf_op | source)
XLA Modules:
  0.0 26.8 jit_solution(5317023050162368287)
XLA Ops:
  0.6 0.9 %cut.1 = (bf16[2,6,3,2,512]{4,3,2,1,0:T(2,128)(2,1)S(1)}, bf16[2,6,3,2,512]{4,3,2,1,0:T(2,128)(2,1)S(1)}, bf16[2,6,3,2,512]{4,3,2,1,0:T(2,128)(2,1)S(1)}) custom-call(bf16[12,6,2,512]{3,2,1,0:T(2,128)(2,1)} %bitcast.5, bf16[12,6,2,512]{3,2,1,0:T(2,128)(2,1)} %bitcast.7), custom_call_target="tpu_custom_call" | custom-call | tf_op jit(solution)/shard_map/cut/pallas_call | solution.py:240
  1.6 2.2 %collective-permute-start = (bf16[2,6,3,2,512]{4,3,2,1,0:T(2,128)(2,1)S(1)}, bf16[2,6,3,2,512]{4,3,2,1,0:T(2,128)(2,1)S(1)}, u32[]{:S(2)}, u32[]{:S(2)}) collective-permute-start(bf16[2,6,3,2,512]{4,3,2,1,0:T(2,128)(2,1)S(1)} %get-tuple-element.19), channel_id=1, source_target_pairs={{0,32},{1,33},{2,34},{3,35},{4,36},{5,37},{6,38},{7,39},{8,40},{9,... | collective-permute-start | bytes 221192 | tf_op jit(solution)/shard_map/ppermute | solution.py:34
  3.8 5.3 %collective-permute-start.1 = (bf16[2,6,3,2,512]{4,3,2,1,0:T(2,128)(2,1)S(1)}, bf16[2,6,3,2,512]{4,3,2,1,0:T(2,128)(2,1)S(1)}, u32[]{:S(2)}, u32[]{:S(2)}) collective-permute-start(bf16[2,6,3,2,512]{4,3,2,1,0:T(2,128)(2,1)S(1)} %get-tuple-element.20), channel_id=1, source_target_pairs={{0,63},{1,32},{2,33},{3,34},{4,35},{5,36},{6,37},{7,38},{8,39},{9,... | collective-permute-start | bytes 221192 | tf_op jit(solution)/shard_map/ppermute | solution.py:34
  9.1 2.6 %collective-permute-start.2 = (bf16[2,6,3,2,512]{4,3,2,1,0:T(2,128)(2,1)S(1)}, bf16[2,6,3,2,512]{4,3,2,1,0:T(2,128)(2,1)S(1)}, u32[]{:S(2)}, u32[]{:S(2)}) collective-permute-start(bf16[2,6,3,2,512]{4,3,2,1,0:T(2,128)(2,1)S(1)} %get-tuple-element.21), channel_id=1, source_target_pairs={{0,31},{1,0},{2,1},{3,2},{4,3},{5,4},{6,5},{7,6},{8,7},{9,8},{10,9... | collective-permute-start | bytes 221192 | tf_op jit(solution)/shard_map/ppermute | solution.py:34
  11.7 2.1 %fetch.1 = (bf16[2,6,3,2,512]{4,3,2,1,0:T(2,128)(2,1)S(1)}, f32[1,512]{1,0:T(1,128)S(1)}, bf16[512,1536]{1,0:T(8,128)(2,1)S(1)}, bf16[512,512]{1,0:T(8,128)(2,1)...) custom-call(bf16[12,6,2,512]{3,2,1,0:T(2,128)(2,1)} %bitcast.6, bf16[12,6,2,512]{3,2,1,0:T(2,128)(2,1)} %bitcast.8, ...), custom_call_target="tpu_custom_call" | custom-call | bytes 4194304 | tf_op jit(solution)/shard_map/fetch/pallas_call | solution.py:254
  13.8 0.0 collective-permute-done.ahead_lat
  13.8 0.0 collective-permute-done.1.ahead_both
  13.8 0.0 collective-permute-done.2.ahead_lon
  13.8 2.8 %window.1 = (bf16[2,6,3,2,512]{4,3,2,1,0:T(2,128)(2,1)S(1)}, bf16[2,6,3,2,512]{4,3,2,1,0:T(2,128)(2,1)S(1)}, bf16[2,6,3,2,512]{4,3,2,1,0:T(2,128)(2,1)S(1)}, bf16[2,6,3,2,512]{4,3,2,1,0:T(2,128)(2,1)S(1)}) custom-call(bf16[2,6,3,2,512]{4,3,2,1,0:T(2,128)(2,1)S(1)} %collective-permute-done.ahead_lat, ...), custom_call_target="tpu_custom_call" | custom-call | tf_op jit(solution)/shard_map/window/pallas_call | solution.py:272
  16.6 2.3 %collective-permute-start.3 = (bf16[2,6,3,2,512]{4,3,2,1,0:T(2,128)(2,1)S(1)}, bf16[2,6,3,2,512]{4,3,2,1,0:T(2,128)(2,1)S(1)}, u32[]{:S(2)}, u32[]{:S(2)}) collective-permute-start(bf16[2,6,3,2,512]{4,3,2,1,0:T(2,128)(2,1)S(1)} %get-tuple-element.28), channel_id=1, source_target_pairs={{0,225},{1,226},{2,227},{3,228},{4,229},{5,230},{6,231},{7,232},{8... | collective-permute-start | bytes 221192 | tf_op jit(solution)/shard_map/ppermute | solution.py:34
  18.9 0.0 collective-permute-start.4
  18.9 2.1 %collective-permute-start.5 = (bf16[2,6,3,2,512]{4,3,2,1,0:T(2,128)(2,1)S(1)}, bf16[2,6,3,2,512]{4,3,2,1,0:T(2,128)(2,1)S(1)}, u32[]{:S(2)}, u32[]{:S(2)}) collective-permute-start(bf16[2,6,3,2,512]{4,3,2,1,0:T(2,128)(2,1)S(1)} %get-tuple-element.30), channel_id=1, source_target_pairs={{0,224},{1,225},{2,226},{3,227},{4,228},{5,229},{6,230},{7,231},{8... | collective-permute-start | bytes 221192 | tf_op jit(solution)/shard_map/ppermute | solution.py:34
  21.0 0.6 %join.2 = (bf16[12,6,2,512]{3,2,1,0:T(2,128)(2,1)}, bf16[12,6,2,512]{3,2,1,0:T(2,128)(2,1)}) custom-call(bf16[2,6,3,2,512]{4,3,2,1,0:T(2,128)(2,1)S(1)} %get-tuple-element.31.refs_0_), custom_call_target="tpu_custom_call" | custom-call | tf_op jit(solution)/shard_map/join/pallas_call | solution.py:297
  21.7 2.1 %collective-permute-done.3.refs_0_ = bf16[2,6,3,2,512]{4,3,2,1,0:T(2,128)(2,1)S(1)} collective-permute-done((bf16[2,6,3,2,512]{4,3,2,1,0:T(2,128)(2,1)S(1)}, bf16[2,6,3,2,512]{4,3,2,1,0:T(2,128)(2,1)S(1)}, u32[]{:S(2)}, u32[]{:S(2)}) %collective-permute-start.3) | collective-permute-done | bytes 73760 | tf_op jit(solution)/shard_map/ppermute | solution.py:34
  23.7 2.3 %collective-permute-done.4.refs_1_ = bf16[2,6,3,2,512]{4,3,2,1,0:T(2,128)(2,1)S(1)} collective-permute-done((bf16[2,6,3,2,512]{4,3,2,1,0:T(2,128)(2,1)S(1)}, bf16[2,6,3,2,512]{4,3,2,1,0:T(2,128)(2,1)S(1)}, u32[]{:S(2)}, u32[]{:S(2)}) %collective-permute-start.4) | collective-permute-done | bytes 73760 | tf_op jit(solution)/shard_map/ppermute | solution.py:34
  26.0 0.0 collective-permute-done.5.refs_2_
  26.0 0.7 %join.3 = (bf16[12,6,2,512]{3,2,1,0:T(2,128)(2,1)}, bf16[12,6,2,512]{3,2,1,0:T(2,128)(2,1)}) custom-call(bf16[2,6,3,2,512]{4,3,2,1,0:T(2,128)(2,1)S(1)} %collective-permute-done.3.refs_0_, bf16[2,6,3,2,512]{4,3,2,1,0:T(2,128)(2,1)S(1)} %collective-permute-done.4.refs_1_, ...), custom_call_target="tpu_custom_call", output_to_operand_aliasing={{0}: (3, {}), {1}: (4, {})} | custom-call | tf_op jit(solution)/shard_map/join/pallas_call | solution.py:297
Async XLA Ops:
  1.6 12.3 %collective-permute-start = (bf16[2,6,3,2,512]{4,3,2,1,0:T(2,128)(2,1)S(1)}, bf16[2,6,3,2,512]{4,3,2,1,0:T(2,128)(2,1)S(1)}, u32[]{:S(2)}, u32[]{:S(2)}) collective-permute-start(bf16[2,6,3,2,512]{4,3,2,1,0:T(2,128)(2,1)S(1)} %get-tuple-element.19), channel_id=1, source_target_pairs={{0,32},{1,33},{2,34},{3,35},{4,36},{5,37},{6,38},{7,39},{8,40},{9,... | collective-permute-start | bytes 221192 | tf_op jit(solution)/shard_map/ppermute | solution.py:34
  3.8 10.1 %collective-permute-start.1 = (bf16[2,6,3,2,512]{4,3,2,1,0:T(2,128)(2,1)S(1)}, bf16[2,6,3,2,512]{4,3,2,1,0:T(2,128)(2,1)S(1)}, u32[]{:S(2)}, u32[]{:S(2)}) collective-permute-start(bf16[2,6,3,2,512]{4,3,2,1,0:T(2,128)(2,1)S(1)} %get-tuple-element.20), channel_id=1, source_target_pairs={{0,63},{1,32},{2,33},{3,34},{4,35},{5,36},{6,37},{7,38},{8,39},{9,... | collective-permute-start | bytes 221192 | tf_op jit(solution)/shard_map/ppermute | solution.py:34
  9.1 4.7 %collective-permute-start.2 = (bf16[2,6,3,2,512]{4,3,2,1,0:T(2,128)(2,1)S(1)}, bf16[2,6,3,2,512]{4,3,2,1,0:T(2,128)(2,1)S(1)}, u32[]{:S(2)}, u32[]{:S(2)}) collective-permute-start(bf16[2,6,3,2,512]{4,3,2,1,0:T(2,128)(2,1)S(1)} %get-tuple-element.21), channel_id=1, source_target_pairs={{0,31},{1,0},{2,1},{3,2},{4,3},{5,4},{6,5},{7,6},{8,7},{9,8},{10,9... | collective-permute-start | bytes 221192 | tf_op jit(solution)/shard_map/ppermute | solution.py:34
  16.6 7.1 %collective-permute-start.3 = (bf16[2,6,3,2,512]{4,3,2,1,0:T(2,128)(2,1)S(1)}, bf16[2,6,3,2,512]{4,3,2,1,0:T(2,128)(2,1)S(1)}, u32[]{:S(2)}, u32[]{:S(2)}) collective-permute-start(bf16[2,6,3,2,512]{4,3,2,1,0:T(2,128)(2,1)S(1)} %get-tuple-element.28), channel_id=1, source_target_pairs={{0,225},{1,226},{2,227},{3,228},{4,229},{5,230},{6,231},{7,232},{8... | collective-permute-start | bytes 221192 | tf_op jit(solution)/shard_map/ppermute | solution.py:34
  18.9 7.1 %collective-permute-start.4 = (bf16[2,6,3,2,512]{4,3,2,1,0:T(2,128)(2,1)S(1)}, bf16[2,6,3,2,512]{4,3,2,1,0:T(2,128)(2,1)S(1)}, u32[]{:S(2)}, u32[]{:S(2)}) collective-permute-start(bf16[2,6,3,2,512]{4,3,2,1,0:T(2,128)(2,1)S(1)} %get-tuple-element.29), channel_id=1, source_target_pairs={{0,1},{1,2},{2,3},{3,4},{4,5},{5,6},{6,7},{7,8},{8,9},{9,10},{10,1... | collective-permute-start | bytes 221192 | tf_op jit(solution)/shard_map/ppermute | solution.py:34
  18.9 7.1 %collective-permute-start.5 = (bf16[2,6,3,2,512]{4,3,2,1,0:T(2,128)(2,1)S(1)}, bf16[2,6,3,2,512]{4,3,2,1,0:T(2,128)(2,1)S(1)}, u32[]{:S(2)}, u32[]{:S(2)}) collective-permute-start(bf16[2,6,3,2,512]{4,3,2,1,0:T(2,128)(2,1)S(1)} %get-tuple-element.30), channel_id=1, source_target_pairs={{0,224},{1,225},{2,226},{3,227},{4,228},{5,229},{6,230},{7,231},{8... | collective-permute-start | bytes 221192 | tf_op jit(solution)/shard_map/ppermute | solution.py:34
